TPU v7x, 32 devices: a whole 2x2x4 slice. The times are simulated.
32 devices in a mesh: dp: 16 (over z, x, core), rep: 2 (over y).
Axes of the slice: x: 2, y: 2, z: 4, core: 2. Of those that a mesh axis runs over, the one named last changes fastest.
Arguments:
- text_states: bfloat16 [14336, 1280], P(('dp', 'rep')), may hold values from -6 to 6
- encoder_frames: bfloat16 [16384, 1280], P(('dp', 'rep')), may hold values from -20 to 20
- out_cotangent: bfloat16 [14336, 1280], P(('dp', 'rep')), may hold values from -6 to 6
- text_lengths: int32 [32], P(('dp', 'rep')), may hold values from 1 to 448, 10752 in all
- q_master: float32 [1280, 640], P('dp'), may hold values from -0.15625 to 0.15625
- q_moment: float32 [1280, 640], P('dp'), may hold values from -3 to 3
- q_second: float32 [1280, 640], P('dp'), may hold values from 0.05 to 2
- key_weight: bfloat16 [1280, 640], P('dp'), may hold values from -0.15625 to 0.15625
- value_weight: bfloat16 [1280, 640], P('dp'), may hold values from -0.15625 to 0.15625
- out_weight: bfloat16 [640, 1280], P(None, 'dp'), may hold values from -0.25 to 0.25
Outputs:
- block_out: bfloat16 [14336, 1280], P(('dp', 'rep'))
- q_gradient: float32 [1280, 640], P('dp')
- new_master: float32 [1280, 640], P('dp')
- new_moment: float32 [1280, 640], P('dp')
- new_second: float32 [1280, 640], P('dp')
All inputs are finite; a program needn't handle non-finite values. No bound on the sum of `text_lengths` on one device may be relied on, other than what follows from the above.
Results may differ from a plain program's by a relative error of at most 0.017.
The roundings to bfloat16 on the way count: a program that leaves them out, or rounds other values in their place, can miss the bound.
Values may be sent and summed in bfloat16 or wider, within the bound.
No kernel may reach another device: no remote copies, remote signals or barrier semaphores. Data moves between devices by JAX's collectives and lax.ppermute only.
A program may use at most 64 MiB of HBM per device.

v0:
```python
import jax
import jax.numpy as jnp
from jax import lax
from jax.sharding import PartitionSpec as P

HEADS = 10
HEAD_DIM = 64
TOK = 448


first_fix = 0.9999734386011124
second_fix = 0.8673804441052468


def contract_rows(left, piece):
    return jnp.dot(left, piece, preferred_element_type=jnp.float32)


def per_device(
    text_states,
    encoder_frames,
    out_cotangent,
    text_lengths,
    q_master,
    q_moment,
    q_second,
    key_weight,
    value_weight,
    out_weight,
):
    scale = HEAD_DIM ** (-0.5)
    tokens_here = text_states.shape[0]
    frames_here = encoder_frames.shape[0]
    width = q_master.shape[1]
    q_weight = q_master.astype(jnp.bfloat16)
    queries = contract_rows(text_states, lax.all_gather(q_weight, "dp", axis=0, tiled=True)).astype(
        jnp.bfloat16
    )
    keys_sum = contract_rows(encoder_frames, lax.all_gather(key_weight, "dp", axis=0, tiled=True))
    values_sum = contract_rows(
        encoder_frames, lax.all_gather(value_weight, "dp", axis=0, tiled=True)
    )
    key_heads = keys_sum.astype(jnp.bfloat16).reshape(frames_here, HEADS, HEAD_DIM)
    value_heads = values_sum.astype(jnp.bfloat16).reshape(frames_here, HEADS, HEAD_DIM)
    query_heads = queries.reshape(tokens_here, HEADS, HEAD_DIM)
    scores = (
        jnp.einsum("thd,fhd->htf", query_heads, key_heads, preferred_element_type=jnp.float32)
        * scale
    )
    attention = jax.nn.softmax(scores, axis=-1).astype(jnp.bfloat16)
    context = (
        jnp.einsum("htf,fhd->thd", attention, value_heads, preferred_element_type=jnp.float32)
        .reshape(tokens_here, width)
        .astype(jnp.bfloat16)
    )
    in_use = jnp.arange(tokens_here, dtype=jnp.int32) < text_lengths[0]
    grad_out = jnp.where(in_use[:, None], out_cotangent, jnp.zeros_like(out_cotangent))
    back_dims = (((1,), (1,)), ((), ()))
    block_out = jnp.dot(
        context,
        lax.all_gather(out_weight, "dp", axis=1, tiled=True),
        preferred_element_type=jnp.float32,
    ).astype(jnp.bfloat16)
    columns = grad_out
    grad_context = lax.dot_general(
        columns,
        lax.all_gather(out_weight, "dp", axis=1, tiled=True),
        back_dims,
        preferred_element_type=jnp.float32,
    )
    grad_heads = grad_context.astype(jnp.bfloat16).reshape(tokens_here, HEADS, HEAD_DIM)
    grad_attention = jnp.einsum(
        "thd,fhd->htf", grad_heads, value_heads, preferred_element_type=jnp.float32
    )
    attn_float = attention.astype(jnp.float32)
    inner = jnp.sum(attn_float * grad_attention, axis=-1, keepdims=True)
    grad_scores = (attn_float * (grad_attention - inner) * scale).astype(jnp.bfloat16)
    grad_queries = (
        jnp.einsum("htf,fhd->thd", grad_scores, key_heads, preferred_element_type=jnp.float32)
        .reshape(tokens_here, width)
        .astype(jnp.bfloat16)
    )
    columns = text_states
    summed = lax.psum_scatter(
        lax.dot_general(
            columns, grad_queries, (((0,), (0,)), ((), ())), preferred_element_type=jnp.float32
        ),
        "dp",
        scatter_dimension=0,
        tiled=True,
    )
    summed = lax.psum(summed, "rep")
    q_gradient = summed * (1.0 / TOK)
    new_moment = 0.9 * q_moment + 0.1 * q_gradient
    new_second = 0.98 * q_second + 0.02 * q_gradient * q_gradient
    update = new_moment / first_fix / (jnp.sqrt(new_second / second_fix) + 1e-06)
    new_master = q_master - 0.001 * (update + 0.01 * q_master)
    return (block_out, q_gradient, new_master, new_moment, new_second)


def solution(mesh):
    in_specs = (
        P(("dp", "rep"), None),
        P(("dp", "rep"), None),
        P(("dp", "rep"), None),
        P(("dp", "rep")),
        P("dp", None),
        P("dp", None),
        P("dp", None),
        P("dp", None),
        P("dp", None),
        P(None, "dp"),
    )
    out_specs = (P(("dp", "rep"), None), P("dp", None), P("dp", None), P("dp", None), P("dp", None))
    return jax.shard_map(
        per_device, mesh=mesh, in_specs=in_specs, out_specs=out_specs, check_vma=False
    )
```

profile of v0, /device:TPU:0, one launch (start us, length us, event | category | flops | bytes accessed | tf_op | source)
XLA Modules:
  0.0 317.5 jit_solution(16998100239686646453)
XLA Ops:
  7.2 0.7 all-gather.5.cloned.1.call-update
  7.9 0.0 all-gather.7.cloned.1.call-start
  8.0 1.6 convert_element_type.46
  9.6 0.0 all-gather.9.cloned.1.call-start
  9.6 0.7 all-gather.9.cloned.1.call-update
  10.3 0.0 all-gather.11.cloned.1.call-start
  10.4 0.5 all-gather.11.cloned.1.call-update
  10.9 0.0 reduce-scatter.4.cloned.1.call-start
  11.6 41.2 %all-gather.5.cloned.1.call-done = bf16[1280,640]{1,0:T(8,128)(2,1)} async-done(((bf16[80,640]{1,0:T(8,128)(2,1)}), bf16[1280,640]{1,0:T(8,128)(2,1)}) %all-gather.5.cloned.1.call-update) | async-done | bytes 1638416 | tf_op jit(solution)/shard_map/all_gather | solution.py:41
  52.8 2.6 convolution_convert_fusion.3
  55.5 0.3 copy.53
  55.7 38.7 %all-gather.7.cloned.1.call-done = bf16[1280,640]{1,0:T(8,128)(2,1)} async-done(((bf16[80,640]{1,0:T(8,128)(2,1)}), bf16[1280,640]{1,0:T(8,128)(2,1)}) %all-gather.7.cloned.1.call-update) | async-done | bytes 1638416 | tf_op jit(solution)/shard_map/all_gather | solution.py:36
  94.4 2.8 convolution_convert_fusion.5
  97.3 1.1 copy.54
  98.4 37.1 %all-gather.9.cloned.1.call-done = bf16[1280,640]{1,0:T(8,128)(2,1)} async-done(((bf16[80,640]{1,0:T(8,128)(2,1)}), bf16[1280,640]{1,0:T(8,128)(2,1)}) %all-gather.9.cloned.1.call-update) | async-done | bytes 1638416 | tf_op jit(solution)/shard_map/all_gather | solution.py:39
  135.5 2.6 convolution_convert_fusion.2
  138.1 0.3 copy.55
  138.3 38.0 %all-gather.11.cloned.1.call-done = bf16[640,1280]{0,1:T(8,128)(2,1)} async-done(((bf16[640,80]{0,1:T(8,128)(2,1)}), bf16[640,1280]{0,1:T(8,128)(2,1)}) %all-gather.11.cloned.1.call-update) | async-done | bytes 1638416 | tf_op jit(solution)/shard_map/all_gather | solution.py:61
  176.3 3.7 %convolution_convert_fusion.4 = bf16[448,640]{1,0:T(8,128)(2,1)} fusion(bf16[640,1280]{0,1:T(8,128)(2,1)} %all-gather.11.cloned.1.call-done, bf16[448,1280]{1,0:T(8,128)(2,1)} %param.12, pred[448]{0:T(512)(128)(4,1)S(1)} %iota_compare_fusion), kind=kOutput, calls=%fused_computation.19 | convolution fusion | flops 734863360 | bytes 3359168 | tf_op jit(solution)/shard_map/dot_general | solution.py:65
  180.1 1.3 copy.56
  181.4 7.4 %fusion.20 = (f32[10,448]{1,0:T(8,128)S(1)}, f32[10,448,512]{2,1,0:T(8,128)}) fusion(bf16[448,10,64]{0,2,1:T(8,128)(2,1)} %bitcast.40, bf16[512,10,64]{0,2,1:T(8,128)(2,1)S(1)} %bitcast.38), kind=kOutput, calls=%fused_computation.34 | convolution fusion | flops 300483072 | bytes 10421760 | tf_op jit(solution)/shard_map/sub | solution.py:50
  188.7 5.6 %divide_convert_fusion = bf16[10,448,512]{2,1,0:T(8,128)(2,1)} fusion(f32[10,448,512]{2,1,0:T(8,128)} %get-tuple-element.25, f32[10,448]{1,0:T(8,128)S(1)} %get-tuple-element.24), kind=kLoop, calls=%fused_computation.6 | loop fusion | flops 4587520 | bytes 13780480 | tf_op jit(solution)/shard_map/convert_element_type | solution.py:50
  194.3 4.9 %fusion.21 = f32[10,448,512]{2,1,0:T(8,128)} fusion(bf16[448,10,64]{0,2,1:T(8,128)(2,1)S(1)} %bitcast.37, bf16[512,10,64]{0,2,1:T(8,128)(2,1)S(1)} %bitcast.35), kind=kOutput, calls=%fused_computation.35 | convolution fusion | flops 293601280 | bytes 10403840 | tf_op jit(solution)/shard_map/thd,fhd->htf/dot_general | solution.py:72
  199.2 11.4 %fusion.10 = bf16[10,64,448]{2,1,0:T(8,128)(2,1)S(1)} fusion(bf16[512,10,64]{0,2,1:T(8,128)(2,1)S(1)} %bitcast.39, bf16[10,448,512]{2,1,0:T(8,128)(2,1)} %divide_convert_fusion, f32[10,448,512]{2,1,0:T(8,128)} %fusion.21), kind=kOutput, calls=%fused_computation.15 | convolution fusion | flops 309949312 | bytes 14991360 | tf_op jit(solution)/shard_map/htf,fhd->thd/dot_general | solution.py:79
  210.6 4.0 %convolution_bitcast_fusion = f32[1280,640]{0,1:T(8,128)} fusion(bf16[448,640]{0,1:T(8,128)(2,1)S(1)} %bitcast.42, bf16[448,1280]{1,0:T(8,128)(2,1)} %param.10), kind=kOutput, calls=%fused_computation.13 | convolution fusion | flops 734003200 | bytes 4997120 | tf_op jit(solution)/shard_map/dot_general | solution.py:85
  214.6 4.6 %copy.58 = f32[1280,640]{1,0:T(8,128)} copy(f32[1280,640]{0,1:T(8,128)} %convolution_bitcast_fusion) | data formatting | bytes 6553600
  219.2 0.0 all-reduce.2.cloned.1.call-start
  219.2 3.7 %convolution_convert_fusion.1 = bf16[10,64,448]{2,1,0:T(8,128)(2,1)S(1)} fusion(bf16[512,10,64]{0,2,1:T(8,128)(2,1)S(1)} %bitcast.36, bf16[10,448,512]{2,1,0:T(8,128)(2,1)} %divide_convert_fusion), kind=kOutput, calls=%fused_computation.16 | convolution fusion | flops 293888000 | bytes 5816320 | tf_op jit(solution)/shard_map/htf,fhd->thd/dot_general | solution.py:52
  223.0 62.1 %reduce-scatter.4.cloned.1.call-done = f32[80,640]{1,0:T(8,128)} async-done(((f32[1280,640]{1,0:T(8,128)}), f32[80,640]{1,0:T(8,128)}) %reduce-scatter.4.cloned.1.call-update) | async-done | bytes 204816 | tf_op jit(solution)/shard_map/reduce_scatter | solution.py:84
  285.1 3.6 %convolution_convert_fusion = bf16[448,1280]{1,0:T(8,128)(2,1)} fusion(bf16[448,640]{0,1:T(8,128)(2,1)S(1)} %bitcast.41, bf16[640,1280]{0,1:T(8,128)(2,1)} %all-gather.11.cloned.1.call-done), kind=kOutput, calls=%fused_computation.14 | convolution fusion | flops 734576640 | bytes 3358720 | tf_op jit(solution)/shard_map/dot_general | solution.py:59
  288.7 19.9 %all-reduce.2.cloned.1.call-done = f32[80,640]{1,0:T(8,128)} async-done(((f32[80,640]{1,0:T(8,128)}), f32[80,640]{1,0:T(8,128)}) %all-reduce.2.cloned.1.call-update) | async-done | bytes 204816 | tf_op jit(solution)/shard_map/psum | solution.py:92
  308.7 1.9 multiply_subtract_fusion
  (13 shorter events, 0.1 us)
Async XLA Ops:
  7.2 45.7 %copy-start = (bf16[512,1280]{1,0:T(8,128)(2,1)S(1)}, bf16[512,1280]{1,0:T(8,128)(2,1)}, u32[]{:S(2)}) copy-start(bf16[512,1280]{1,0:T(8,128)(2,1)} %param.11) | copy-start | bytes 3932164
  7.2 45.7 %all-gather.5.cloned.1.call-start = ((), (), s32[]{:S(2)}) async-start(), calls=%async_computation.1 | async-start | bytes 1740800 | tf_op jit(solution)/shard_map/all_gather | solution.py:41
  7.9 86.5 %all-gather.7.cloned.1.call-start = ((), (), s32[]{:S(2)}) async-start(), calls=%async_computation.2 | async-start | bytes 1740800 | tf_op jit(solution)/shard_map/all_gather | solution.py:36
  9.6 125.9 %all-gather.9.cloned.1.call-start = ((), (), s32[]{:S(2)}) async-start(), calls=%async_computation.3 | async-start | bytes 1740800 | tf_op jit(solution)/shard_map/all_gather | solution.py:39
  10.3 166.0 %all-gather.11.cloned.1.call-start = ((), (), s32[]{:S(2)}) async-start(), calls=%async_computation.4 | async-start | bytes 1740800 | tf_op jit(solution)/shard_map/all_gather | solution.py:61
  10.9 274.2 %reduce-scatter.4.cloned.1.call-start = ((), (), s32[]{:S(2)}) async-start(), calls=%async_computation.6 | async-start | bytes 3481600 | tf_op jit(solution)/shard_map/reduce_scatter | solution.py:84
  219.2 89.5 %all-reduce.2.cloned.1.call-start = ((), (), s32[]{:S(2)}) async-start(), calls=%async_computation.5 | async-start | bytes 409600 | tf_op jit(solution)/shard_map/psum | solution.py:92
  285.1 23.6 %copy-start.1 = (f32[80,640]{1,0:T(8,128)S(1)}, f32[80,640]{1,0:T(8,128)}, u32[]{:S(2)}) copy-start(f32[80,640]{1,0:T(8,128)} %param.14) | copy-start | bytes 614404
  285.1 23.6 %copy-start.2 = (f32[80,640]{1,0:T(8,128)S(1)}, f32[80,640]{1,0:T(8,128)}, u32[]{:S(2)}) copy-start(f32[80,640]{1,0:T(8,128)} %param.15) | copy-start | bytes 614404
  285.1 23.6 %copy-start.3 = (f32[80,640]{1,0:T(8,128)S(1)}, f32[80,640]{1,0:T(8,128)}, u32[]{:S(2)}) copy-start(f32[80,640]{1,0:T(8,128)} %param.16) | copy-start | bytes 614404
Sparse Core Ops, SparseCore 0:
  10.2 42.6 all-gather.4
  55.6 38.8 all-gather.6
  96.6 38.8 all-gather.8
  137.5 38.8 all-gather.10
  219.3 65.7 reduce-scatter.3
  287.3 21.3 all-reduce.1
where the time goes:
time: 318 us; the launch traced here: 317 us
  waiting for transfers between devices  239 us (75%)
  matrix products  46.8 us (15%)
  between operations  14.8 us (5%)
  other arithmetic  9.11 us (3%)
  local copies, waits for them, and re-layouts  7.48 us (2%)
    reduce_scatter x1, waiting for transfers between devices, per_device(): lax.psum_scatter(lax.dot_general(columns, grad_queries, (((0,), (0,)), ((...  62.1 us
    all_gather x1, waiting for transfers between devices, per_device(): lax.all_gather(value_weight, 'dp', axis=0, tiled=True)  41.2 us
    all_gather x1, waiting for transfers between devices, per_device(): lax.all_gather(q_weight, 'dp', axis=0, tiled=True)  38.7 us
    all_gather x1, waiting for transfers between devices, per_device(): lax.all_gather(out_weight, 'dp', axis=1, tiled=True)  38 us
    all_gather x1, waiting for transfers between devices, per_device(): lax.all_gather(key_weight, 'dp', axis=0, tiled=True)  37.1 us
    psum x1, waiting for transfers between devices, per_device(): summed = lax.psum(summed, 'rep')  19.9 us
    dot_general x1, matrix products, per_device(): jnp.einsum('htf,fhd->thd', grad_scores, key_heads, preferred_element_type...  11.4 us
    dot_general x3, matrix products, contract_rows(): return jnp.dot(left, piece, preferred_element_type=jnp.float32)  8.05 us
  transfers between devices with their start and end apart: 6, of which 6 were waited for; matrix products, arithmetic and copies ran while one was open for 6% of the time, Pallas kernels for 0%

commit v1 on v0

v1 whole, which is shorter than its diff:
```python
import functools

import jax
import jax.numpy as jnp
from jax import lax
from jax.experimental import pallas as pl
from jax.experimental.pallas import tpu as pltpu
from jax.sharding import PartitionSpec as P

HEADS = 10
HEAD_DIM = 64
TOK = 448
CORES = 2
CORE_HEADS = HEADS // CORES
GROUPS = ((0, 3), (3, 2))
RING_MOST = 8

first_fix = 0.9999734386011124
second_fix = 0.8673804441052468
BF = jnp.bfloat16
F32 = jnp.float32


def dot(a, b, dims=((1,), (0,))):
    return lax.dot_general(a, b, (dims, ((), ())), preferred_element_type=F32)


def ring_order(chips):
    return list(range(0, chips, 2)) + list(range(chips - 1, 0, -2))


def ring_pairs(chips, step):
    order = ring_order(chips)
    return [
        (CORES * order[i] + c, CORES * order[(i + step) % chips] + c)
        for i in range(chips)
        for c in range(CORES)
    ]


def head_kernel(number, rows_of, pieces, *refs):
    width = number * HEAD_DIM
    refs = list(refs)
    take = lambda n: [refs.pop(0) for _ in range(n)]
    (offs,) = take(1)
    blocks = take(len(rows_of))
    acts = take(8)
    (share, ctx_own) = take(2)
    sums = take(len(pieces))
    (w, x0, x1, e0, e1, g0, g1, t0, t1, wsem, asem) = take(11)
    acts_v = (x0, x1, e0, e1, g0, g1, t0, t1)
    copies = [
        pltpu.make_async_copy(
            b, w.at[pl.ds(pl.multiple_of(offs[i], 16 if n % 16 == 0 else n), n)], wsem.at[i]
        )
        for i, (b, n) in enumerate(zip(blocks, rows_of))
    ]
    loads = [pltpu.make_async_copy(a, v, asem.at[i]) for i, (a, v) in enumerate(zip(acts, acts_v))]
    for c in copies + loads:
        c.start()
    for c in copies:
        c.wait()
    wq, wk, wv, wo = [w[:, i * width : (i + 1) * width] for i in range(4)]
    grads = []
    for clip in range(2):
        xs, es, gs_ = acts_v[clip], acts_v[2 + clip], acts_v[4 + clip]
        loads[clip].wait()
        q = (dot(xs[...], wq) * 0.125).astype(BF)
        loads[2 + clip].wait()
        k = dot(es[...], wk).astype(BF)
        v = dot(es[...], wv).astype(BF)
        loads[4 + clip].wait()
        gc = dot(gs_[...], wo).astype(BF)
        ctxs, gqs = [], []
        for h in range(number):
            cols = slice(h * HEAD_DIM, (h + 1) * HEAD_DIM)
            qh, kh, vh, gh = q[:, cols], k[:, cols], v[:, cols], gc[:, cols]
            s = dot(qh, kh, ((1,), (1,)))
            p = jnp.exp(s - jnp.max(s, axis=1, keepdims=True))
            a = (p * (1.0 / jnp.sum(p, axis=1, keepdims=True))).astype(BF)
            ctx = dot(a, vh)
            ga = dot(gh, vh, ((1,), (1,)))
            inner = jnp.sum(gh.astype(F32) * ctx, axis=1, keepdims=True)
            gs = (a.astype(F32) * (ga - inner)).astype(BF)
            gqs.append((dot(gs, kh) * 0.125).astype(BF))
            ctxs.append(ctx.astype(BF))
        grads.append(jnp.concatenate(gqs, axis=1))
        if clip == 0:
            ctx_own[...] = jnp.concatenate(ctxs, axis=1)
        else:
            share[:TOK, :] = jnp.concatenate(ctxs, axis=1)
    share[TOK:, :] = wo
    loads[6].wait()
    loads[7].wait()
    for out, (at, skip, n) in zip(sums, pieces):
        rows = pl.ds(pl.multiple_of(offs[at], 16 if n % 16 == 0 else n) + skip, n)
        out[...] = dot(t0[rows, :], grads[0]) + dot(t1[rows, :], grads[1])


def head_group(number, offs, blocks, rows_of, pieces, acts):
    depth = acts[6].shape[0]
    frames = acts[2].shape[0]
    width = number * HEAD_DIM
    hbm = pl.BlockSpec(memory_space=pl.ANY)
    vm = pl.BlockSpec(memory_space=pltpu.VMEM)
    return pl.pallas_call(
        functools.partial(head_kernel, number, rows_of, pieces),
        out_shape=(
            jax.ShapeDtypeStruct((TOK + depth, width), BF),
            jax.ShapeDtypeStruct((TOK, width), BF),
        )
        + tuple(jax.ShapeDtypeStruct((n, width), F32) for _, _, n in pieces),
        in_specs=[pl.BlockSpec(memory_space=pltpu.SMEM)] + [hbm] * (len(blocks) + 8),
        out_specs=(vm,) * (2 + len(pieces)),
        scratch_shapes=[
            pltpu.VMEM((depth, 4 * width), BF),
            pltpu.VMEM((TOK, depth), BF),
            pltpu.VMEM((TOK, depth), BF),
            pltpu.VMEM((frames, depth), BF),
            pltpu.VMEM((frames, depth), BF),
            pltpu.VMEM((TOK, depth), BF),
            pltpu.VMEM((TOK, depth), BF),
            pltpu.VMEM((depth, TOK), BF),
            pltpu.VMEM((depth, TOK), BF),
            pltpu.SemaphoreType.DMA((len(blocks),)),
            pltpu.SemaphoreType.DMA((8,)),
        ],
        compiler_params=pltpu.CompilerParams(vmem_limit_bytes=48 * 2**20),
        cost_estimate=pl.CostEstimate(
            flops=number * 2 * 2 * 480 * 64 * (5 * depth + 4 * 512),
            bytes_accessed=2 * 4 * 1280 * 960 * 2,
            transcendentals=number * 2 * TOK * frames,
        ),
    )(offs, *blocks, *acts)


def per_device(
    chips,
    reps,
    text_states,
    encoder_frames,
    out_cotangent,
    text_lengths,
    q_master,
    q_moment,
    q_second,
    key_weight,
    value_weight,
    out_weight,
):
    rows, width = q_master.shape
    depth = text_states.shape[1]
    half = width // CORES
    me = lax.axis_index("dp")
    core, chip = me % CORES, me // CORES
    first = core == 0
    mates = [(i, i ^ 1) for i in range(CORES * chips)]
    swap = lambda a: lax.ppermute(a, "dp", mates)
    ring = 1 < chips <= RING_MOST
    right = lambda a: lax.ppermute(a, "dp", ring_pairs(chips, 1))
    left = lambda a: lax.ppermute(a, "dp", ring_pairs(chips, -1))

    parts = (q_master.astype(BF), key_weight, value_weight, out_weight.T)
    def pack(c):
        return jnp.concatenate(
            [
                w[:, c * half + h * HEAD_DIM : c * half + (h + n) * HEAD_DIM]
                for h, n in GROUPS
                for w in parts
            ],
            axis=1,
        )
    packs = [pack(c) for c in range(CORES)]
    keep = jnp.where(first, packs[0], packs[1])
    got = swap(jnp.where(first, packs[1], packs[0]))
    block = jnp.where(
        first, jnp.concatenate([keep, got], axis=0), jnp.concatenate([got, keep], axis=0)
    )

    in_use = jnp.arange(TOK, dtype=jnp.int32) < text_lengths[0]
    grad_out = jnp.where(in_use[:, None], out_cotangent, jnp.zeros_like(out_cotangent))
    x0, e0, g0 = text_states, encoder_frames, grad_out
    x1, e1, g1 = swap(x0), swap(e0), swap(g0)
    acts = (x0, x1, e0, e1, g0, g1, x0.T, x1.T)

    chip_rows = CORES * rows
    lower = chip_rows // 2
    if ring:
        order = ring_order(chips)
        place = [order.index(c) for c in range(chips)]
        table = [
            [chip_rows * order[(place[c] + k) % chips] for k in range(chips)] for c in range(chips)
        ]
        at = jnp.asarray(table, jnp.int32)[chip]
        far = chips // 2
    starts = [4 * HEAD_DIM * h for h, _ in GROUPS]
    shares, owns, totals = [], [], []
    for (h, n), start in zip(GROUPS, starts):
        mine = block[:, start : start + 4 * HEAD_DIM * n]
        if ring:
            blocks, steps = [mine], [0]
            r = l = mine
            for k in range(1, far):
                r, l = right(r), left(l)
                blocks += [r, l]
                steps += [chips - k, k]
            blocks += [right(r[:lower]), left(l[lower:])]
            offs = jnp.stack([at[k] for k in steps] + [at[far], at[far] + lower])
            rows_of = [chip_rows] * len(steps) + [lower, lower]
            pieces = [(len(steps), 0, lower), (len(steps), lower, lower)]
            for k in range(far - 1, 0, -1):
                pieces += [(steps.index(k), 0, chip_rows), (steps.index(chips - k), 0, chip_rows)]
            pieces += [(0, 0, chip_rows)]
            pieces[1] = (len(steps) + 1, 0, lower)
        else:
            blocks = [
                lax.all_gather(
                    mine,
                    "dp",
                    axis=0,
                    tiled=True,
                    axis_index_groups=[
                        [CORES * i + c for i in range(chips)] for c in range(CORES)
                    ],
                )
            ]
            offs = jnp.zeros((1,), jnp.int32)
            rows_of = [depth]
            pieces = [(0, 0, depth)]
        share, own, *sums = head_group(n, offs, blocks, rows_of, pieces, acts)
        shares.append(share)
        owns.append(own)
        if ring:
            r, l = right(sums[0]), left(sums[1])
            for k in range(far - 1, 0, -1):
                toward_right, toward_left = sums[2 * (far - k)], sums[2 * (far - k) + 1]
                if k == far - 1:
                    r = jnp.concatenate([toward_right[:lower] + r, toward_right[lower:]], axis=0)
                    l = jnp.concatenate([toward_left[:lower], toward_left[lower:] + l], axis=0)
                else:
                    r, l = toward_right + r, toward_left + l
                r, l = right(r), left(l)
            totals.append(sums[-1] + r + l)
        else:
            totals.append(
                lax.psum_scatter(
                    sums[0],
                    "dp",
                    scatter_dimension=0,
                    tiled=True,
                    axis_index_groups=[
                        [CORES * i + c for i in range(chips)] for c in range(CORES)
                    ],
                )
            )

    mine = jnp.concatenate([s[TOK:] for s in shares], axis=1)
    swapped = [swap(s) for s in shares]
    context = jnp.concatenate(owns + [s[:TOK] for s in swapped], axis=1)
    out_rows = jnp.concatenate([s[TOK:] for s in shares + swapped], axis=1)
    block_out = dot(context, out_rows, ((1,), (1,))).astype(BF)

    total = jnp.concatenate(totals, axis=1)
    keep = jnp.where(first, total[:rows], total[rows:])
    got = swap(jnp.where(first, total[rows:], total[:rows]))
    summed = jnp.where(
        first, jnp.concatenate([keep, got], axis=1), jnp.concatenate([got, keep], axis=1)
    )
    if reps == 2:
        summed = summed + lax.ppermute(summed, "rep", [(0, 1), (1, 0)])
    else:
        summed = lax.psum(summed, "rep")
    q_gradient = summed * (1.0 / TOK)
    new_moment = 0.9 * q_moment + 0.1 * q_gradient
    new_second = 0.98 * q_second + 0.02 * q_gradient * q_gradient
    update = new_moment / first_fix / (jnp.sqrt(new_second / second_fix) + 1e-06)
    new_master = q_master - 0.001 * (update + 0.01 * q_master)
    return (block_out, q_gradient, new_master, new_moment, new_second)


def solution(mesh):
    in_specs = (
        P(("dp", "rep"), None),
        P(("dp", "rep"), None),
        P(("dp", "rep"), None),
        P(("dp", "rep")),
        P("dp", None),
        P("dp", None),
        P("dp", None),
        P("dp", None),
        P("dp", None),
        P(None, "dp"),
    )
    out_specs = (P(("dp", "rep"), None), P("dp", None), P("dp", None), P("dp", None), P("dp", None))
    return jax.shard_map(
        functools.partial(per_device, mesh.shape["dp"] // CORES, mesh.shape["rep"]),
        mesh=mesh,
        in_specs=in_specs,
        out_specs=out_specs,
        check_vma=False,
    )
```

time: 318 us -> 148 us (0.47)
  waiting for transfers between devices: 239 us -> 31.7 us
  matrix products: 46.8 us -> 3.36 us
  starting transfers between devices: 0.24 us -> 41 us
  Pallas kernels: 0 us -> 26.8 us
  local copies, waits for them, and re-layouts: 7.48 us -> 32.6 us
  between operations: 14.8 us -> 2.44 us
    all_gather x4 -> x0, waiting for transfers between devices: 155 us -> none  [the longest x1 41.2 us: per_device(): lax.all_gather(value_weight, 'dp', axis=0, tiled=True)]
    reduce_scatter x1 -> x0, waiting for transfers between devices: 62.1 us -> none  [per_device(): lax.psum_scatter(lax.dot_general(columns, grad_queries, (((0,), (0,)), ((...]
    ppermute x0 -> x40, starting transfers between devices: none -> 41 us  [the longest x16 20.9 us: per_device(): right = lambda a: lax.ppermute(a, 'dp', ring_pairs(chips, 1))]
    dot_general x9 -> x1, matrix products: 39.4 us -> 3.36 us  [dot(): return lax.dot_general(a, b, (dims, ((), ())), preferred_element_type=F32)]
    ppermute x0 -> x40, waiting for transfers between devices: none -> 31.7 us  [the longest x16 15.2 us: per_device(): left = lambda a: lax.ppermute(a, 'dp', ring_pairs(chips, -1))]
    pallas_call x0 -> x2, Pallas kernels: none -> 26.8 us  [head_group(): pl.pallas_call(functools.partial(head_kernel, number, rows_of, pieces), o...]
    psum x1 -> x0, waiting for transfers between devices: 19.9 us -> none  [per_device(): summed = lax.psum(summed, 'rep')]
    slice x0 -> x18, local copies, waits for them, and re-layouts: none -> 13.6 us  [the longest x4 6.17 us: per_device(): blocks += [right(r[:lower]), left(l[lower:])]]
  transfers between devices with their start and end apart: 6 -> 40, of which waited for: 6 -> 12; matrix products, arithmetic and copies ran while one was open for 6% -> 19% of each run, Pallas kernels for 0% -> 18%
where the time goes in v1:
time: 148 us; the launch traced here: 147 us
  starting transfers between devices  41 us (28%)
  local copies, waits for them, and re-layouts  32.6 us (22%)
  waiting for transfers between devices  31.7 us (21%)
  Pallas kernels  26.8 us (18%)
  other arithmetic  9.03 us (6%)
  matrix products  3.36 us (2%)
  between operations  2.44 us (2%)
    pallas_call x2, Pallas kernels, head_group(): pl.pallas_call(functools.partial(head_kernel, number, rows_of, pieces), o...  26.8 us
    ppermute x16, starting transfers between devices, per_device(): right = lambda a: lax.ppermute(a, 'dp', ring_pairs(chips, 1))  20.9 us
    ppermute x16, starting transfers between devices, per_device(): left = lambda a: lax.ppermute(a, 'dp', ring_pairs(chips, -1))  16.9 us
    ppermute x16, waiting for transfers between devices, per_device(): left = lambda a: lax.ppermute(a, 'dp', ring_pairs(chips, -1))  15.2 us
    ppermute x16, waiting for transfers between devices, per_device(): right = lambda a: lax.ppermute(a, 'dp', ring_pairs(chips, 1))  13.9 us
    unnamed x65, local copies, waits for them, and re-layouts  11.3 us
    slice x4, local copies, waits for them, and re-layouts, per_device(): blocks += [right(r[:lower]), left(l[lower:])]  6.17 us
    another operation x1, local copies, waits for them, and re-layouts, per_device(): offs = jnp.stack([at[k] for k in steps] + [at[far], at[far] + lower])  4.89 us
  transfers between devices with their start and end apart: 40, of which 12 were waited for; matrix products, arithmetic and copies ran while one was open for 19% of the time, Pallas kernels for 18%

profile of v1, /device:TPU:0, one launch (start us, length us, event | category | flops | bytes accessed | tf_op | source)
XLA Modules:
  0.0 146.9 jit_solution(10812531465626035602)
XLA Ops:
  7.3 3.0 %collective-permute-start.12 = (bf16[160,512]{1,0:T(8,128)(2,1)S(1)}, bf16[160,512]{1,0:T(8,128)(2,1)S(1)}, u32[]{:S(2)}, u32[]{:S(2)}) collective-permute-start(bf16[160,512]{1,0:T(8,128)(2,1)S(1)} %slice.239.refs_1_), channel_id=1, source_target_pairs={{0,8},{2,10},{8,16},{10,18},{16,24},{18,26},{24,28},{26,30},{28,20... | collective-permute-start | bytes 491528 | tf_op jit(solution)/shard_map/ppermute | solution.py:160
  11.6 1.6 %collective-permute-start.1 = (bf16[160,768]{1,0:T(8,128)(2,1)S(1)}, bf16[160,768]{1,0:T(8,128)(2,1)S(1)}, u32[]{:S(2)}, u32[]{:S(2)}) collective-permute-start(bf16[160,768]{1,0:T(8,128)(2,1)S(1)} %slice.236.refs_1_), channel_id=1, source_target_pairs={{0,8},{2,10},{8,16},{10,18},{16,24},{18,26},{24,28},{26,30},{28,20... | collective-permute-start | bytes 737288 | tf_op jit(solution)/shard_map/ppermute | solution.py:160
  13.6 1.6 %collective-permute-done.12.refs_2_ = bf16[160,512]{1,0:T(8,128)(2,1)S(1)} collective-permute-done((bf16[160,512]{1,0:T(8,128)(2,1)S(1)}, bf16[160,512]{1,0:T(8,128)(2,1)S(1)}, u32[]{:S(2)}, u32[]{:S(2)}) %collective-permute-start.12) | collective-permute-done | bytes 163872 | tf_op jit(solution)/shard_map/ppermute | solution.py:160
  15.2 2.1 %collective-permute-start.13 = (bf16[160,512]{1,0:T(8,128)(2,1)S(1)}, bf16[160,512]{1,0:T(8,128)(2,1)S(1)}, u32[]{:S(2)}, u32[]{:S(2)}) collective-permute-start(bf16[160,512]{1,0:T(8,128)(2,1)S(1)} %slice.239.refs_1_), channel_id=1, source_target_pairs={{0,4},{2,6},{8,0},{10,2},{16,8},{18,10},{24,16},{26,18},{28,24},{3... | collective-permute-start | bytes 491528 | tf_op jit(solution)/shard_map/ppermute | solution.py:161
  17.5 6.8 %collective-permute-done.13.refs_3_ = bf16[160,512]{1,0:T(8,128)(2,1)S(1)} collective-permute-done((bf16[160,512]{1,0:T(8,128)(2,1)S(1)}, bf16[160,512]{1,0:T(8,128)(2,1)S(1)}, u32[]{:S(2)}, u32[]{:S(2)}) %collective-permute-start.13) | collective-permute-done | bytes 163872 | tf_op jit(solution)/shard_map/ppermute | solution.py:161
  24.3 1.6 %collective-permute-start.14 = (bf16[160,512]{1,0:T(8,128)(2,1)S(1)}, bf16[160,512]{1,0:T(8,128)(2,1)S(1)}, u32[]{:S(2)}, u32[]{:S(2)}) collective-permute-start(bf16[160,512]{1,0:T(8,128)(2,1)S(1)} %collective-permute-done.12.refs_2_), channel_id=1, source_target_pairs={{0,8},{2,10},{8,16},{10,18},{16,24},{18,26},{24,28},{26,30},{28,20... | collective-permute-start | bytes 491528 | tf_op jit(solution)/shard_map/ppermute | solution.py:160
  27.0 3.9 %collective-permute-done.14.refs_4_ = bf16[160,512]{1,0:T(8,128)(2,1)S(1)} collective-permute-done((bf16[160,512]{1,0:T(8,128)(2,1)S(1)}, bf16[160,512]{1,0:T(8,128)(2,1)S(1)}, u32[]{:S(2)}, u32[]{:S(2)}) %collective-permute-start.14) | collective-permute-done | bytes 163872 | tf_op jit(solution)/shard_map/ppermute | solution.py:160
  30.9 1.6 %collective-permute-start.3 = (bf16[160,768]{1,0:T(8,128)(2,1)S(1)}, bf16[160,768]{1,0:T(8,128)(2,1)}, u32[]{:S(2)}, u32[]{:S(2)}) collective-permute-start(bf16[160,768]{1,0:T(8,128)(2,1)S(1)} %collective-permute-done.1.refs_2_), channel_id=1, source_target_pairs={{0,8},{2,10},{8,16},{10,18},{16,24},{18,26},{24,28},{26,30},{28,20... | collective-permute-start | bytes 737288 | tf_op jit(solution)/shard_map/ppermute | solution.py:160
  34.3 4.3 %collective-permute-done.3.refs_4_ = bf16[160,768]{1,0:T(8,128)(2,1)} collective-permute-done((bf16[160,768]{1,0:T(8,128)(2,1)S(1)}, bf16[160,768]{1,0:T(8,128)(2,1)}, u32[]{:S(2)}, u32[]{:S(2)}) %collective-permute-start.3) | collective-permute-done | bytes 245792 | tf_op jit(solution)/shard_map/ppermute | solution.py:160
  38.6 1.6 %collective-permute-start.16 = (bf16[160,512]{1,0:T(8,128)(2,1)S(1)}, bf16[160,512]{1,0:T(8,128)(2,1)}, u32[]{:S(2)}, u32[]{:S(2)}) collective-permute-start(bf16[160,512]{1,0:T(8,128)(2,1)S(1)} %collective-permute-done.14.refs_4_), channel_id=1, source_target_pairs={{0,8},{2,10},{8,16},{10,18},{16,24},{18,26},{24,28},{26,30},{28,20... | collective-permute-start | bytes 491528 | tf_op jit(solution)/shard_map/ppermute | solution.py:160
  42.0 2.1 %collective-permute-done.16.refs_6_ = bf16[160,512]{1,0:T(8,128)(2,1)} collective-permute-done((bf16[160,512]{1,0:T(8,128)(2,1)S(1)}, bf16[160,512]{1,0:T(8,128)(2,1)}, u32[]{:S(2)}, u32[]{:S(2)}) %collective-permute-start.16) | collective-permute-done | bytes 163872 | tf_op jit(solution)/shard_map/ppermute | solution.py:160
  44.0 1.6 %collective-permute-start.5 = (bf16[160,768]{1,0:T(8,128)(2,1)}, bf16[160,768]{1,0:T(8,128)(2,1)}, u32[]{:S(2)}, u32[]{:S(2)}) collective-permute-start(bf16[160,768]{1,0:T(8,128)(2,1)} %collective-permute-done.3.refs_4_), channel_id=1, source_target_pairs={{0,8},{2,10},{8,16},{10,18},{16,24},{18,26},{24,28},{26,30},{28,20... | collective-permute-start | bytes 737288 | tf_op jit(solution)/shard_map/ppermute | solution.py:160
  51.9 1.6 %collective-permute-start.18 = (bf16[80,512]{1,0:T(8,128)(2,1)}, bf16[80,512]{1,0:T(8,128)(2,1)S(1)}, u32[]{:S(2)}, u32[]{:S(2)}) collective-permute-start(bf16[80,512]{1,0:T(8,128)(2,1)} %slice.240), channel_id=1, source_target_pairs={{0,8},{2,10},{8,16},{10,18},{16,24},{18,26},{24,28},{26,30},{28,20... | collective-permute-start | bytes 245768 | tf_op jit(solution)/shard_map/ppermute | solution.py:160
  55.2 4.9 %stack.9.refs_0_ = s32[9]{0:T(128)S(1)} concatenate(s32[1]{0:T(128)} %bitcast, s32[1]{0:T(128)} %bitcast.1, s32[1]{0:T(128)} %bitcast.2, s32[1]{0:T(128)} %bitcast.3, s32[1]{0:T(128)} %bitcast.4, s32[1]{0:T(128)} %bitcast.5, s32[1]{0:T(128)} %bitcast.6, s32[1]{0:T(128)} %bitcast.7, s32[1]{0:T(128)} %bitcast.8), dimensions={0} | concatenate | bytes 72 | tf_op jit(solution)/shard_map/stack | solution.py:208
  60.1 1.6 %slice.237 = bf16[80,768]{1,0:T(8,128)(2,1)} slice(bf16[160,768]{1,0:T(8,128)(2,1)} %collective-permute-done.5.refs_6_), slice={[0:80], [0:768]} | slice | bytes 245760 | tf_op jit(solution)/shard_map/slice | solution.py:207
  61.7 1.6 %slice.238 = bf16[80,768]{1,0:T(8,128)(2,1)} slice(bf16[160,768]{1,0:T(8,128)(2,1)} %collective-permute-done.6.refs_7_), slice={[80:160], [0:768]} | slice | bytes 245760 | tf_op jit(solution)/shard_map/slice | solution.py:207
  63.2 1.6 %collective-permute-start.7 = (bf16[80,768]{1,0:T(8,128)(2,1)}, bf16[80,768]{1,0:T(8,128)(2,1)}, u32[]{:S(2)}, u32[]{:S(2)}) collective-permute-start(bf16[80,768]{1,0:T(8,128)(2,1)} %slice.237), channel_id=1, source_target_pairs={{0,8},{2,10},{8,16},{10,18},{16,24},{18,26},{24,28},{26,30},{28,20... | collective-permute-start | bytes 368648 | tf_op jit(solution)/shard_map/ppermute | solution.py:160
  71.4 12.8 %shard_map.147 = (bf16[1728,128]{1,0:T(8,128)(2,1)S(1)}, bf16[448,128]{1,0:T(8,128)(2,1)S(1)}, f32[80,128]{1,0:T(8,128)S(1)}, f32[80,128]{1,0:T(8,128)S(1)}, f32...) custom-call(s32[9]{0:T(128)S(1)} %stack.9.refs_0_, ...), custom_call_target="tpu_custom_call" | custom-call | flops 2076180480 | bytes 19660800 | tf_op jit(solution)/shard_map/pallas_call | solution.py:106
  85.6 1.6 %collective-permute-start.30 = (f32[80,128]{1,0:T(8,128)S(1)}, f32[80,128]{1,0:T(8,128)S(1)}, u32[]{:S(2)}, u32[]{:S(2)}) collective-permute-start(f32[80,128]{1,0:T(8,128)S(1)} %get-tuple-element.44), channel_id=1, source_target_pairs={{0,8},{2,10},{8,16},{10,18},{16,24},{18,26},{24,28},{26,30},{28,20... | collective-permute-start | bytes 122888 | tf_op jit(solution)/shard_map/ppermute | solution.py:160
  87.2 14.1 %shard_map.146 = (bf16[1728,192]{1,0:T(8,128)(2,1)S(1)}, bf16[448,192]{1,0:T(8,128)(2,1)S(1)}, f32[80,192]{1,0:T(8,128)S(1)}, f32[80,192]{1,0:T(8,128)S(1)}, f32...) custom-call(s32[9]{0:T(128)S(1)} %stack.9.refs_0_, ...), custom_call_target="tpu_custom_call" | custom-call | flops 3114270720 | bytes 19660800 | tf_op jit(solution)/shard_map/pallas_call | solution.py:106
  103.9 1.6 %collective-permute-start.31 = (f32[160,128]{1,0:T(8,128)S(1)}, f32[160,128]{1,0:T(8,128)S(1)}, u32[]{:S(2)}, u32[]{:S(2)}) collective-permute-start(f32[160,128]{1,0:T(8,128)S(1)} %pad_maximum_fusion.3), channel_id=1, source_target_pairs={{0,8},{2,10},{8,16},{10,18},{16,24},{18,26},{24,28},{26,30},{28,20... | collective-permute-start | bytes 245768 | tf_op jit(solution)/shard_map/ppermute | solution.py:160
  105.5 3.5 %collective-permute-done.34 = f32[80,128]{1,0:T(8,128)S(1)} collective-permute-done((f32[80,128]{1,0:T(8,128)S(1)}, f32[80,128]{1,0:T(8,128)S(1)}, u32[]{:S(2)}, u32[]{:S(2)}) %collective-permute-start.34) | collective-permute-done | bytes 40992 | tf_op jit(solution)/shard_map/ppermute | solution.py:161
  109.6 1.7 %collective-permute-start.27 = (f32[160,192]{1,0:T(8,128)S(1)}, f32[160,192]{1,0:T(8,128)S(1)}, u32[]{:S(2)}, u32[]{:S(2)}) collective-permute-start(f32[160,192]{1,0:T(8,128)S(1)} %pad_maximum_fusion.1), channel_id=1, source_target_pairs={{0,4},{2,6},{8,0},{10,2},{16,8},{18,10},{24,16},{26,18},{28,24},{3... | collective-permute-start | bytes 368648 | tf_op jit(solution)/shard_map/ppermute | solution.py:161
  113.4 3.0 %collective-permute-done.35 = f32[160,128]{1,0:T(8,128)S(1)} collective-permute-done((f32[160,128]{1,0:T(8,128)S(1)}, f32[160,128]{1,0:T(8,128)S(1)}, u32[]{:S(2)}, u32[]{:S(2)}) %collective-permute-start.35) | collective-permute-done | bytes 81952 | tf_op jit(solution)/shard_map/ppermute | solution.py:161
  116.4 2.1 %collective-permute-start.36 = (f32[160,128]{1,0:T(8,128)S(1)}, f32[160,128]{1,0:T(8,128)S(1)}, u32[]{:S(2)}, u32[]{:S(2)}) collective-permute-start(f32[160,128]{1,0:T(8,128)S(1)} %add.95), channel_id=1, source_target_pairs={{0,4},{2,6},{8,0},{10,2},{16,8},{18,10},{24,16},{26,18},{28,24},{3... | collective-permute-start | bytes 245768 | tf_op jit(solution)/shard_map/ppermute | solution.py:161
  119.9 2.0 %collective-permute-start.28 = (f32[160,192]{1,0:T(8,128)}, f32[160,192]{1,0:T(8,128)}, u32[]{:S(2)}, u32[]{:S(2)}) collective-permute-start(f32[160,192]{1,0:T(8,128)} %add.87), channel_id=1, source_target_pairs={{0,4},{2,6},{8,0},{10,2},{16,8},{18,10},{24,16},{26,18},{28,24},{3... | collective-permute-start | bytes 368648 | tf_op jit(solution)/shard_map/ppermute | solution.py:161
  123.3 2.0 %collective-permute-start.37 = (f32[160,128]{1,0:T(8,128)}, f32[160,128]{1,0:T(8,128)}, u32[]{:S(2)}, u32[]{:S(2)}) collective-permute-start(f32[160,128]{1,0:T(8,128)} %add.96), channel_id=1, source_target_pairs={{0,4},{2,6},{8,0},{10,2},{16,8},{18,10},{24,16},{26,18},{28,24},{3... | collective-permute-start | bytes 245768 | tf_op jit(solution)/shard_map/ppermute | solution.py:161
  128.1 2.3 %collective-permute-start.29 = (f32[160,192]{1,0:T(8,128)S(1)}, f32[160,192]{1,0:T(8,128)S(1)}, u32[]{:S(2)}, u32[]{:S(2)}) collective-permute-start(f32[160,192]{1,0:T(8,128)S(1)} %add.88), channel_id=1, source_target_pairs={{0,4},{2,6},{8,0},{10,2},{16,8},{18,10},{24,16},{26,18},{28,24},{3... | collective-permute-start | bytes 368648 | tf_op jit(solution)/shard_map/ppermute | solution.py:161
  131.4 2.0 %collective-permute-done.25 = f32[160,192]{1,0:T(8,128)S(1)} collective-permute-done((f32[160,192]{1,0:T(8,128)S(1)}, f32[160,192]{1,0:T(8,128)S(1)}, u32[]{:S(2)}, u32[]{:S(2)}) %collective-permute-start.25) | collective-permute-done | bytes 122912 | tf_op jit(solution)/shard_map/ppermute | solution.py:160
  137.3 1.6 %collective-permute-start.39 = (f32[80,640]{1,0:T(8,128)S(1)}, f32[80,640]{1,0:T(8,128)}, u32[]{:S(2)}, u32[]{:S(2)}) collective-permute-start(f32[80,640]{1,0:T(8,128)S(1)} %maximum_select_fusion.1), channel_id=1, source_target_pairs={{0,1},{1,0},{2,3},{3,2},{4,5},{5,4},{6,7},{7,6},{8,9},{9,8},{10,11... | collective-permute-start | bytes 614408 | tf_op jit(solution)/shard_map/ppermute | solution.py:270
  140.1 3.4 %convolution_convert_fusion = bf16[448,1280]{1,0:T(8,128)(2,1)} fusion(bf16[1280,128]{1,0:T(8,128)(2,1)S(1)} %slice-done, bf16[1280,192]{1,0:T(8,128)(2,1)S(1)} %copy.26, bf16[1280,128]{1,0:T(8,128)(2,1)} %slice.215, bf16[1280,192]{1,0:T(8,128)(2,1)S(1)} %copy-done.27, bf16[448,128]{1,0:T(8,128)(2,1)} %slice.243, bf16[448,192]{1,0:T(8,128)(2,1)S(1)} %copy.25, ...), kind=kOutput, calls=%fused_computation | convolution fusion | flops 743424000 | bytes 3358720 | tf_op jit(solution)/shard_map/dot_general | solution.py:25
  145.0 1.9 %multiply_subtract_fusion = (f32[80,640]{1,0:T(8,128)}, f32[80,640]{1,0:T(8,128)}, f32[80,640]{1,0:T(8,128)}, f32[80,640]{1,0:T(8,128)}) fusion(f32[80,640]{1,0:T(8,128)S(1)} %copy-done.26, f32[80,640]{1,0:T(8,128)S(1)} %maximum_select_fusion.1, f32[80,640]{1,0:T(8,128)} %collective-permute-done.39, f32[80,640]{1,0:T(8,128)S(1)} %copy-done.29, ...), kind=kLoop, calls=%fused_computation.20 | loop fusion | flops 870400 | bytes 1843200 | tf_op jit(solution)/shard_map/sub | solution.py:277
  (166 shorter events, 46.1 us)
Async XLA Ops:
  7.3 7.9 %collective-permute-start.12 = (bf16[160,512]{1,0:T(8,128)(2,1)S(1)}, bf16[160,512]{1,0:T(8,128)(2,1)S(1)}, u32[]{:S(2)}, u32[]{:S(2)}) collective-permute-start(bf16[160,512]{1,0:T(8,128)(2,1)S(1)} %slice.239.refs_1_), channel_id=1, source_target_pairs={{0,8},{2,10},{8,16},{10,18},{16,24},{18,26},{24,28},{26,30},{28,20... | collective-permute-start | bytes 491528 | tf_op jit(solution)/shard_map/ppermute | solution.py:160
  10.3 52.9 %collective-permute-start.9 = (bf16[448,1280]{1,0:T(8,128)(2,1)S(1)}, bf16[448,1280]{1,0:T(8,128)(2,1)S(1)}, u32[]{:S(2)}, u32[]{:S(2)}) collective-permute-start(bf16[448,1280]{1,0:T(8,128)(2,1)S(1)} %copy-done), channel_id=1, source_target_pairs={{0,2},{2,0},{4,6},{6,4},{8,10},{10,8},{12,14},{14,12},{16,18},{18,... | collective-permute-start | bytes 3440648 | tf_op jit(solution)/shard_map/ppermute | solution.py:158
  10.3 56.4 %collective-permute-start.10 = (bf16[512,1280]{1,0:T(8,128)(2,1)}, bf16[512,1280]{1,0:T(8,128)(2,1)}, u32[]{:S(2)}, u32[]{:S(2)}) collective-permute-start(bf16[512,1280]{1,0:T(8,128)(2,1)} %refs_12_.3), channel_id=1, source_target_pairs={{0,2},{2,0},{4,6},{6,4},{8,10},{10,8},{12,14},{14,12},{16,18},{18,... | collective-permute-start | bytes 3932168 | tf_op jit(solution)/shard_map/ppermute | solution.py:158
  11.6 12.7 %collective-permute-start.1 = (bf16[160,768]{1,0:T(8,128)(2,1)S(1)}, bf16[160,768]{1,0:T(8,128)(2,1)S(1)}, u32[]{:S(2)}, u32[]{:S(2)}) collective-permute-start(bf16[160,768]{1,0:T(8,128)(2,1)S(1)} %slice.236.refs_1_), channel_id=1, source_target_pairs={{0,8},{2,10},{8,16},{10,18},{16,24},{18,26},{24,28},{26,30},{28,20... | collective-permute-start | bytes 737288 | tf_op jit(solution)/shard_map/ppermute | solution.py:160
  13.2 12.7 %collective-permute-start.2 = (bf16[160,768]{1,0:T(8,128)(2,1)S(1)}, bf16[160,768]{1,0:T(8,128)(2,1)S(1)}, u32[]{:S(2)}, u32[]{:S(2)}) collective-permute-start(bf16[160,768]{1,0:T(8,128)(2,1)S(1)} %slice.236.refs_1_), channel_id=1, source_target_pairs={{0,4},{2,6},{8,0},{10,2},{16,8},{18,10},{24,16},{26,18},{28,24},{3... | collective-permute-start | bytes 737288 | tf_op jit(solution)/shard_map/ppermute | solution.py:161
  15.2 9.0 %collective-permute-start.13 = (bf16[160,512]{1,0:T(8,128)(2,1)S(1)}, bf16[160,512]{1,0:T(8,128)(2,1)S(1)}, u32[]{:S(2)}, u32[]{:S(2)}) collective-permute-start(bf16[160,512]{1,0:T(8,128)(2,1)S(1)} %slice.239.refs_1_), channel_id=1, source_target_pairs={{0,4},{2,6},{8,0},{10,2},{16,8},{18,10},{24,16},{26,18},{28,24},{3... | collective-permute-start | bytes 491528 | tf_op jit(solution)/shard_map/ppermute | solution.py:161
  24.3 42.5 %collective-permute-start.11 = (bf16[448,1280]{1,0:T(8,128)(2,1)S(1)}, bf16[448,1280]{1,0:T(8,128)(2,1)}, u32[]{:S(2)}, u32[]{:S(2)}) collective-permute-start(bf16[448,1280]{1,0:T(8,128)(2,1)S(1)} %broadcast_select_fusion.refs_14_), channel_id=1, source_target_pairs={{0,2},{2,0},{4,6},{6,4},{8,10},{10,8},{12,14},{14,12},{16,18},{18,... | collective-permute-start | bytes 3440648 | tf_op jit(solution)/shard_map/ppermute | solution.py:158
  24.3 6.6 %collective-permute-start.14 = (bf16[160,512]{1,0:T(8,128)(2,1)S(1)}, bf16[160,512]{1,0:T(8,128)(2,1)S(1)}, u32[]{:S(2)}, u32[]{:S(2)}) collective-permute-start(bf16[160,512]{1,0:T(8,128)(2,1)S(1)} %collective-permute-done.12.refs_2_), channel_id=1, source_target_pairs={{0,8},{2,10},{8,16},{10,18},{16,24},{18,26},{24,28},{26,30},{28,20... | collective-permute-start | bytes 491528 | tf_op jit(solution)/shard_map/ppermute | solution.py:160
  25.9 7.3 %collective-permute-start.15 = (bf16[160,512]{1,0:T(8,128)(2,1)S(1)}, bf16[160,512]{1,0:T(8,128)(2,1)S(1)}, u32[]{:S(2)}, u32[]{:S(2)}) collective-permute-start(bf16[160,512]{1,0:T(8,128)(2,1)S(1)} %collective-permute-done.13.refs_3_), channel_id=1, source_target_pairs={{0,4},{2,6},{8,0},{10,2},{16,8},{18,10},{24,16},{26,18},{28,24},{3... | collective-permute-start | bytes 491528 | tf_op jit(solution)/shard_map/ppermute | solution.py:161
  30.9 7.7 %collective-permute-start.3 = (bf16[160,768]{1,0:T(8,128)(2,1)S(1)}, bf16[160,768]{1,0:T(8,128)(2,1)}, u32[]{:S(2)}, u32[]{:S(2)}) collective-permute-start(bf16[160,768]{1,0:T(8,128)(2,1)S(1)} %collective-permute-done.1.refs_2_), channel_id=1, source_target_pairs={{0,8},{2,10},{8,16},{10,18},{16,24},{18,26},{24,28},{26,30},{28,20... | collective-permute-start | bytes 737288 | tf_op jit(solution)/shard_map/ppermute | solution.py:160
  33.2 7.7 %collective-permute-start.4 = (bf16[160,768]{1,0:T(8,128)(2,1)S(1)}, bf16[160,768]{1,0:T(8,128)(2,1)}, u32[]{:S(2)}, u32[]{:S(2)}) collective-permute-start(bf16[160,768]{1,0:T(8,128)(2,1)S(1)} %collective-permute-done.2.refs_3_), channel_id=1, source_target_pairs={{0,4},{2,6},{8,0},{10,2},{16,8},{18,10},{24,16},{26,18},{28,24},{3... | collective-permute-start | bytes 737288 | tf_op jit(solution)/shard_map/ppermute | solution.py:161
  44.0 7.9 %collective-permute-start.5 = (bf16[160,768]{1,0:T(8,128)(2,1)}, bf16[160,768]{1,0:T(8,128)(2,1)}, u32[]{:S(2)}, u32[]{:S(2)}) collective-permute-start(bf16[160,768]{1,0:T(8,128)(2,1)} %collective-permute-done.3.refs_4_), channel_id=1, source_target_pairs={{0,8},{2,10},{8,16},{10,18},{16,24},{18,26},{24,28},{26,30},{28,20... | collective-permute-start | bytes 737288 | tf_op jit(solution)/shard_map/ppermute | solution.py:160
  46.3 7.2 %collective-permute-start.6 = (bf16[160,768]{1,0:T(8,128)(2,1)}, bf16[160,768]{1,0:T(8,128)(2,1)}, u32[]{:S(2)}, u32[]{:S(2)}) collective-permute-start(bf16[160,768]{1,0:T(8,128)(2,1)} %collective-permute-done.4.refs_5_), channel_id=1, source_target_pairs={{0,4},{2,6},{8,0},{10,2},{16,8},{18,10},{24,16},{26,18},{28,24},{3... | collective-permute-start | bytes 737288 | tf_op jit(solution)/shard_map/ppermute | solution.py:161
  51.9 14.4 %collective-permute-start.18 = (bf16[80,512]{1,0:T(8,128)(2,1)}, bf16[80,512]{1,0:T(8,128)(2,1)S(1)}, u32[]{:S(2)}, u32[]{:S(2)}) collective-permute-start(bf16[80,512]{1,0:T(8,128)(2,1)} %slice.240), channel_id=1, source_target_pairs={{0,8},{2,10},{8,16},{10,18},{16,24},{18,26},{24,28},{26,30},{28,20... | collective-permute-start | bytes 245768 | tf_op jit(solution)/shard_map/ppermute | solution.py:160
  53.5 13.3 %collective-permute-start.19 = (bf16[80,512]{1,0:T(8,128)(2,1)}, bf16[80,512]{1,0:T(8,128)(2,1)}, u32[]{:S(2)}, u32[]{:S(2)}) collective-permute-start(bf16[80,512]{1,0:T(8,128)(2,1)} %slice.241), channel_id=1, source_target_pairs={{0,4},{2,6},{8,0},{10,2},{16,8},{18,10},{24,16},{26,18},{28,24},{3... | collective-permute-start | bytes 245768 | tf_op jit(solution)/shard_map/ppermute | solution.py:161
  63.2 24.0 %collective-permute-start.7 = (bf16[80,768]{1,0:T(8,128)(2,1)}, bf16[80,768]{1,0:T(8,128)(2,1)}, u32[]{:S(2)}, u32[]{:S(2)}) collective-permute-start(bf16[80,768]{1,0:T(8,128)(2,1)} %slice.237), channel_id=1, source_target_pairs={{0,8},{2,10},{8,16},{10,18},{16,24},{18,26},{24,28},{26,30},{28,20... | collective-permute-start | bytes 368648 | tf_op jit(solution)/shard_map/ppermute | solution.py:160
  66.3 20.9 %collective-permute-start.8 = (bf16[80,768]{1,0:T(8,128)(2,1)}, bf16[80,768]{1,0:T(8,128)(2,1)S(1)}, u32[]{:S(2)}, u32[]{:S(2)}) collective-permute-start(bf16[80,768]{1,0:T(8,128)(2,1)} %slice.238), channel_id=1, source_target_pairs={{0,4},{2,6},{8,0},{10,2},{16,8},{18,10},{24,16},{26,18},{28,24},{3... | collective-permute-start | bytes 368648 | tf_op jit(solution)/shard_map/ppermute | solution.py:161
  85.6 18.2 %collective-permute-start.30 = (f32[80,128]{1,0:T(8,128)S(1)}, f32[80,128]{1,0:T(8,128)S(1)}, u32[]{:S(2)}, u32[]{:S(2)}) collective-permute-start(f32[80,128]{1,0:T(8,128)S(1)} %get-tuple-element.44), channel_id=1, source_target_pairs={{0,8},{2,10},{8,16},{10,18},{16,24},{18,26},{24,28},{26,30},{28,20... | collective-permute-start | bytes 122888 | tf_op jit(solution)/shard_map/ppermute | solution.py:160
  101.3 7.7 %collective-permute-start.22 = (f32[80,192]{1,0:T(8,128)S(1)}, f32[80,192]{1,0:T(8,128)S(1)}, u32[]{:S(2)}, u32[]{:S(2)}) collective-permute-start(f32[80,192]{1,0:T(8,128)S(1)} %get-tuple-element.35), channel_id=1, source_target_pairs={{0,8},{2,10},{8,16},{10,18},{16,24},{18,26},{24,28},{26,30},{28,20... | collective-permute-start | bytes 184328 | tf_op jit(solution)/shard_map/ppermute | solution.py:160
  102.9 6.7 %collective-permute-start.26 = (f32[80,192]{1,0:T(8,128)S(1)}, f32[80,192]{1,0:T(8,128)S(1)}, u32[]{:S(2)}, u32[]{:S(2)}) collective-permute-start(f32[80,192]{1,0:T(8,128)S(1)} %get-tuple-element.39), channel_id=1, source_target_pairs={{0,4},{2,6},{8,0},{10,2},{16,8},{18,10},{24,16},{26,18},{28,24},{3... | collective-permute-start | bytes 184328 | tf_op jit(solution)/shard_map/ppermute | solution.py:161
  103.9 8.0 %collective-permute-start.31 = (f32[160,128]{1,0:T(8,128)S(1)}, f32[160,128]{1,0:T(8,128)S(1)}, u32[]{:S(2)}, u32[]{:S(2)}) collective-permute-start(f32[160,128]{1,0:T(8,128)S(1)} %pad_maximum_fusion.3), channel_id=1, source_target_pairs={{0,8},{2,10},{8,16},{10,18},{16,24},{18,26},{24,28},{26,30},{28,20... | collective-permute-start | bytes 245768 | tf_op jit(solution)/shard_map/ppermute | solution.py:160
  109.1 9.4 %collective-permute-start.23 = (f32[160,192]{1,0:T(8,128)S(1)}, f32[160,192]{1,0:T(8,128)S(1)}, u32[]{:S(2)}, u32[]{:S(2)}) collective-permute-start(f32[160,192]{1,0:T(8,128)S(1)} %pad_maximum_fusion), channel_id=1, source_target_pairs={{0,8},{2,10},{8,16},{10,18},{16,24},{18,26},{24,28},{26,30},{28,20... | collective-permute-start | bytes 368648 | tf_op jit(solution)/shard_map/ppermute | solution.py:160
  109.6 9.6 %collective-permute-start.27 = (f32[160,192]{1,0:T(8,128)S(1)}, f32[160,192]{1,0:T(8,128)S(1)}, u32[]{:S(2)}, u32[]{:S(2)}) collective-permute-start(f32[160,192]{1,0:T(8,128)S(1)} %pad_maximum_fusion.1), channel_id=1, source_target_pairs={{0,4},{2,6},{8,0},{10,2},{16,8},{18,10},{24,16},{26,18},{28,24},{3... | collective-permute-start | bytes 368648 | tf_op jit(solution)/shard_map/ppermute | solution.py:161
  111.9 10.1 %collective-permute-start.32 = (f32[160,128]{1,0:T(8,128)S(1)}, f32[160,128]{1,0:T(8,128)S(1)}, u32[]{:S(2)}, u32[]{:S(2)}) collective-permute-start(f32[160,128]{1,0:T(8,128)S(1)} %add.91), channel_id=1, source_target_pairs={{0,8},{2,10},{8,16},{10,18},{16,24},{18,26},{24,28},{26,30},{28,20... | collective-permute-start | bytes 245768 | tf_op jit(solution)/shard_map/ppermute | solution.py:160
  119.2 6.4 %collective-permute-start.24 = (f32[160,192]{1,0:T(8,128)}, f32[160,192]{1,0:T(8,128)}, u32[]{:S(2)}, u32[]{:S(2)}) collective-permute-start(f32[160,192]{1,0:T(8,128)} %add.83), channel_id=1, source_target_pairs={{0,8},{2,10},{8,16},{10,18},{16,24},{18,26},{24,28},{26,30},{28,20... | collective-permute-start | bytes 368648 | tf_op jit(solution)/shard_map/ppermute | solution.py:160
  119.9 7.2 %collective-permute-start.28 = (f32[160,192]{1,0:T(8,128)}, f32[160,192]{1,0:T(8,128)}, u32[]{:S(2)}, u32[]{:S(2)}) collective-permute-start(f32[160,192]{1,0:T(8,128)} %add.87), channel_id=1, source_target_pairs={{0,4},{2,6},{8,0},{10,2},{16,8},{18,10},{24,16},{26,18},{28,24},{3... | collective-permute-start | bytes 368648 | tf_op jit(solution)/shard_map/ppermute | solution.py:161
  123.3 7.2 %collective-permute-start.37 = (f32[160,128]{1,0:T(8,128)}, f32[160,128]{1,0:T(8,128)}, u32[]{:S(2)}, u32[]{:S(2)}) collective-permute-start(f32[160,128]{1,0:T(8,128)} %add.96), channel_id=1, source_target_pairs={{0,4},{2,6},{8,0},{10,2},{16,8},{18,10},{24,16},{26,18},{28,24},{3... | collective-permute-start | bytes 245768 | tf_op jit(solution)/shard_map/ppermute | solution.py:161
  125.6 13.4 %collective-permute-start.20 = (bf16[1728,192]{0,1:T(8,128)(2,1)S(1)}, bf16[1728,192]{0,1:T(8,128)(2,1)S(1)}, u32[]{:S(2)}, u32[]{:S(2)}) collective-permute-start(bf16[1728,192]{0,1:T(8,128)(2,1)S(1)} %copy.22), channel_id=1, source_target_pairs={{0,2},{2,0},{4,6},{6,4},{8,10},{10,8},{12,14},{14,12},{16,18},{18,... | collective-permute-start | bytes 1990664 | tf_op jit(solution)/shard_map/ppermute | solution.py:158
  125.7 10.8 %collective-permute-start.21 = (bf16[1728,128]{1,0:T(8,128)(2,1)S(1)}, bf16[1728,128]{1,0:T(8,128)(2,1)S(1)}, u32[]{:S(2)}, u32[]{:S(2)}) collective-permute-start(bf16[1728,128]{1,0:T(8,128)(2,1)S(1)} %copy-done.12), channel_id=1, source_target_pairs={{0,2},{2,0},{4,6},{6,4},{8,10},{10,8},{12,14},{14,12},{16,18},{18,... | collective-permute-start | bytes 1327112 | tf_op jit(solution)/shard_map/ppermute | solution.py:158
  127.1 6.2 %collective-permute-start.25 = (f32[160,192]{1,0:T(8,128)S(1)}, f32[160,192]{1,0:T(8,128)S(1)}, u32[]{:S(2)}, u32[]{:S(2)}) collective-permute-start(f32[160,192]{1,0:T(8,128)S(1)} %add.84), channel_id=1, source_target_pairs={{0,8},{2,10},{8,16},{10,18},{16,24},{18,26},{24,28},{26,30},{28,20... | collective-permute-start | bytes 368648 | tf_op jit(solution)/shard_map/ppermute | solution.py:160
  128.1 6.5 %collective-permute-start.29 = (f32[160,192]{1,0:T(8,128)S(1)}, f32[160,192]{1,0:T(8,128)S(1)}, u32[]{:S(2)}, u32[]{:S(2)}) collective-permute-start(f32[160,192]{1,0:T(8,128)S(1)} %add.88), channel_id=1, source_target_pairs={{0,4},{2,6},{8,0},{10,2},{16,8},{18,10},{24,16},{26,18},{28,24},{3... | collective-permute-start | bytes 368648 | tf_op jit(solution)/shard_map/ppermute | solution.py:161
  137.3 7.6 %collective-permute-start.39 = (f32[80,640]{1,0:T(8,128)S(1)}, f32[80,640]{1,0:T(8,128)}, u32[]{:S(2)}, u32[]{:S(2)}) collective-permute-start(f32[80,640]{1,0:T(8,128)S(1)} %maximum_select_fusion.1), channel_id=1, source_target_pairs={{0,1},{1,0},{2,3},{3,2},{4,5},{5,4},{6,7},{7,6},{8,9},{9,8},{10,11... | collective-permute-start | bytes 614408 | tf_op jit(solution)/shard_map/ppermute | solution.py:270
  (40 other events, 274.5 us)

commit v2 on v0

v2 whole, which is shorter than its diff:
```python
import functools

import jax
import jax.numpy as jnp
from jax import lax
from jax.experimental import pallas as pl
from jax.experimental.pallas import tpu as pltpu
from jax.sharding import PartitionSpec as P

HEADS = 10
HEAD_DIM = 64
TOK = 448
CORES = 2
CORE_HEADS = HEADS // CORES
WIDE = CORE_HEADS * HEAD_DIM
ROOM = 384
RING_MOST = 8

first_fix = 0.9999734386011124
second_fix = 0.8673804441052468
BF = jnp.bfloat16
F32 = jnp.float32
VM = pl.BlockSpec(memory_space=pltpu.VMEM)
SM = pl.BlockSpec(memory_space=pltpu.SMEM)
ANY = pl.BlockSpec(memory_space=pl.ANY)
HBM = pl.BlockSpec(memory_space=pltpu.HBM)
SMALL = pltpu.CompilerParams(vmem_limit_bytes=4 * 2**20)


def dot(a, b, dims=((1,), (0,))):
    return lax.dot_general(a, b, (dims, ((), ())), preferred_element_type=F32)


def ring_order(chips):
    return list(range(0, chips, 2)) + list(range(chips - 1, 0, -2))


def ring_pairs(chips, step):
    order = ring_order(chips)
    return [
        (CORES * order[i] + c, CORES * order[(i + step) % chips] + c)
        for i in range(chips)
        for c in range(CORES)
    ]


def chip_at(me_ref, chips, step):
    chip = me_ref[0] // CORES
    odd = chip % 2
    place = (1 - odd) * (chip // 2) + odd * (chips - 1 - chip // 2)
    place = (place + step + chips) % chips
    back = (place >= chips // 2).astype(jnp.int32)
    return (1 - back) * (2 * place) + back * (2 * (chips - 1 - place) + 1)


def pack_kernel(me, q, k, v, o, keep, send, qv, kv, vv, ov, sem):
    copies = [
        pltpu.make_async_copy(src, dst, sem.at[i])
        for i, (src, dst) in enumerate(((q, qv), (k, kv), (v, vv), (o, ov)))
    ]
    for c in copies:
        c.start()
    for c in copies:
        c.wait()
    first = me[0] % CORES == 0
    parts = (qv[...].astype(BF), kv[...], vv[...], ov[...])
    halves = [jnp.concatenate([w[:, c * WIDE : (c + 1) * WIDE] for w in parts], axis=1) for c in (0, 1)]

    @pl.when(first)
    def _():
        keep[...] = halves[0]
        send[...] = halves[1]

    @pl.when(jnp.logical_not(first))
    def _():
        keep[...] = halves[1]
        send[...] = halves[0]


def turn_kernel(x, t):
    t[...] = x[...].T


def turn(x):
    return pl.pallas_call(
        turn_kernel,
        out_shape=jax.ShapeDtypeStruct(x.shape[::-1], BF),
        in_specs=[VM],
        out_specs=VM,
        compiler_params=pltpu.CompilerParams(vmem_limit_bytes=8 * 2**20),
        cost_estimate=pl.CostEstimate(flops=0, bytes_accessed=5 * 10**6, transcendentals=0),
    )(x)


def join_kernel(me, keep, got, *blocks):
    core = me[0] % CORES
    rows = keep.shape[0]
    cols = keep.shape[1] // len(blocks)
    mine = pl.ds(pl.multiple_of(core * rows, rows), rows)
    other = pl.ds(pl.multiple_of((1 - core) * rows, rows), rows)
    for i, block in enumerate(blocks):
        block[mine, :] = keep[:, i * cols : (i + 1) * cols]
        block[other, :] = got[:, i * cols : (i + 1) * cols]


def head_kernel(chips, steps, pieces, *refs):
    refs = list(refs)
    take = lambda n: [refs.pop(0) for _ in range(n)]
    (me,) = take(1)
    blocks = take(2 * len(steps))
    x0, x1, e0, e1, g0, g1, t0, t1 = take(8)
    share, ctx_own = take(2)
    sums = take(len(pieces))
    wqk, wvo, sem = take(3)
    chip_rows = wqk.shape[0] // chips
    if len(steps) == 1:
        places = [0]
    else:
        places = [pl.multiple_of(chip_at(me, chips, k) * chip_rows, chip_rows) for k in range(chips)]
    copies = []
    for i, k in enumerate(steps):
        for j, w in enumerate((wqk, wvo)):
            b = blocks[2 * i + j]
            at = pl.ds(places[k], b.shape[0])
            copies.append(pltpu.make_async_copy(b, w.at[at, :], sem.at[2 * i + j]))
    for c in copies:
        c.start()
    for c in copies:
        c.wait()
    grads = []
    for xs, es, gs in ((x0, e0, g0), (x1, e1, g1)):
        q = (dot(xs[...], wqk[:, :WIDE]) * 0.125).astype(BF)
        k = dot(es[...], wqk[:, WIDE:]).astype(BF)
        v = dot(es[...], wvo[:, :WIDE]).astype(BF)
        gc = dot(gs[...], wvo[:, WIDE:]).astype(BF)
        ctxs, gqs = [], []
        for h in range(CORE_HEADS):
            cols = slice(h * HEAD_DIM, (h + 1) * HEAD_DIM)
            qh, kh, vh, gh = q[:, cols], k[:, cols], v[:, cols], gc[:, cols]
            s = dot(qh, kh, ((1,), (1,)))
            p = jnp.exp(s - jnp.max(s, axis=1, keepdims=True))
            a = (p * (1.0 / jnp.sum(p, axis=1, keepdims=True))).astype(BF)
            ctx = dot(a, vh)
            ga = dot(gh, vh, ((1,), (1,)))
            inner = jnp.sum(gh.astype(F32) * ctx, axis=1, keepdims=True)
            gsc = (a.astype(F32) * (ga - inner)).astype(BF)
            gqs.append((dot(gsc, kh) * 0.125).astype(BF))
            ctxs.append(ctx.astype(BF))
        grads.append(jnp.concatenate(gqs, axis=1))
        if xs is x0:
            ctx_own[...] = jnp.concatenate(ctxs, axis=1)
        else:
            share[:TOK, :WIDE] = jnp.concatenate(ctxs, axis=1)
    share[TOK:, :WIDE] = wvo[:, WIDE:]
    for out, (k, skip) in zip(sums, pieces):
        rows = pl.ds(places[k] + skip, out.shape[0])
        out[...] = dot(t0[rows, :], grads[0]) + dot(t1[rows, :], grads[1])


def heads(chips, me, blocks, steps, acts, pieces, piece_rows):
    depth = acts[6].shape[0]
    return pl.pallas_call(
        functools.partial(head_kernel, chips, steps, pieces),
        out_shape=(
            jax.ShapeDtypeStruct((TOK + depth, ROOM), BF),
            jax.ShapeDtypeStruct((TOK, WIDE), BF),
        )
        + (jax.ShapeDtypeStruct((piece_rows, WIDE), F32),) * len(pieces),
        in_specs=[SM] + [ANY] * len(blocks) + [VM] * 8,
        out_specs=(VM,) * (2 + len(pieces)),
        scratch_shapes=[
            pltpu.VMEM((depth, 2 * WIDE), BF),
            pltpu.VMEM((depth, 2 * WIDE), BF),
            pltpu.SemaphoreType.DMA((len(blocks),)),
        ],
        compiler_params=pltpu.CompilerParams(vmem_limit_bytes=14 * 2**20),
        cost_estimate=pl.CostEstimate(
            flops=9 * 10**9, bytes_accessed=20 * 10**6, transcendentals=2 * 10**6
        ),
    )(me, *blocks, *acts)


def out_kernel(ctx_own, share, got, out):
    out[...] = (
        dot(ctx_own[...], share[TOK:, :WIDE], ((1,), (1,)))
        + dot(got[:TOK, :WIDE], got[TOK:, :WIDE], ((1,), (1,)))
    ).astype(BF)


def total_kernel(me, own0, r0, l0, own1, r1, l1, keep, send):
    first = me[0] % CORES == 0
    low = own0[...] + r0[...] + l0[...]
    high = own1[...] + r1[...] + l1[...]

    @pl.when(first)
    def _():
        keep[...] = low
        send[...] = high

    @pl.when(jnp.logical_not(first))
    def _():
        keep[...] = high
        send[...] = low


def adam(q_master, q_moment, q_second, summed):
    q_gradient = summed * (1.0 / TOK)
    new_moment = 0.9 * q_moment + 0.1 * q_gradient
    new_second = 0.98 * q_second + 0.02 * q_gradient * q_gradient
    update = new_moment / first_fix / (jnp.sqrt(new_second / second_fix) + 1e-06)
    new_master = q_master - 0.001 * (update + 0.01 * q_master)
    return q_gradient, new_master, new_moment, new_second


def step_kernel(me, keep, keep_y, got, got_y, master, moment, second, *outs):
    core = me[0] % CORES
    mine = keep[...] + keep_y[...]
    other = got[...] + got_y[...]
    for c in range(CORES):

        @pl.when(core == c)
        def _():
            summed = jnp.concatenate([mine, other] if c == 0 else [other, mine], axis=1)
            for out, value in zip(outs, adam(master[...], moment[...], second[...], summed)):
                out[...] = value


def per_device(
    chips,
    reps,
    text_states,
    encoder_frames,
    out_cotangent,
    text_lengths,
    q_master,
    q_moment,
    q_second,
    key_weight,
    value_weight,
    out_weight,
):
    rows, width = q_master.shape
    depth = text_states.shape[1]
    chip_rows = CORES * rows
    index = lax.axis_index("dp")
    me = index.astype(jnp.int32).reshape(1)
    first = index % CORES == 0
    mates = [(i, i ^ 1) for i in range(CORES * chips)]
    swap = lambda a: lax.ppermute(a, "dp", mates)
    ring = 1 < chips <= RING_MOST and reps == 2
    right = lambda a: lax.ppermute(a, "dp", ring_pairs(chips, 1))
    left = lambda a: lax.ppermute(a, "dp", ring_pairs(chips, -1))
    same_core = [[CORES * i + c for i in range(chips)] for c in range(CORES)]

    in_use = jnp.arange(TOK, dtype=jnp.int32) < text_lengths[0]
    grad_out = jnp.where(in_use[:, None], out_cotangent, jnp.zeros_like(out_cotangent))
    x0, e0, g0 = text_states, encoder_frames, grad_out
    x1, e1, g1 = swap(x0), swap(e0), swap(g0)

    if ring:
        keep, send = pl.pallas_call(
            pack_kernel,
            out_shape=(jax.ShapeDtypeStruct((rows, 4 * WIDE), BF),) * 2,
            in_specs=[SM] + [HBM] * 4,
            out_specs=(VM, VM),
            scratch_shapes=[pltpu.VMEM((rows, width), F32)]
            + [pltpu.VMEM((rows, width), BF)] * 3
            + [pltpu.SemaphoreType.DMA((4,))],
            compiler_params=SMALL,
        )(me, q_master, key_weight, value_weight, out_weight.T)
        got, x1, e1, g1 = lax.optimization_barrier((swap(send), x1, e1, g1))
        pair = pl.pallas_call(
            join_kernel,
            out_shape=(jax.ShapeDtypeStruct((chip_rows, 2 * WIDE), BF),) * 2,
            in_specs=[SM] + [VM] * 2,
            out_specs=(VM, VM),
            compiler_params=SMALL,
        )(me, keep, got)
    else:
        parts = (q_master.astype(BF), key_weight, value_weight, out_weight.T)
        packs = [
            jnp.concatenate([w[:, c * WIDE : (c + 1) * WIDE] for w in parts], axis=1)
            for c in range(CORES)
        ]
        keep = jnp.where(first, packs[0], packs[1])
        got = swap(jnp.where(first, packs[1], packs[0]))
        block = jnp.where(
            first, jnp.concatenate([keep, got], axis=0), jnp.concatenate([got, keep], axis=0)
        )
        pair = (block[:, : 2 * WIDE], block[:, 2 * WIDE :])

    acts = (x0, x1, e0, e1, g0, g1, turn(x0), turn(x1))
    if ring:
        far = chips // 2
        steps, blocks = [0], list(pair)
        r = l = pair
        for k in range(1, far):
            r, l = [right(a) for a in r], [left(a) for a in l]
            steps += [chips - k, k]
            blocks += r + l
        steps += [far]
        blocks += [right(r[0]), left(l[1])]
        order = [(k, h * rows) for k in range(far, -1, -1) for h in range(2)]
        order += [(chips - k, h * rows) for k in range(far - 1, 0, -1) for h in range(2)]
        share, ctx_own, *sums = heads(chips, me, blocks, steps, acts, order, rows)
        term = dict(zip(order, sums))
        moves = {}
        for h, (away, back) in ((0, (right, left)), (1, (left, right))):
            sign = 1 if h == 0 else -1
            moves[h] = [away(term[far, h * rows]), back(term[(-sign * (far - 1)) % chips, h * rows])]
        for k in range(far - 1, 0, -1):
            for h, (away, back) in ((0, (right, left)), (1, (left, right))):
                sign = 1 if h == 0 else -1
                a, b = moves[h]
                if k > 1:
                    a = a + term[(sign * k) % chips, h * rows]
                    b = b + term[(-sign * (k - 1)) % chips, h * rows]
                    moves[h] = [away(a), back(b)]
                else:
                    moves[h] = [away(a + term[sign % chips, h * rows]), b]
        keep, send = pl.pallas_call(
            total_kernel,
            out_shape=(jax.ShapeDtypeStruct((rows, WIDE), F32),) * 2,
            in_specs=[SM] + [VM] * 6,
            out_specs=(VM, VM),
            compiler_params=SMALL,
        )(me, term[0, 0], *moves[0], term[0, rows], *moves[1])
        both = ("dp", "rep")
        across = [(i * reps + y, i * reps + (1 - y)) for i in range(CORES * chips) for y in range(reps)]
        cross = [(i * reps + y, (i ^ 1) * reps + (1 - y)) for i in range(CORES * chips) for y in range(reps)]
        got = swap(send)
        keep_y = lax.ppermute(keep, both, across)
        got_y = lax.ppermute(send, both, cross)
    else:
        blocks = [
            lax.all_gather(a, "dp", axis=0, tiled=True, axis_index_groups=same_core) for a in pair
        ]
        share, ctx_own, total = heads(chips, me, blocks, [0], acts, [(0, 0)], depth)
        total = lax.psum_scatter(
            total, "dp", scatter_dimension=0, tiled=True, axis_index_groups=same_core
        )
        keep = jnp.where(first, total[:rows], total[rows:])
        got = swap(jnp.where(first, total[rows:], total[:rows]))
        summed = jnp.where(
            first, jnp.concatenate([keep, got], axis=1), jnp.concatenate([got, keep], axis=1)
        )
        summed = lax.psum(summed, "rep")

    block_out = pl.pallas_call(
        out_kernel,
        out_shape=jax.ShapeDtypeStruct((TOK, depth), BF),
        in_specs=[VM] * 3,
        out_specs=VM,
        compiler_params=pltpu.CompilerParams(vmem_limit_bytes=8 * 2**20),
        cost_estimate=pl.CostEstimate(
            flops=2 * TOK * width * depth, bytes_accessed=4 * 10**6, transcendentals=0
        ),
    )(ctx_own, share, swap(share))
    if ring:
        got, keep_y, got_y, block_out = lax.optimization_barrier((got, keep_y, got_y, block_out))
        results = pl.pallas_call(
            step_kernel,
            out_shape=(jax.ShapeDtypeStruct((rows, width), F32),) * 4,
            in_specs=[SM] + [VM] * 7,
            out_specs=(VM,) * 4,
            compiler_params=SMALL,
        )(me, keep, keep_y, got, got_y, q_master, q_moment, q_second)
    else:
        results = adam(q_master, q_moment, q_second, summed)
    return (block_out, *results)


def solution(mesh):
    in_specs = (
        P(("dp", "rep"), None),
        P(("dp", "rep"), None),
        P(("dp", "rep"), None),
        P(("dp", "rep")),
        P("dp", None),
        P("dp", None),
        P("dp", None),
        P("dp", None),
        P("dp", None),
        P(None, "dp"),
    )
    out_specs = (P(("dp", "rep"), None), P("dp", None), P("dp", None), P("dp", None), P("dp", None))
    return jax.shard_map(
        functools.partial(per_device, mesh.shape["dp"] // CORES, mesh.shape["rep"]),
        mesh=mesh,
        in_specs=in_specs,
        out_specs=out_specs,
        check_vma=False,
    )
```

time: 318 us -> 103 us (0.32)
  waiting for transfers between devices: 239 us -> 35.2 us
  matrix products: 46.8 us -> 0 us
  starting transfers between devices: 0.24 us -> 33.5 us
  Pallas kernels: 0 us -> 28.4 us
  between operations: 14.8 us -> 1.47 us
  other arithmetic: 9.11 us -> 1.66 us
  local copies, waits for them, and re-layouts: 7.48 us -> 2.75 us
    all_gather x4 -> x0, waiting for transfers between devices: 155 us -> none  [the longest x1 41.2 us: per_device(): lax.all_gather(value_weight, 'dp', axis=0, tiled=True)]
    reduce_scatter x1 -> x0, waiting for transfers between devices: 62.1 us -> none  [per_device(): lax.psum_scatter(lax.dot_general(columns, grad_queries, (((0,), (0,)), ((...]
    dot_general x9 -> x0, matrix products: 39.4 us -> none  [the longest x1 11.4 us: per_device(): jnp.einsum('htf,fhd->thd', grad_scores, key_heads, preferred_element_type...]
    ppermute x0 -> x36, waiting for transfers between devices: none -> 35.2 us  [the longest x14 20.3 us: per_device(): left = lambda a: lax.ppermute(a, 'dp', ring_pairs(chips, -1))]
    ppermute x0 -> x36, starting transfers between devices: none -> 33.5 us  [the longest x14 24.9 us: per_device(): right = lambda a: lax.ppermute(a, 'dp', ring_pairs(chips, 1))]
    pallas_call x0 -> x8, Pallas kernels: none -> 28.4 us  [the longest x1 23.1 us: heads(): pl.pallas_call(functools.partial(head_kernel, chips, steps, pieces), out_...]
    psum x1 -> x0, waiting for transfers between devices: 19.9 us -> none  [per_device(): summed = lax.psum(summed, 'rep')]
    sub x1 -> x0, matrix products: 7.35 us -> none  [per_device(): attention = jax.nn.softmax(scores, axis=-1).astype(jnp.bfloat16)]
  transfers between devices with their start and end apart: 6 -> 36, of which waited for: 6 -> 18; matrix products, arithmetic and copies ran while one was open for 6% -> 2% of each run, Pallas kernels for 0% -> 4%
where the time goes in v2:
time: 103 us
  waiting for transfers between devices  35.2 us (34%)
  starting transfers between devices  33.5 us (33%)
  Pallas kernels  28.4 us (28%)
  local copies, waits for them, and re-layouts  2.75 us (3%)
  other arithmetic  1.66 us (2%)
  between operations  1.47 us (1%)
    ppermute x14, starting transfers between devices, per_device(): right = lambda a: lax.ppermute(a, 'dp', ring_pairs(chips, 1))  24.9 us
    pallas_call x1, Pallas kernels, heads(): pl.pallas_call(functools.partial(head_kernel, chips, steps, pieces), out_...  23.1 us
    ppermute x14, waiting for transfers between devices, per_device(): left = lambda a: lax.ppermute(a, 'dp', ring_pairs(chips, -1))  20.3 us
    ppermute x14, waiting for transfers between devices, per_device(): right = lambda a: lax.ppermute(a, 'dp', ring_pairs(chips, 1))  9.82 us
    ppermute x14, starting transfers between devices, per_device(): left = lambda a: lax.ppermute(a, 'dp', ring_pairs(chips, -1))  5.11 us
    ppermute x6, starting transfers between devices, per_device(): swap = lambda a: lax.ppermute(a, 'dp', mates)  2.93 us
    unnamed x18, local copies, waits for them, and re-layouts  2.75 us
    ppermute x1, waiting for transfers between devices, per_device(): keep_y = lax.ppermute(keep, both, across)  2.7 us
  transfers between devices with their start and end apart: 36, of which 18 were waited for; matrix products, arithmetic and copies ran while one was open for 2% of the time, Pallas kernels for 4%

profile of v2, /device:TPU:0, one launch (start us, length us, event | category | flops | bytes accessed | tf_op | source)
XLA Modules:
  0.0 103.0 jit_solution(8033807602548575658)
XLA Ops:
  1.8 1.5 %broadcast_select_fusion.refs_21_ = bf16[448,1280]{1,0:T(8,128)(2,1)S(1)} fusion(bf16[448,1280]{1,0:T(8,128)(2,1)} %param.12, pred[448]{0:T(512)(128)(4,1)S(1)} %iota_compare_fusion), kind=kLoop, calls=%fused_computation | loop fusion | flops 573440 | bytes 2294208 | tf_op jit(solution)/shard_map/jit(_where)/select_n | solution.py:256
  7.6 1.4 %collective-permute-done.got = bf16[80,1280]{1,0:T(8,128)(2,1)S(1)} collective-permute-done((bf16[80,1280]{1,0:T(8,128)(2,1)S(1)}, bf16[80,1280]{1,0:T(8,128)(2,1)S(1)}, u32[]{:S(2)}, u32[]{:S(2)}) %collective-permute-start) | collective-permute-done | bytes 204832 | tf_op jit(solution)/shard_map/ppermute | solution.py:249
  9.1 2.8 %collective-permute-start.4 = (bf16[160,640]{1,0:T(8,128)(2,1)S(1)}, bf16[160,640]{1,0:T(8,128)(2,1)S(1)}, u32[]{:S(2)}, u32[]{:S(2)}) collective-permute-start(bf16[160,640]{1,0:T(8,128)(2,1)S(1)} %get-tuple-element.44.refs_1_), channel_id=1, source_target_pairs={{0,8},{2,10},{8,16},{10,18},{16,24},{18,26},{24,28},{26,30},{28,20... | collective-permute-start | bytes 614408 | tf_op jit(solution)/shard_map/ppermute | solution.py:251
  11.9 1.9 %collective-permute-start.6 = (bf16[160,640]{1,0:T(8,128)(2,1)S(1)}, bf16[160,640]{1,0:T(8,128)(2,1)S(1)}, u32[]{:S(2)}, u32[]{:S(2)}) collective-permute-start(bf16[160,640]{1,0:T(8,128)(2,1)S(1)} %get-tuple-element.44.refs_1_), channel_id=1, source_target_pairs={{0,4},{2,6},{8,0},{10,2},{16,8},{18,10},{24,16},{26,18},{28,24},{3... | collective-permute-start | bytes 614408 | tf_op jit(solution)/shard_map/ppermute | solution.py:252
  13.9 3.8 %collective-permute-done.4.refs_3_ = bf16[160,640]{1,0:T(8,128)(2,1)S(1)} collective-permute-done((bf16[160,640]{1,0:T(8,128)(2,1)S(1)}, bf16[160,640]{1,0:T(8,128)(2,1)S(1)}, u32[]{:S(2)}, u32[]{:S(2)}) %collective-permute-start.4) | collective-permute-done | bytes 204832 | tf_op jit(solution)/shard_map/ppermute | solution.py:251
  17.7 2.1 %collective-permute-start.8 = (bf16[160,640]{1,0:T(8,128)(2,1)S(1)}, bf16[160,640]{1,0:T(8,128)(2,1)S(1)}, u32[]{:S(2)}, u32[]{:S(2)}) collective-permute-start(bf16[160,640]{1,0:T(8,128)(2,1)S(1)} %collective-permute-done.4.refs_3_), channel_id=1, source_target_pairs={{0,8},{2,10},{8,16},{10,18},{16,24},{18,26},{24,28},{26,30},{28,20... | collective-permute-start | bytes 614408 | tf_op jit(solution)/shard_map/ppermute | solution.py:251
  19.8 4.4 %collective-permute-done.6.refs_5_ = bf16[160,640]{1,0:T(8,128)(2,1)S(1)} collective-permute-done((bf16[160,640]{1,0:T(8,128)(2,1)S(1)}, bf16[160,640]{1,0:T(8,128)(2,1)S(1)}, u32[]{:S(2)}, u32[]{:S(2)}) %collective-permute-start.6) | collective-permute-done | bytes 204832 | tf_op jit(solution)/shard_map/ppermute | solution.py:252
  24.2 2.0 %collective-permute-start.9 = (bf16[160,640]{1,0:T(8,128)(2,1)S(1)}, bf16[160,640]{1,0:T(8,128)(2,1)S(1)}, u32[]{:S(2)}, u32[]{:S(2)}) collective-permute-start(bf16[160,640]{1,0:T(8,128)(2,1)S(1)} %collective-permute-done.5.refs_4_), channel_id=1, source_target_pairs={{0,8},{2,10},{8,16},{10,18},{16,24},{18,26},{24,28},{26,30},{28,20... | collective-permute-start | bytes 614408 | tf_op jit(solution)/shard_map/ppermute | solution.py:251
  26.5 2.1 %collective-permute-start.12 = (bf16[160,640]{1,0:T(8,128)(2,1)S(1)}, bf16[160,640]{1,0:T(8,128)(2,1)S(1)}, u32[]{:S(2)}, u32[]{:S(2)}) collective-permute-start(bf16[160,640]{1,0:T(8,128)(2,1)S(1)} %collective-permute-done.8.refs_7_), channel_id=1, source_target_pairs={{0,8},{2,10},{8,16},{10,18},{16,24},{18,26},{24,28},{26,30},{28,20... | collective-permute-start | bytes 614408 | tf_op jit(solution)/shard_map/ppermute | solution.py:251
  28.6 4.4 %collective-permute-done.10.refs_9_ = bf16[160,640]{1,0:T(8,128)(2,1)S(1)} collective-permute-done((bf16[160,640]{1,0:T(8,128)(2,1)S(1)}, bf16[160,640]{1,0:T(8,128)(2,1)S(1)}, u32[]{:S(2)}, u32[]{:S(2)}) %collective-permute-start.10) | collective-permute-done | bytes 204832 | tf_op jit(solution)/shard_map/ppermute | solution.py:252
  33.0 2.0 %collective-permute-start.13 = (bf16[160,640]{1,0:T(8,128)(2,1)S(1)}, bf16[160,640]{1,0:T(8,128)(2,1)S(1)}, u32[]{:S(2)}, u32[]{:S(2)}) collective-permute-start(bf16[160,640]{1,0:T(8,128)(2,1)S(1)} %collective-permute-done.9.refs_8_), channel_id=1, source_target_pairs={{0,8},{2,10},{8,16},{10,18},{16,24},{18,26},{24,28},{26,30},{28,20... | collective-permute-start | bytes 614408 | tf_op jit(solution)/shard_map/ppermute | solution.py:251
  35.5 2.2 %collective-permute-start.16 = (bf16[160,640]{1,0:T(8,128)(2,1)S(1)}, bf16[160,640]{1,0:T(8,128)(2,1)S(1)}, u32[]{:S(2)}, u32[]{:S(2)}) collective-permute-start(bf16[160,640]{1,0:T(8,128)(2,1)S(1)} %collective-permute-done.12.refs_11_), channel_id=1, source_target_pairs={{0,8},{2,10},{8,16},{10,18},{16,24},{18,26},{24,28},{26,30},{28,20... | collective-permute-start | bytes 614408 | tf_op jit(solution)/shard_map/ppermute | solution.py:251
  38.6 3.1 %collective-permute-done.14.refs_13_ = bf16[160,640]{1,0:T(8,128)(2,1)S(1)} collective-permute-done((bf16[160,640]{1,0:T(8,128)(2,1)S(1)}, bf16[160,640]{1,0:T(8,128)(2,1)S(1)}, u32[]{:S(2)}, u32[]{:S(2)}) %collective-permute-start.14) | collective-permute-done | bytes 204832 | tf_op jit(solution)/shard_map/ppermute | solution.py:252
  41.7 2.0 %collective-permute-done.16.refs_15_ = bf16[160,640]{1,0:T(8,128)(2,1)S(1)} collective-permute-done((bf16[160,640]{1,0:T(8,128)(2,1)S(1)}, bf16[160,640]{1,0:T(8,128)(2,1)S(1)}, u32[]{:S(2)}, u32[]{:S(2)}) %collective-permute-start.16) | collective-permute-done | bytes 204832 | tf_op jit(solution)/shard_map/ppermute | solution.py:251
  43.7 1.5 %collective-permute-done.17.refs_16_ = bf16[160,640]{1,0:T(8,128)(2,1)S(1)} collective-permute-done((bf16[160,640]{1,0:T(8,128)(2,1)S(1)}, bf16[160,640]{1,0:T(8,128)(2,1)S(1)}, u32[]{:S(2)}, u32[]{:S(2)}) %collective-permute-start.17) | collective-permute-done | bytes 204832 | tf_op jit(solution)/shard_map/ppermute | solution.py:252
  45.2 23.1 %shard_map.141 = (bf16[1728,384]{1,0:T(8,128)(2,1)S(1)}, bf16[448,320]{1,0:T(8,128)(2,1)S(1)}, f32[80,320]{1,0:T(8,128)S(1)}, f32[80,320]{1,0:T(8,128)S(1)}, f32...) custom-call(s32[1]{0:T(128)} %bitcast.me.refs_0_, ...), custom_call_target="tpu_custom_call" | custom-call | flops 8999999488 | bytes 20000000 | tf_op jit(solution)/shard_map/pallas_call | solution.py:162
  68.4 1.6 %collective-permute-start.18 = (f32[80,320]{1,0:T(8,128)S(1)}, f32[80,320]{1,0:T(8,128)S(1)}, u32[]{:S(2)}, u32[]{:S(2)}) collective-permute-start(f32[80,320]{1,0:T(8,128)S(1)} %get-tuple-element.50), channel_id=1, source_target_pairs={{0,8},{2,10},{8,16},{10,18},{16,24},{18,26},{24,28},{26,30},{28,20... | collective-permute-start | bytes 307208 | tf_op jit(solution)/shard_map/ppermute | solution.py:251
  70.8 1.7 %collective-permute-start.29 = (f32[80,320]{1,0:T(8,128)S(1)}, f32[80,320]{1,0:T(8,128)S(1)}, u32[]{:S(2)}, u32[]{:S(2)}) collective-permute-start(f32[80,320]{1,0:T(8,128)S(1)} %get-tuple-element.62), channel_id=1, source_target_pairs={{0,8},{2,10},{8,16},{10,18},{16,24},{18,26},{24,28},{26,30},{28,20... | collective-permute-start | bytes 307208 | tf_op jit(solution)/shard_map/ppermute | solution.py:251
  72.6 2.1 %collective-permute-done.18 = f32[80,320]{1,0:T(8,128)S(1)} collective-permute-done((f32[80,320]{1,0:T(8,128)S(1)}, f32[80,320]{1,0:T(8,128)S(1)}, u32[]{:S(2)}, u32[]{:S(2)}) %collective-permute-start.18) | collective-permute-done | bytes 102432 | tf_op jit(solution)/shard_map/ppermute | solution.py:251
  74.6 1.6 %collective-permute-start.19 = (f32[80,320]{1,0:T(8,128)S(1)}, f32[80,320]{1,0:T(8,128)S(1)}, u32[]{:S(2)}, u32[]{:S(2)}) collective-permute-start(f32[80,320]{1,0:T(8,128)S(1)} %add.30), channel_id=1, source_target_pairs={{0,8},{2,10},{8,16},{10,18},{16,24},{18,26},{24,28},{26,30},{28,20... | collective-permute-start | bytes 307208 | tf_op jit(solution)/shard_map/ppermute | solution.py:251
  76.8 1.5 %collective-permute-done.22 = f32[80,320]{1,0:T(8,128)S(1)} collective-permute-done((f32[80,320]{1,0:T(8,128)S(1)}, f32[80,320]{1,0:T(8,128)S(1)}, u32[]{:S(2)}, u32[]{:S(2)}) %collective-permute-start.22) | collective-permute-done | bytes 102432 | tf_op jit(solution)/shard_map/ppermute | solution.py:252
  78.8 1.6 %collective-permute-start.30 = (f32[80,320]{1,0:T(8,128)S(1)}, f32[80,320]{1,0:T(8,128)S(1)}, u32[]{:S(2)}, u32[]{:S(2)}) collective-permute-start(f32[80,320]{1,0:T(8,128)S(1)} %add.38), channel_id=1, source_target_pairs={{0,8},{2,10},{8,16},{10,18},{16,24},{18,26},{24,28},{26,30},{28,20... | collective-permute-start | bytes 307208 | tf_op jit(solution)/shard_map/ppermute | solution.py:251
  80.5 1.6 %collective-permute-start.20 = (f32[80,320]{1,0:T(8,128)S(1)}, f32[80,320]{1,0:T(8,128)S(1)}, u32[]{:S(2)}, u32[]{:S(2)}) collective-permute-start(f32[80,320]{1,0:T(8,128)S(1)} %add.31), channel_id=1, source_target_pairs={{0,8},{2,10},{8,16},{10,18},{16,24},{18,26},{24,28},{26,30},{28,20... | collective-permute-start | bytes 307208 | tf_op jit(solution)/shard_map/ppermute | solution.py:251
  82.9 1.7 %collective-permute-done.23 = f32[80,320]{1,0:T(8,128)S(1)} collective-permute-done((f32[80,320]{1,0:T(8,128)S(1)}, f32[80,320]{1,0:T(8,128)S(1)}, u32[]{:S(2)}, u32[]{:S(2)}) %collective-permute-start.23) | collective-permute-done | bytes 102432 | tf_op jit(solution)/shard_map/ppermute | solution.py:252
  85.1 1.6 %collective-permute-start.31 = (f32[80,320]{1,0:T(8,128)S(1)}, f32[80,320]{1,0:T(8,128)S(1)}, u32[]{:S(2)}, u32[]{:S(2)}) collective-permute-start(f32[80,320]{1,0:T(8,128)S(1)} %add.39), channel_id=1, source_target_pairs={{0,8},{2,10},{8,16},{10,18},{16,24},{18,26},{24,28},{26,30},{28,20... | collective-permute-start | bytes 307208 | tf_op jit(solution)/shard_map/ppermute | solution.py:251
  86.7 1.7 %collective-permute-start.21 = (f32[80,320]{1,0:T(8,128)S(1)}, f32[80,320]{1,0:T(8,128)S(1)}, u32[]{:S(2)}, u32[]{:S(2)}) collective-permute-start(f32[80,320]{1,0:T(8,128)S(1)} %add.32), channel_id=1, source_target_pairs={{0,8},{2,10},{8,16},{10,18},{16,24},{18,26},{24,28},{26,30},{28,20... | collective-permute-start | bytes 307208 | tf_op jit(solution)/shard_map/ppermute | solution.py:251
  88.9 1.6 %collective-permute-done.24.l0 = f32[80,320]{1,0:T(8,128)S(1)} collective-permute-done((f32[80,320]{1,0:T(8,128)S(1)}, f32[80,320]{1,0:T(8,128)S(1)}, u32[]{:S(2)}, u32[]{:S(2)}) %collective-permute-start.24) | collective-permute-done | bytes 102432 | tf_op jit(solution)/shard_map/ppermute | solution.py:252
  91.7 1.7 %collective-permute-done.28.r1 = f32[80,320]{1,0:T(8,128)S(1)} collective-permute-done((f32[80,320]{1,0:T(8,128)S(1)}, f32[80,320]{1,0:T(8,128)S(1)}, u32[]{:S(2)}, u32[]{:S(2)}) %collective-permute-start.28) | collective-permute-done | bytes 102432 | tf_op jit(solution)/shard_map/ppermute | solution.py:252
  93.6 1.6 %collective-permute-start.32 = (f32[80,320]{1,0:T(8,128)S(1)}, f32[80,320]{1,0:T(8,128)S(1)}, u32[]{:S(2)}, u32[]{:S(2)}) collective-permute-start(f32[80,320]{1,0:T(8,128)S(1)} %get-tuple-element.65), channel_id=1, source_target_pairs={{0,2},{2,0},{4,6},{6,4},{8,10},{10,8},{12,14},{14,12},{16,18},{18,... | collective-permute-start | bytes 307208 | tf_op jit(solution)/shard_map/ppermute | solution.py:249
  95.7 2.4 %shard_map.143 = bf16[448,1280]{1,0:T(8,128)(2,1)} custom-call(bf16[448,320]{1,0:T(8,128)(2,1)S(1)} %get-tuple-element.67.ctx_own, bf16[1728,384]{1,0:T(8,128)(2,1)S(1)} %get-tuple-element.68.share, bf16[1728,384]{1,0:T(8,128)(2,1)S(1)} %collective-permute-done.35.got), custom_call_target="tpu_custom_call" | custom-call | flops 734003200 | bytes 4000000 | tf_op jit(solution)/shard_map/pallas_call | solution.py:349
  99.1 2.7 %collective-permute-done.33.keep_y = f32[80,320]{1,0:T(8,128)S(1)} collective-permute-done((f32[80,320]{1,0:T(8,128)S(1)}, f32[80,320]{1,0:T(8,128)S(1)}, u32[]{:S(2)}, u32[]{:S(2)}) %collective-permute-start.33) | collective-permute-done | bytes 102432 | tf_op jit(solution)/shard_map/ppermute | solution.py:332
  101.8 1.2 %shard_map.144 = (f32[80,640]{1,0:T(8,128)}, f32[80,640]{1,0:T(8,128)}, f32[80,640]{1,0:T(8,128)}, f32[80,640]{1,0:T(8,128)}) custom-call(s32[1]{0:T(128)} %bitcast.me.refs_0_, f32[80,320]{1,0:T(8,128)S(1)} %get-tuple-element.66.keep, f32[80,320]{1,0:T(8,128)S(1)} %collective-permute-done.33.keep_y, f32[80,320]{1,0:T(8,128)S(1)} %collective-permute-done.32.got, ...), custom_call_target="tpu_custom_call" | custom-call | tf_op jit(solution)/shard_map/pallas_call | solution.py:361
  (78 shorter events, 13.2 us)
Async XLA Ops:
  0.6 8.4 %collective-permute-start.2 = (bf16[512,1280]{1,0:T(8,128)(2,1)}, bf16[512,1280]{1,0:T(8,128)(2,1)}, u32[]{:S(2)}, u32[]{:S(2)}) collective-permute-start(bf16[512,1280]{1,0:T(8,128)(2,1)} %refs_19_.1), channel_id=1, source_target_pairs={{0,2},{2,0},{4,6},{6,4},{8,10},{10,8},{12,14},{14,12},{16,18},{18,... | collective-permute-start | bytes 3932168 | tf_op jit(solution)/shard_map/ppermute | solution.py:249
  3.3 5.7 %collective-permute-start.3 = (bf16[448,1280]{1,0:T(8,128)(2,1)S(1)}, bf16[448,1280]{1,0:T(8,128)(2,1)}, u32[]{:S(2)}, u32[]{:S(2)}) collective-permute-start(bf16[448,1280]{1,0:T(8,128)(2,1)S(1)} %broadcast_select_fusion.refs_21_), channel_id=1, source_target_pairs={{0,2},{2,0},{4,6},{6,4},{8,10},{10,8},{12,14},{14,12},{16,18},{18,... | collective-permute-start | bytes 3440648 | tf_op jit(solution)/shard_map/ppermute | solution.py:249
  3.5 5.5 %collective-permute-start.1 = (bf16[448,1280]{1,0:T(8,128)(2,1)S(1)}, bf16[448,1280]{1,0:T(8,128)(2,1)S(1)}, u32[]{:S(2)}, u32[]{:S(2)}) collective-permute-start(bf16[448,1280]{1,0:T(8,128)(2,1)S(1)} %copy-done), channel_id=1, source_target_pairs={{0,2},{2,0},{4,6},{6,4},{8,10},{10,8},{12,14},{14,12},{16,18},{18,... | collective-permute-start | bytes 3440648 | tf_op jit(solution)/shard_map/ppermute | solution.py:249
  9.1 8.6 %collective-permute-start.4 = (bf16[160,640]{1,0:T(8,128)(2,1)S(1)}, bf16[160,640]{1,0:T(8,128)(2,1)S(1)}, u32[]{:S(2)}, u32[]{:S(2)}) collective-permute-start(bf16[160,640]{1,0:T(8,128)(2,1)S(1)} %get-tuple-element.44.refs_1_), channel_id=1, source_target_pairs={{0,8},{2,10},{8,16},{10,18},{16,24},{18,26},{24,28},{26,30},{28,20... | collective-permute-start | bytes 614408 | tf_op jit(solution)/shard_map/ppermute | solution.py:251
  11.8 7.9 %collective-permute-start.7 = (bf16[160,640]{1,0:T(8,128)(2,1)S(1)}, bf16[160,640]{1,0:T(8,128)(2,1)S(1)}, u32[]{:S(2)}, u32[]{:S(2)}) collective-permute-start(bf16[160,640]{1,0:T(8,128)(2,1)S(1)} %get-tuple-element.45.refs_2_), channel_id=1, source_target_pairs={{0,4},{2,6},{8,0},{10,2},{16,8},{18,10},{24,16},{26,18},{28,24},{3... | collective-permute-start | bytes 614408 | tf_op jit(solution)/shard_map/ppermute | solution.py:252
  11.9 12.3 %collective-permute-start.6 = (bf16[160,640]{1,0:T(8,128)(2,1)S(1)}, bf16[160,640]{1,0:T(8,128)(2,1)S(1)}, u32[]{:S(2)}, u32[]{:S(2)}) collective-permute-start(bf16[160,640]{1,0:T(8,128)(2,1)S(1)} %get-tuple-element.44.refs_1_), channel_id=1, source_target_pairs={{0,4},{2,6},{8,0},{10,2},{16,8},{18,10},{24,16},{26,18},{28,24},{3... | collective-permute-start | bytes 614408 | tf_op jit(solution)/shard_map/ppermute | solution.py:252
  13.8 10.4 %collective-permute-start.5 = (bf16[160,640]{1,0:T(8,128)(2,1)S(1)}, bf16[160,640]{1,0:T(8,128)(2,1)S(1)}, u32[]{:S(2)}, u32[]{:S(2)}) collective-permute-start(bf16[160,640]{1,0:T(8,128)(2,1)S(1)} %get-tuple-element.45.refs_2_), channel_id=1, source_target_pairs={{0,8},{2,10},{8,16},{10,18},{16,24},{18,26},{24,28},{26,30},{28,20... | collective-permute-start | bytes 614408 | tf_op jit(solution)/shard_map/ppermute | solution.py:251
  17.7 8.8 %collective-permute-start.8 = (bf16[160,640]{1,0:T(8,128)(2,1)S(1)}, bf16[160,640]{1,0:T(8,128)(2,1)S(1)}, u32[]{:S(2)}, u32[]{:S(2)}) collective-permute-start(bf16[160,640]{1,0:T(8,128)(2,1)S(1)} %collective-permute-done.4.refs_3_), channel_id=1, source_target_pairs={{0,8},{2,10},{8,16},{10,18},{16,24},{18,26},{24,28},{26,30},{28,20... | collective-permute-start | bytes 614408 | tf_op jit(solution)/shard_map/ppermute | solution.py:251
  19.8 8.8 %collective-permute-start.11 = (bf16[160,640]{1,0:T(8,128)(2,1)S(1)}, bf16[160,640]{1,0:T(8,128)(2,1)S(1)}, u32[]{:S(2)}, u32[]{:S(2)}) collective-permute-start(bf16[160,640]{1,0:T(8,128)(2,1)S(1)} %collective-permute-done.7.refs_6_), channel_id=1, source_target_pairs={{0,4},{2,6},{8,0},{10,2},{16,8},{18,10},{24,16},{26,18},{28,24},{3... | collective-permute-start | bytes 614408 | tf_op jit(solution)/shard_map/ppermute | solution.py:252
  24.2 8.8 %collective-permute-start.10 = (bf16[160,640]{1,0:T(8,128)(2,1)S(1)}, bf16[160,640]{1,0:T(8,128)(2,1)S(1)}, u32[]{:S(2)}, u32[]{:S(2)}) collective-permute-start(bf16[160,640]{1,0:T(8,128)(2,1)S(1)} %collective-permute-done.6.refs_5_), channel_id=1, source_target_pairs={{0,4},{2,6},{8,0},{10,2},{16,8},{18,10},{24,16},{26,18},{28,24},{3... | collective-permute-start | bytes 614408 | tf_op jit(solution)/shard_map/ppermute | solution.py:252
  24.2 8.8 %collective-permute-start.9 = (bf16[160,640]{1,0:T(8,128)(2,1)S(1)}, bf16[160,640]{1,0:T(8,128)(2,1)S(1)}, u32[]{:S(2)}, u32[]{:S(2)}) collective-permute-start(bf16[160,640]{1,0:T(8,128)(2,1)S(1)} %collective-permute-done.5.refs_4_), channel_id=1, source_target_pairs={{0,8},{2,10},{8,16},{10,18},{16,24},{18,26},{24,28},{26,30},{28,20... | collective-permute-start | bytes 614408 | tf_op jit(solution)/shard_map/ppermute | solution.py:251
  26.5 9.1 %collective-permute-start.12 = (bf16[160,640]{1,0:T(8,128)(2,1)S(1)}, bf16[160,640]{1,0:T(8,128)(2,1)S(1)}, u32[]{:S(2)}, u32[]{:S(2)}) collective-permute-start(bf16[160,640]{1,0:T(8,128)(2,1)S(1)} %collective-permute-done.8.refs_7_), channel_id=1, source_target_pairs={{0,8},{2,10},{8,16},{10,18},{16,24},{18,26},{24,28},{26,30},{28,20... | collective-permute-start | bytes 614408 | tf_op jit(solution)/shard_map/ppermute | solution.py:251
  28.6 9.2 %collective-permute-start.15 = (bf16[160,640]{1,0:T(8,128)(2,1)S(1)}, bf16[160,640]{1,0:T(8,128)(2,1)S(1)}, u32[]{:S(2)}, u32[]{:S(2)}) collective-permute-start(bf16[160,640]{1,0:T(8,128)(2,1)S(1)} %collective-permute-done.11.refs_10_), channel_id=1, source_target_pairs={{0,4},{2,6},{8,0},{10,2},{16,8},{18,10},{24,16},{26,18},{28,24},{3... | collective-permute-start | bytes 614408 | tf_op jit(solution)/shard_map/ppermute | solution.py:252
  32.9 8.8 %collective-permute-start.14 = (bf16[160,640]{1,0:T(8,128)(2,1)S(1)}, bf16[160,640]{1,0:T(8,128)(2,1)S(1)}, u32[]{:S(2)}, u32[]{:S(2)}) collective-permute-start(bf16[160,640]{1,0:T(8,128)(2,1)S(1)} %collective-permute-done.10.refs_9_), channel_id=1, source_target_pairs={{0,4},{2,6},{8,0},{10,2},{16,8},{18,10},{24,16},{26,18},{28,24},{3... | collective-permute-start | bytes 614408 | tf_op jit(solution)/shard_map/ppermute | solution.py:252
  33.0 8.8 %collective-permute-start.13 = (bf16[160,640]{1,0:T(8,128)(2,1)S(1)}, bf16[160,640]{1,0:T(8,128)(2,1)S(1)}, u32[]{:S(2)}, u32[]{:S(2)}) collective-permute-start(bf16[160,640]{1,0:T(8,128)(2,1)S(1)} %collective-permute-done.9.refs_8_), channel_id=1, source_target_pairs={{0,8},{2,10},{8,16},{10,18},{16,24},{18,26},{24,28},{26,30},{28,20... | collective-permute-start | bytes 614408 | tf_op jit(solution)/shard_map/ppermute | solution.py:251
  35.5 8.2 %collective-permute-start.16 = (bf16[160,640]{1,0:T(8,128)(2,1)S(1)}, bf16[160,640]{1,0:T(8,128)(2,1)S(1)}, u32[]{:S(2)}, u32[]{:S(2)}) collective-permute-start(bf16[160,640]{1,0:T(8,128)(2,1)S(1)} %collective-permute-done.12.refs_11_), channel_id=1, source_target_pairs={{0,8},{2,10},{8,16},{10,18},{16,24},{18,26},{24,28},{26,30},{28,20... | collective-permute-start | bytes 614408 | tf_op jit(solution)/shard_map/ppermute | solution.py:251
  37.8 7.5 %collective-permute-start.17 = (bf16[160,640]{1,0:T(8,128)(2,1)S(1)}, bf16[160,640]{1,0:T(8,128)(2,1)S(1)}, u32[]{:S(2)}, u32[]{:S(2)}) collective-permute-start(bf16[160,640]{1,0:T(8,128)(2,1)S(1)} %collective-permute-done.15.refs_14_), channel_id=1, source_target_pairs={{0,4},{2,6},{8,0},{10,2},{16,8},{18,10},{24,16},{26,18},{28,24},{3... | collective-permute-start | bytes 614408 | tf_op jit(solution)/shard_map/ppermute | solution.py:252
  68.4 27.3 %collective-permute-start.35 = (bf16[1728,384]{1,0:T(8,128)(2,1)S(1)}, bf16[1728,384]{1,0:T(8,128)(2,1)S(1)}, u32[]{:S(2)}, u32[]{:S(2)}) collective-permute-start(bf16[1728,384]{1,0:T(8,128)(2,1)S(1)} %get-tuple-element.68.share), channel_id=1, source_target_pairs={{0,2},{2,0},{4,6},{6,4},{8,10},{10,8},{12,14},{14,12},{16,18},{18,... | collective-permute-start | bytes 3981320 | tf_op jit(solution)/shard_map/ppermute | solution.py:249
  68.4 6.2 %collective-permute-start.18 = (f32[80,320]{1,0:T(8,128)S(1)}, f32[80,320]{1,0:T(8,128)S(1)}, u32[]{:S(2)}, u32[]{:S(2)}) collective-permute-start(f32[80,320]{1,0:T(8,128)S(1)} %get-tuple-element.50), channel_id=1, source_target_pairs={{0,8},{2,10},{8,16},{10,18},{16,24},{18,26},{24,28},{26,30},{28,20... | collective-permute-start | bytes 307208 | tf_op jit(solution)/shard_map/ppermute | solution.py:251
  70.1 6.2 %collective-permute-start.25 = (f32[80,320]{1,0:T(8,128)S(1)}, f32[80,320]{1,0:T(8,128)S(1)}, u32[]{:S(2)}, u32[]{:S(2)}) collective-permute-start(f32[80,320]{1,0:T(8,128)S(1)} %get-tuple-element.58), channel_id=1, source_target_pairs={{0,4},{2,6},{8,0},{10,2},{16,8},{18,10},{24,16},{26,18},{28,24},{3... | collective-permute-start | bytes 307208 | tf_op jit(solution)/shard_map/ppermute | solution.py:252
  70.5 7.7 %collective-permute-start.22 = (f32[80,320]{1,0:T(8,128)S(1)}, f32[80,320]{1,0:T(8,128)S(1)}, u32[]{:S(2)}, u32[]{:S(2)}) collective-permute-start(f32[80,320]{1,0:T(8,128)S(1)} %get-tuple-element.54), channel_id=1, source_target_pairs={{0,4},{2,6},{8,0},{10,2},{16,8},{18,10},{24,16},{26,18},{28,24},{3... | collective-permute-start | bytes 307208 | tf_op jit(solution)/shard_map/ppermute | solution.py:252
  70.8 8.0 %collective-permute-start.29 = (f32[80,320]{1,0:T(8,128)S(1)}, f32[80,320]{1,0:T(8,128)S(1)}, u32[]{:S(2)}, u32[]{:S(2)}) collective-permute-start(f32[80,320]{1,0:T(8,128)S(1)} %get-tuple-element.62), channel_id=1, source_target_pairs={{0,8},{2,10},{8,16},{10,18},{16,24},{18,26},{24,28},{26,30},{28,20... | collective-permute-start | bytes 307208 | tf_op jit(solution)/shard_map/ppermute | solution.py:251
  74.6 5.8 %collective-permute-start.19 = (f32[80,320]{1,0:T(8,128)S(1)}, f32[80,320]{1,0:T(8,128)S(1)}, u32[]{:S(2)}, u32[]{:S(2)}) collective-permute-start(f32[80,320]{1,0:T(8,128)S(1)} %add.30), channel_id=1, source_target_pairs={{0,8},{2,10},{8,16},{10,18},{16,24},{18,26},{24,28},{26,30},{28,20... | collective-permute-start | bytes 307208 | tf_op jit(solution)/shard_map/ppermute | solution.py:251
  76.3 6.1 %collective-permute-start.26 = (f32[80,320]{1,0:T(8,128)S(1)}, f32[80,320]{1,0:T(8,128)S(1)}, u32[]{:S(2)}, u32[]{:S(2)}) collective-permute-start(f32[80,320]{1,0:T(8,128)S(1)} %add.35), channel_id=1, source_target_pairs={{0,4},{2,6},{8,0},{10,2},{16,8},{18,10},{24,16},{26,18},{28,24},{3... | collective-permute-start | bytes 307208 | tf_op jit(solution)/shard_map/ppermute | solution.py:252
  78.3 6.3 %collective-permute-start.23 = (f32[80,320]{1,0:T(8,128)S(1)}, f32[80,320]{1,0:T(8,128)S(1)}, u32[]{:S(2)}, u32[]{:S(2)}) collective-permute-start(f32[80,320]{1,0:T(8,128)S(1)} %add.33), channel_id=1, source_target_pairs={{0,4},{2,6},{8,0},{10,2},{16,8},{18,10},{24,16},{26,18},{28,24},{3... | collective-permute-start | bytes 307208 | tf_op jit(solution)/shard_map/ppermute | solution.py:252
  78.8 6.3 %collective-permute-start.30 = (f32[80,320]{1,0:T(8,128)S(1)}, f32[80,320]{1,0:T(8,128)S(1)}, u32[]{:S(2)}, u32[]{:S(2)}) collective-permute-start(f32[80,320]{1,0:T(8,128)S(1)} %add.38), channel_id=1, source_target_pairs={{0,8},{2,10},{8,16},{10,18},{16,24},{18,26},{24,28},{26,30},{28,20... | collective-permute-start | bytes 307208 | tf_op jit(solution)/shard_map/ppermute | solution.py:251
  80.5 6.3 %collective-permute-start.20 = (f32[80,320]{1,0:T(8,128)S(1)}, f32[80,320]{1,0:T(8,128)S(1)}, u32[]{:S(2)}, u32[]{:S(2)}) collective-permute-start(f32[80,320]{1,0:T(8,128)S(1)} %add.31), channel_id=1, source_target_pairs={{0,8},{2,10},{8,16},{10,18},{16,24},{18,26},{24,28},{26,30},{28,20... | collective-permute-start | bytes 307208 | tf_op jit(solution)/shard_map/ppermute | solution.py:251
  82.4 6.1 %collective-permute-start.27 = (f32[80,320]{1,0:T(8,128)S(1)}, f32[80,320]{1,0:T(8,128)S(1)}, u32[]{:S(2)}, u32[]{:S(2)}) collective-permute-start(f32[80,320]{1,0:T(8,128)S(1)} %add.36), channel_id=1, source_target_pairs={{0,4},{2,6},{8,0},{10,2},{16,8},{18,10},{24,16},{26,18},{28,24},{3... | collective-permute-start | bytes 307208 | tf_op jit(solution)/shard_map/ppermute | solution.py:252
  84.6 5.9 %collective-permute-start.24 = (f32[80,320]{1,0:T(8,128)S(1)}, f32[80,320]{1,0:T(8,128)S(1)}, u32[]{:S(2)}, u32[]{:S(2)}) collective-permute-start(f32[80,320]{1,0:T(8,128)S(1)} %add.34), channel_id=1, source_target_pairs={{0,4},{2,6},{8,0},{10,2},{16,8},{18,10},{24,16},{26,18},{28,24},{3... | collective-permute-start | bytes 307208 | tf_op jit(solution)/shard_map/ppermute | solution.py:252
  93.5 5.6 %collective-permute-start.34 = (f32[80,320]{1,0:T(8,128)S(1)}, f32[80,320]{1,0:T(8,128)S(1)}, u32[]{:S(2)}, u32[]{:S(2)}) collective-permute-start(f32[80,320]{1,0:T(8,128)S(1)} %get-tuple-element.65), channel_id=1, source_target_pairs={{0,3},{1,2},{2,1},{3,0},{4,7},{5,6},{6,5},{7,4},{8,11},{9,10},{10,... | collective-permute-start | bytes 307208 | tf_op jit(solution)/shard_map/ppermute | solution.py:333
  93.6 5.5 %collective-permute-start.32 = (f32[80,320]{1,0:T(8,128)S(1)}, f32[80,320]{1,0:T(8,128)S(1)}, u32[]{:S(2)}, u32[]{:S(2)}) collective-permute-start(f32[80,320]{1,0:T(8,128)S(1)} %get-tuple-element.65), channel_id=1, source_target_pairs={{0,2},{2,0},{4,6},{6,4},{8,10},{10,8},{12,14},{14,12},{16,18},{18,... | collective-permute-start | bytes 307208 | tf_op jit(solution)/shard_map/ppermute | solution.py:249
  95.2 6.6 %collective-permute-start.33 = (f32[80,320]{1,0:T(8,128)S(1)}, f32[80,320]{1,0:T(8,128)S(1)}, u32[]{:S(2)}, u32[]{:S(2)}) collective-permute-start(f32[80,320]{1,0:T(8,128)S(1)} %get-tuple-element.66.keep), channel_id=1, source_target_pairs={{0,1},{1,0},{2,3},{3,2},{4,5},{5,4},{6,7},{7,6},{8,9},{9,8},{10,11... | collective-permute-start | bytes 307208 | tf_op jit(solution)/shard_map/ppermute | solution.py:332
  (13 other events, 48.7 us)

commit v3 on v2

v3 whole, which is shorter than its diff:
```python
import functools

import jax
import jax.numpy as jnp
from jax import lax
from jax.experimental import pallas as pl
from jax.experimental.pallas import tpu as pltpu
from jax.sharding import PartitionSpec as P

HEADS = 10
HEAD_DIM = 64
TOK = 448
CORES = 2
CORE_HEADS = HEADS // CORES
WIDE = CORE_HEADS * HEAD_DIM
CHAINS = 2
RING_MOST = 8

first_fix = 0.9999734386011124
second_fix = 0.8673804441052468
BF = jnp.bfloat16
F32 = jnp.float32
VM = pl.BlockSpec(memory_space=pltpu.VMEM)
SM = pl.BlockSpec(memory_space=pltpu.SMEM)
ANY = pl.BlockSpec(memory_space=pl.ANY)
HBM = pl.BlockSpec(memory_space=pltpu.HBM)
SMALL = pltpu.CompilerParams(vmem_limit_bytes=4 * 2**20)


ROWS = ((1,), (1,))


def padded(width):
    return -(-width // 128) * 128


def dot(a, b, dims=((1,), (0,))):
    return lax.dot_general(a, b, (dims, ((), ())), preferred_element_type=F32)


def ring_order(chips):
    return list(range(0, chips, 2)) + list(range(chips - 1, 0, -2))


def ring_pairs(chips, step):
    order = ring_order(chips)
    return [
        (CORES * order[i] + c, CORES * order[(i + step) % chips] + c)
        for i in range(chips)
        for c in range(CORES)
    ]


def chip_at(me_ref, chips, step):
    chip = me_ref[0] // CORES
    odd = chip % 2
    place = (1 - odd) * (chip // 2) + odd * (chips - 1 - chip // 2)
    place = (place + step + chips) % chips
    back = (place >= chips // 2).astype(jnp.int32)
    return (1 - back) * (2 * place) + back * (2 * (chips - 1 - place) + 1)


def pack(parts, core):
    return jnp.concatenate([w[:, core * WIDE : (core + 1) * WIDE] for w in parts], axis=1)


def pack_kernel(me, q, k, v, o, keep, send, qv, kv, vv, ov, sem):
    copies = [
        pltpu.make_async_copy(src, dst, sem.at[i])
        for i, (src, dst) in enumerate(((q, qv), (k, kv), (v, vv), (o, ov)))
    ]
    for c in copies:
        c.start()
    for c in copies:
        c.wait()
    first = me[0] % CORES == 0
    parts = (qv[...].astype(BF), kv[...], vv[...], ov[...])
    halves = [pack(parts, c) for c in range(CORES)]

    @pl.when(first)
    def _():
        keep[...] = halves[0]
        send[...] = halves[1]

    @pl.when(jnp.logical_not(first))
    def _():
        keep[...] = halves[1]
        send[...] = halves[0]


def turn_kernel(x, t):
    t[...] = x[...].T


def turn(x):
    return pl.pallas_call(
        turn_kernel,
        out_shape=jax.ShapeDtypeStruct(x.shape[::-1], BF),
        in_specs=[VM],
        out_specs=VM,
        compiler_params=pltpu.CompilerParams(vmem_limit_bytes=8 * 2**20),
        cost_estimate=pl.CostEstimate(flops=0, bytes_accessed=5 * 10**6, transcendentals=0),
    )(x)


def join_kernel(me, keep, got, *blocks):
    core = me[0] % CORES
    rows = keep.shape[0]
    mine = pl.ds(pl.multiple_of(core * rows, rows), rows)
    other = pl.ds(pl.multiple_of((1 - core) * rows, rows), rows)
    at = 0
    for block in blocks:
        cols = slice(at, at + block.shape[1])
        block[mine, :] = keep[:, cols]
        block[other, :] = got[:, cols]
        at += block.shape[1]


def head_kernel(chips, steps, pieces, *refs):
    refs = list(refs)
    take = lambda n: [refs.pop(0) for _ in range(n)]
    (me,) = take(1)
    chains = [take(len(s)) for s in steps]
    x0, x1, e0, e1, g0, g1, t0, t1 = take(8)
    share, ctx_own = take(2)
    sums = take(len(pieces))
    (w,) = take(1)
    number, width = CORE_HEADS, WIDE
    chip_rows = w.shape[0] // chips
    if len(steps[0]) == 1:
        places = [0]
    else:
        places = [pl.multiple_of(chip_at(me, chips, k) * chip_rows, chip_rows) for k in range(chips)]
    cols = w.shape[1] // len(chains)
    for i, blocks in enumerate(chains):
        for k, block in zip(steps[i], blocks):
            w[pl.ds(places[k], block.shape[0]), i * cols : (i + 1) * cols] = block[...]

    acts = ((x0, e0, g0), (x1, e1, g1))
    rows_of = []
    for xs, es, gs in acts:
        q = (dot(xs[...], w[:, :width]) * 0.125).astype(BF)
        kv = dot(es[...], w[:, width : 3 * width]).astype(BF)
        g = dot(gs[...], w[:, 3 * width :]).astype(BF)
        k, v = kv[:, :width], kv[:, width:]
        rows_of.append((q, k, v, g, k.T, v.T, g.T))

    def begin(clip, h):
        q, k, v, g, _, _, _ = rows_of[clip]
        cols = slice(h * HEAD_DIM, (h + 1) * HEAD_DIM)
        return dot(k[:, cols], q[:, cols], ROWS), dot(v[:, cols], g[:, cols], ROWS)

    def finish(clip, h, scores, grad_attention):
        _, _, _, _, kt, vt, gt = rows_of[clip]
        cols = slice(h * HEAD_DIM, (h + 1) * HEAD_DIM)
        e = jnp.exp(scores - jnp.max(scores, axis=0, keepdims=True))
        attention = (e * (1.0 / jnp.sum(e, axis=0, keepdims=True))).astype(BF)
        ctx = dot(vt[cols], attention)
        inner = jnp.sum(gt[cols].astype(F32) * ctx, axis=0, keepdims=True)
        grad_scores = (attention.astype(F32) * (grad_attention - inner)).astype(BF)
        return ctx.astype(BF), (dot(kt[cols], grad_scores) * 0.125).astype(BF)

    items = [(clip, h) for clip in range(2) for h in range(number)]
    begun = begin(*items[0])
    done = []
    for i, item in enumerate(items):
        now = begun
        if i + 1 < len(items):
            begun = begin(*items[i + 1])
        done.append(finish(*item, *now))
    ctx_own[...] = jnp.concatenate([c for c, _ in done[:number]], axis=0).T
    share[:TOK, :width] = jnp.concatenate([c for c, _ in done[number:]], axis=0).T
    share[TOK:, :width] = w[:, 3 * width :]
    grads = [
        jnp.concatenate([g for _, g in done[c * number : (c + 1) * number]], axis=0) for c in (0, 1)
    ]
    for out, (k, skip) in zip(sums, pieces):
        rows = pl.ds(places[k] + skip, out.shape[0])
        out[...] = dot(t0[rows, :], grads[0], ROWS) + dot(t1[rows, :], grads[1], ROWS)


def heads(chips, me, chains, steps, acts, pieces, piece_rows):
    depth = acts[6].shape[0]
    width = WIDE
    blocks = [b for chain in chains for b in chain]
    return pl.pallas_call(
        functools.partial(head_kernel, chips, steps, pieces),
        out_shape=(
            jax.ShapeDtypeStruct((TOK + depth, padded(width)), BF),
            jax.ShapeDtypeStruct((TOK, width), BF),
        )
        + (jax.ShapeDtypeStruct((piece_rows, width), F32),) * len(pieces),
        in_specs=[SM] + [VM] * (len(blocks) + 8),
        out_specs=(VM,) * (2 + len(pieces)),
        scratch_shapes=[pltpu.VMEM((depth, 4 * width), BF)],
        compiler_params=pltpu.CompilerParams(vmem_limit_bytes=16 * 2**20),
        cost_estimate=pl.CostEstimate(
            flops=9 * 10**9, bytes_accessed=15 * 10**6, transcendentals=2 * 10**6
        ),
    )(me, *blocks, *acts)


def out_kernel(ctx_own, share, got, out):
    out[...] = (
        dot(ctx_own[...], share[TOK:, :WIDE], ROWS) + dot(got[:TOK, :WIDE], got[TOK:, :WIDE], ROWS)
    ).astype(BF)


def total_kernel(me, *refs):
    *parts, keep, send = refs
    halves = [parts[i][...] + parts[i + 1][...] + parts[i + 2][...] for i in (0, 3)]
    for c in range(CORES):

        @pl.when(me[0] % CORES == c)
        def _():
            keep[...] = halves[c]
            send[...] = halves[1 - c]


def adam(q_master, q_moment, q_second, summed):
    q_gradient = summed * (1.0 / TOK)
    new_moment = 0.9 * q_moment + 0.1 * q_gradient
    new_second = 0.98 * q_second + 0.02 * q_gradient * q_gradient
    update = new_moment / first_fix / (jnp.sqrt(new_second / second_fix) + 1e-06)
    new_master = q_master - 0.001 * (update + 0.01 * q_master)
    return q_gradient, new_master, new_moment, new_second


def step_kernel(me, keep, keep_y, got, got_y, master, moment, second, *outs):
    core = me[0] % CORES
    mine = keep[...] + keep_y[...]
    other = got[...] + got_y[...]
    for c in range(CORES):

        @pl.when(core == c)
        def _():
            summed = jnp.concatenate([mine, other] if c == 0 else [other, mine], axis=1)
            for out, value in zip(outs, adam(master[...], moment[...], second[...], summed)):
                out[...] = value


def per_device(
    chips,
    reps,
    text_states,
    encoder_frames,
    out_cotangent,
    text_lengths,
    q_master,
    q_moment,
    q_second,
    key_weight,
    value_weight,
    out_weight,
):
    rows, width = q_master.shape
    depth = text_states.shape[1]
    chip_rows = CORES * rows
    index = lax.axis_index("dp")
    me = index.astype(jnp.int32).reshape(1)
    first = index % CORES == 0
    mates = [(i, i ^ 1) for i in range(CORES * chips)]
    swap = lambda a: lax.ppermute(a, "dp", mates)
    ring = 1 < chips <= RING_MOST and reps == 2
    right = lambda a: lax.ppermute(a, "dp", ring_pairs(chips, 1))
    left = lambda a: lax.ppermute(a, "dp", ring_pairs(chips, -1))
    same_core = [[CORES * i + c for i in range(chips)] for c in range(CORES)]

    in_use = jnp.arange(TOK, dtype=jnp.int32) < text_lengths[0]
    grad_out = jnp.where(in_use[:, None], out_cotangent, jnp.zeros_like(out_cotangent))
    x0, e0, g0 = text_states, encoder_frames, grad_out
    x1, e1, g1 = swap(x0), swap(e0), swap(g0)

    if ring:
        keep, send = pl.pallas_call(
            pack_kernel,
            out_shape=(jax.ShapeDtypeStruct((rows, 4 * WIDE), BF),) * 2,
            in_specs=[SM] + [HBM] * 4,
            out_specs=(VM, VM),
            scratch_shapes=[pltpu.VMEM((rows, width), F32)]
            + [pltpu.VMEM((rows, width), BF)] * 3
            + [pltpu.SemaphoreType.DMA((4,))],
            compiler_params=SMALL,
        )(me, q_master, key_weight, value_weight, out_weight.T)
        got, x1, e1, g1 = lax.optimization_barrier((swap(send), x1, e1, g1))
        own_blocks = pl.pallas_call(
            join_kernel,
            out_shape=(jax.ShapeDtypeStruct((chip_rows, 4 * WIDE // CHAINS), BF),) * CHAINS,
            in_specs=[SM] + [VM] * 2,
            out_specs=(VM,) * CHAINS,
            compiler_params=SMALL,
        )(me, keep, got)
    else:
        parts = (q_master.astype(BF), key_weight, value_weight, out_weight.T)
        packs = [pack(parts, c) for c in range(CORES)]
        keep = jnp.where(first, packs[0], packs[1])
        got = swap(jnp.where(first, packs[1], packs[0]))
        block = jnp.where(
            first, jnp.concatenate([keep, got], axis=0), jnp.concatenate([got, keep], axis=0)
        )
        own_blocks = [block]

    acts = (x0, x1, e0, e1, g0, g1, turn(x0), turn(x1))
    far = chips // 2
    if ring:
        steps, chains = [], []
        for i, own in enumerate(own_blocks):
            at, blocks = [0], [own]
            r = l = own
            for k in range(1, far):
                r, l = right(r), left(l)
                at += [chips - k, k]
                blocks += [r, l]
            at += [far]
            blocks += [right(r) if i % 2 == 0 else left(l)]
            steps.append(at)
            chains.append(blocks)
        pieces = [(k, h * rows) for k in range(far, 0, -1) for h in range(2)]
        pieces += [(chips - k, h * rows) for k in range(far - 1, 0, -1) for h in range(2)]
        pieces += [(0, h * rows) for h in range(2)]
        share, ctx_own, *sums = heads(chips, me, chains, steps, acts, pieces, rows)
        got_share = swap(share)
        totals = []
        for h in range(2):
            term = {k: s for (k, skip), s in zip(pieces, sums) if skip == h * rows}
            away, back, sign = (right, left, 1) if h == 0 else (left, right, -1)
            a, b = away(term[far]), back(term[-sign * (far - 1) % chips])
            for k in range(far - 1, 0, -1):
                a = away(a + term[sign * k % chips])
                if k > 1:
                    b = back(b + term[-sign * (k - 1) % chips])
            totals += [term[0], a, b]
        keep, send = pl.pallas_call(
            total_kernel,
            out_shape=(jax.ShapeDtypeStruct((rows, WIDE), F32),) * 2,
            in_specs=[SM] + [VM] * len(totals),
            out_specs=(VM, VM),
            compiler_params=SMALL,
        )(me, *totals)
        both = ("dp", "rep")
        across = [(i * reps + y, i * reps + (1 - y)) for i in range(CORES * chips) for y in range(reps)]
        cross = [(i * reps + y, (i ^ 1) * reps + (1 - y)) for i in range(CORES * chips) for y in range(reps)]
        got = swap(send)
        keep_y = lax.ppermute(keep, both, across)
        got_y = lax.ppermute(send, both, cross)
    else:
        block = lax.all_gather(own_blocks[0], "dp", axis=0, tiled=True, axis_index_groups=same_core)
        share, ctx_own, total = heads(chips, me, [[block]], [[0]], acts, [(0, 0)], depth)
        got_share = swap(share)
        total = lax.psum_scatter(
            total, "dp", scatter_dimension=0, tiled=True, axis_index_groups=same_core
        )
        keep = jnp.where(first, total[:rows], total[rows:])
        got = swap(jnp.where(first, total[rows:], total[:rows]))
        summed = jnp.where(
            first, jnp.concatenate([keep, got], axis=1), jnp.concatenate([got, keep], axis=1)
        )
        summed = lax.psum(summed, "rep")

    block_out = pl.pallas_call(
        out_kernel,
        out_shape=jax.ShapeDtypeStruct((TOK, depth), BF),
        in_specs=[VM] * 3,
        out_specs=VM,
        compiler_params=pltpu.CompilerParams(vmem_limit_bytes=8 * 2**20),
        cost_estimate=pl.CostEstimate(
            flops=2 * TOK * width * depth, bytes_accessed=4 * 10**6, transcendentals=0
        ),
    )(ctx_own, share, got_share)
    if ring:
        got, keep_y, got_y, block_out = lax.optimization_barrier((got, keep_y, got_y, block_out))
        results = pl.pallas_call(
            step_kernel,
            out_shape=(jax.ShapeDtypeStruct((rows, width), F32),) * 4,
            in_specs=[SM] + [VM] * 7,
            out_specs=(VM,) * 4,
            compiler_params=SMALL,
        )(me, keep, keep_y, got, got_y, q_master, q_moment, q_second)
    else:
        results = adam(q_master, q_moment, q_second, summed)
    return (block_out, *results)


def solution(mesh):
    in_specs = (
        P(("dp", "rep"), None),
        P(("dp", "rep"), None),
        P(("dp", "rep"), None),
        P(("dp", "rep")),
        P("dp", None),
        P("dp", None),
        P("dp", None),
        P("dp", None),
        P("dp", None),
        P(None, "dp"),
    )
    out_specs = (P(("dp", "rep"), None), P("dp", None), P("dp", None), P("dp", None), P("dp", None))
    return jax.shard_map(
        functools.partial(per_device, mesh.shape["dp"] // CORES, mesh.shape["rep"]),
        mesh=mesh,
        in_specs=in_specs,
        out_specs=out_specs,
        check_vma=False,
    )
```

time: 103 us -> 97.3 us (0.945)
  Pallas kernels: 28.4 us -> 22.4 us
    pallas_call x1, Pallas kernels: 23.1 us -> 17.1 us  [heads(): pl.pallas_call(functools.partial(head_kernel, chips, steps, pieces), out_...]
where the time goes in v3:
time: 97.3 us; the launch traced here: 97 us
  waiting for transfers between devices  35.2 us (36%)
  starting transfers between devices  33.5 us (34%)
  Pallas kernels  22.4 us (23%)
  local copies, waits for them, and re-layouts  2.75 us (3%)
  other arithmetic  1.67 us (2%)
  between operations  1.46 us (2%)
    ppermute x14, starting transfers between devices, per_device(): right = lambda a: lax.ppermute(a, 'dp', ring_pairs(chips, 1))  24.9 us
    ppermute x14, waiting for transfers between devices, per_device(): left = lambda a: lax.ppermute(a, 'dp', ring_pairs(chips, -1))  20.3 us
    pallas_call x1, Pallas kernels, heads(): pl.pallas_call(functools.partial(head_kernel, chips, steps, pieces), out_...  17.1 us
    ppermute x14, waiting for transfers between devices, per_device(): right = lambda a: lax.ppermute(a, 'dp', ring_pairs(chips, 1))  9.8 us
    ppermute x14, starting transfers between devices, per_device(): left = lambda a: lax.ppermute(a, 'dp', ring_pairs(chips, -1))  5.1 us
    ppermute x6, starting transfers between devices, per_device(): swap = lambda a: lax.ppermute(a, 'dp', mates)  2.93 us
    unnamed x18, local copies, waits for them, and re-layouts  2.75 us
    ppermute x1, waiting for transfers between devices, per_device(): keep_y = lax.ppermute(keep, both, across)  2.7 us
  transfers between devices with their start and end apart: 36, of which 18 were waited for; matrix products, arithmetic and copies ran while one was open for 2% of the time, Pallas kernels for 4%

profile of v3, /device:TPU:0, one launch (start us, length us, event | category | flops | bytes accessed | tf_op | source)
XLA Modules:
  0.0 97.0 jit_solution(16288201494915534187)
XLA Ops:
  1.8 1.5 %broadcast_select_fusion.refs_21_ = bf16[448,1280]{1,0:T(8,128)(2,1)S(1)} fusion(bf16[448,1280]{1,0:T(8,128)(2,1)} %param.12, pred[448]{0:T(512)(128)(4,1)S(1)} %iota_compare_fusion), kind=kLoop, calls=%fused_computation | loop fusion | flops 573440 | bytes 2294208 | tf_op jit(solution)/shard_map/jit(_where)/select_n | solution.py:270
  7.6 1.4 %collective-permute-done.got = bf16[80,1280]{1,0:T(8,128)(2,1)S(1)} collective-permute-done((bf16[80,1280]{1,0:T(8,128)(2,1)S(1)}, bf16[80,1280]{1,0:T(8,128)(2,1)S(1)}, u32[]{:S(2)}, u32[]{:S(2)}) %collective-permute-start) | collective-permute-done | bytes 204832 | tf_op jit(solution)/shard_map/ppermute | solution.py:263
  9.1 2.8 %collective-permute-start.4 = (bf16[160,640]{1,0:T(8,128)(2,1)S(1)}, bf16[160,640]{1,0:T(8,128)(2,1)S(1)}, u32[]{:S(2)}, u32[]{:S(2)}) collective-permute-start(bf16[160,640]{1,0:T(8,128)(2,1)S(1)} %get-tuple-element.44.refs_1_), channel_id=1, source_target_pairs={{0,8},{2,10},{8,16},{10,18},{16,24},{18,26},{24,28},{26,30},{28,20... | collective-permute-start | bytes 614408 | tf_op jit(solution)/shard_map/ppermute | solution.py:265
  11.9 1.9 %collective-permute-start.5 = (bf16[160,640]{1,0:T(8,128)(2,1)S(1)}, bf16[160,640]{1,0:T(8,128)(2,1)S(1)}, u32[]{:S(2)}, u32[]{:S(2)}) collective-permute-start(bf16[160,640]{1,0:T(8,128)(2,1)S(1)} %get-tuple-element.44.refs_1_), channel_id=1, source_target_pairs={{0,4},{2,6},{8,0},{10,2},{16,8},{18,10},{24,16},{26,18},{28,24},{3... | collective-permute-start | bytes 614408 | tf_op jit(solution)/shard_map/ppermute | solution.py:266
  13.9 3.8 %collective-permute-done.4.refs_2_ = bf16[160,640]{1,0:T(8,128)(2,1)S(1)} collective-permute-done((bf16[160,640]{1,0:T(8,128)(2,1)S(1)}, bf16[160,640]{1,0:T(8,128)(2,1)S(1)}, u32[]{:S(2)}, u32[]{:S(2)}) %collective-permute-start.4) | collective-permute-done | bytes 204832 | tf_op jit(solution)/shard_map/ppermute | solution.py:265
  17.7 2.1 %collective-permute-start.6 = (bf16[160,640]{1,0:T(8,128)(2,1)S(1)}, bf16[160,640]{1,0:T(8,128)(2,1)S(1)}, u32[]{:S(2)}, u32[]{:S(2)}) collective-permute-start(bf16[160,640]{1,0:T(8,128)(2,1)S(1)} %collective-permute-done.4.refs_2_), channel_id=1, source_target_pairs={{0,8},{2,10},{8,16},{10,18},{16,24},{18,26},{24,28},{26,30},{28,20... | collective-permute-start | bytes 614408 | tf_op jit(solution)/shard_map/ppermute | solution.py:265
  19.8 4.4 %collective-permute-done.5.refs_3_ = bf16[160,640]{1,0:T(8,128)(2,1)S(1)} collective-permute-done((bf16[160,640]{1,0:T(8,128)(2,1)S(1)}, bf16[160,640]{1,0:T(8,128)(2,1)S(1)}, u32[]{:S(2)}, u32[]{:S(2)}) %collective-permute-start.5) | collective-permute-done | bytes 204832 | tf_op jit(solution)/shard_map/ppermute | solution.py:266
  24.2 2.0 %collective-permute-start.13 = (bf16[160,640]{1,0:T(8,128)(2,1)S(1)}, bf16[160,640]{1,0:T(8,128)(2,1)S(1)}, u32[]{:S(2)}, u32[]{:S(2)}) collective-permute-start(bf16[160,640]{1,0:T(8,128)(2,1)S(1)} %collective-permute-done.11.refs_10_), channel_id=1, source_target_pairs={{0,8},{2,10},{8,16},{10,18},{16,24},{18,26},{24,28},{26,30},{28,20... | collective-permute-start | bytes 614408 | tf_op jit(solution)/shard_map/ppermute | solution.py:265
  26.5 2.1 %collective-permute-start.8 = (bf16[160,640]{1,0:T(8,128)(2,1)S(1)}, bf16[160,640]{1,0:T(8,128)(2,1)S(1)}, u32[]{:S(2)}, u32[]{:S(2)}) collective-permute-start(bf16[160,640]{1,0:T(8,128)(2,1)S(1)} %collective-permute-done.6.refs_4_), channel_id=1, source_target_pairs={{0,8},{2,10},{8,16},{10,18},{16,24},{18,26},{24,28},{26,30},{28,20... | collective-permute-start | bytes 614408 | tf_op jit(solution)/shard_map/ppermute | solution.py:265
  28.6 4.4 %collective-permute-done.7.refs_5_ = bf16[160,640]{1,0:T(8,128)(2,1)S(1)} collective-permute-done((bf16[160,640]{1,0:T(8,128)(2,1)S(1)}, bf16[160,640]{1,0:T(8,128)(2,1)S(1)}, u32[]{:S(2)}, u32[]{:S(2)}) %collective-permute-start.7) | collective-permute-done | bytes 204832 | tf_op jit(solution)/shard_map/ppermute | solution.py:266
  33.0 2.0 %collective-permute-start.15 = (bf16[160,640]{1,0:T(8,128)(2,1)S(1)}, bf16[160,640]{1,0:T(8,128)(2,1)S(1)}, u32[]{:S(2)}, u32[]{:S(2)}) collective-permute-start(bf16[160,640]{1,0:T(8,128)(2,1)S(1)} %collective-permute-done.13.refs_12_), channel_id=1, source_target_pairs={{0,8},{2,10},{8,16},{10,18},{16,24},{18,26},{24,28},{26,30},{28,20... | collective-permute-start | bytes 614408 | tf_op jit(solution)/shard_map/ppermute | solution.py:265
  35.5 2.2 %collective-permute-start.10 = (bf16[160,640]{1,0:T(8,128)(2,1)S(1)}, bf16[160,640]{1,0:T(8,128)(2,1)S(1)}, u32[]{:S(2)}, u32[]{:S(2)}) collective-permute-start(bf16[160,640]{1,0:T(8,128)(2,1)S(1)} %collective-permute-done.8.refs_6_), channel_id=1, source_target_pairs={{0,8},{2,10},{8,16},{10,18},{16,24},{18,26},{24,28},{26,30},{28,20... | collective-permute-start | bytes 614408 | tf_op jit(solution)/shard_map/ppermute | solution.py:265
  38.6 3.1 %collective-permute-done.9.refs_7_ = bf16[160,640]{1,0:T(8,128)(2,1)S(1)} collective-permute-done((bf16[160,640]{1,0:T(8,128)(2,1)S(1)}, bf16[160,640]{1,0:T(8,128)(2,1)S(1)}, u32[]{:S(2)}, u32[]{:S(2)}) %collective-permute-start.9) | collective-permute-done | bytes 204832 | tf_op jit(solution)/shard_map/ppermute | solution.py:266
  41.7 2.0 %collective-permute-done.10.refs_8_ = bf16[160,640]{1,0:T(8,128)(2,1)S(1)} collective-permute-done((bf16[160,640]{1,0:T(8,128)(2,1)S(1)}, bf16[160,640]{1,0:T(8,128)(2,1)S(1)}, u32[]{:S(2)}, u32[]{:S(2)}) %collective-permute-start.10) | collective-permute-done | bytes 204832 | tf_op jit(solution)/shard_map/ppermute | solution.py:265
  43.7 1.5 %collective-permute-done.17.refs_16_ = bf16[160,640]{1,0:T(8,128)(2,1)S(1)} collective-permute-done((bf16[160,640]{1,0:T(8,128)(2,1)S(1)}, bf16[160,640]{1,0:T(8,128)(2,1)S(1)}, u32[]{:S(2)}, u32[]{:S(2)}) %collective-permute-start.17) | collective-permute-done | bytes 204832 | tf_op jit(solution)/shard_map/ppermute | solution.py:266
  45.2 17.1 %shard_map.141 = (bf16[1728,384]{1,0:T(8,128)(2,1)S(1)}, bf16[448,320]{1,0:T(8,128)(2,1)S(1)}, f32[80,320]{1,0:T(8,128)S(1)}, f32[80,320]{1,0:T(8,128)S(1)}, f32...) custom-call(s32[1]{0:T(128)} %bitcast.me.refs_0_, ...), custom_call_target="tpu_custom_call" | custom-call | flops 8999999488 | bytes 15000000 | tf_op jit(solution)/shard_map/pallas_call | solution.py:186
  62.5 1.6 %collective-permute-start.18 = (f32[80,320]{1,0:T(8,128)S(1)}, f32[80,320]{1,0:T(8,128)S(1)}, u32[]{:S(2)}, u32[]{:S(2)}) collective-permute-start(f32[80,320]{1,0:T(8,128)S(1)} %get-tuple-element.50), channel_id=1, source_target_pairs={{0,8},{2,10},{8,16},{10,18},{16,24},{18,26},{24,28},{26,30},{28,20... | collective-permute-start | bytes 307208 | tf_op jit(solution)/shard_map/ppermute | solution.py:265
  64.8 1.7 %collective-permute-start.29 = (f32[80,320]{1,0:T(8,128)S(1)}, f32[80,320]{1,0:T(8,128)S(1)}, u32[]{:S(2)}, u32[]{:S(2)}) collective-permute-start(f32[80,320]{1,0:T(8,128)S(1)} %get-tuple-element.62), channel_id=1, source_target_pairs={{0,8},{2,10},{8,16},{10,18},{16,24},{18,26},{24,28},{26,30},{28,20... | collective-permute-start | bytes 307208 | tf_op jit(solution)/shard_map/ppermute | solution.py:265
  66.6 2.1 %collective-permute-done.18 = f32[80,320]{1,0:T(8,128)S(1)} collective-permute-done((f32[80,320]{1,0:T(8,128)S(1)}, f32[80,320]{1,0:T(8,128)S(1)}, u32[]{:S(2)}, u32[]{:S(2)}) %collective-permute-start.18) | collective-permute-done | bytes 102432 | tf_op jit(solution)/shard_map/ppermute | solution.py:265
  68.7 1.6 %collective-permute-start.19 = (f32[80,320]{1,0:T(8,128)S(1)}, f32[80,320]{1,0:T(8,128)S(1)}, u32[]{:S(2)}, u32[]{:S(2)}) collective-permute-start(f32[80,320]{1,0:T(8,128)S(1)} %add.30), channel_id=1, source_target_pairs={{0,8},{2,10},{8,16},{10,18},{16,24},{18,26},{24,28},{26,30},{28,20... | collective-permute-start | bytes 307208 | tf_op jit(solution)/shard_map/ppermute | solution.py:265
  70.8 1.5 %collective-permute-done.22 = f32[80,320]{1,0:T(8,128)S(1)} collective-permute-done((f32[80,320]{1,0:T(8,128)S(1)}, f32[80,320]{1,0:T(8,128)S(1)}, u32[]{:S(2)}, u32[]{:S(2)}) %collective-permute-start.22) | collective-permute-done | bytes 102432 | tf_op jit(solution)/shard_map/ppermute | solution.py:266
  72.8 1.6 %collective-permute-start.30 = (f32[80,320]{1,0:T(8,128)S(1)}, f32[80,320]{1,0:T(8,128)S(1)}, u32[]{:S(2)}, u32[]{:S(2)}) collective-permute-start(f32[80,320]{1,0:T(8,128)S(1)} %add.38), channel_id=1, source_target_pairs={{0,8},{2,10},{8,16},{10,18},{16,24},{18,26},{24,28},{26,30},{28,20... | collective-permute-start | bytes 307208 | tf_op jit(solution)/shard_map/ppermute | solution.py:265
  74.5 1.6 %collective-permute-start.20 = (f32[80,320]{1,0:T(8,128)S(1)}, f32[80,320]{1,0:T(8,128)S(1)}, u32[]{:S(2)}, u32[]{:S(2)}) collective-permute-start(f32[80,320]{1,0:T(8,128)S(1)} %add.31), channel_id=1, source_target_pairs={{0,8},{2,10},{8,16},{10,18},{16,24},{18,26},{24,28},{26,30},{28,20... | collective-permute-start | bytes 307208 | tf_op jit(solution)/shard_map/ppermute | solution.py:265
  76.9 1.7 %collective-permute-done.23 = f32[80,320]{1,0:T(8,128)S(1)} collective-permute-done((f32[80,320]{1,0:T(8,128)S(1)}, f32[80,320]{1,0:T(8,128)S(1)}, u32[]{:S(2)}, u32[]{:S(2)}) %collective-permute-start.23) | collective-permute-done | bytes 102432 | tf_op jit(solution)/shard_map/ppermute | solution.py:266
  79.1 1.6 %collective-permute-start.31 = (f32[80,320]{1,0:T(8,128)S(1)}, f32[80,320]{1,0:T(8,128)S(1)}, u32[]{:S(2)}, u32[]{:S(2)}) collective-permute-start(f32[80,320]{1,0:T(8,128)S(1)} %add.39), channel_id=1, source_target_pairs={{0,8},{2,10},{8,16},{10,18},{16,24},{18,26},{24,28},{26,30},{28,20... | collective-permute-start | bytes 307208 | tf_op jit(solution)/shard_map/ppermute | solution.py:265
  80.8 1.7 %collective-permute-start.21 = (f32[80,320]{1,0:T(8,128)S(1)}, f32[80,320]{1,0:T(8,128)S(1)}, u32[]{:S(2)}, u32[]{:S(2)}) collective-permute-start(f32[80,320]{1,0:T(8,128)S(1)} %add.32), channel_id=1, source_target_pairs={{0,8},{2,10},{8,16},{10,18},{16,24},{18,26},{24,28},{26,30},{28,20... | collective-permute-start | bytes 307208 | tf_op jit(solution)/shard_map/ppermute | solution.py:265
  82.9 1.6 %collective-permute-done.24.refs_2_ = f32[80,320]{1,0:T(8,128)S(1)} collective-permute-done((f32[80,320]{1,0:T(8,128)S(1)}, f32[80,320]{1,0:T(8,128)S(1)}, u32[]{:S(2)}, u32[]{:S(2)}) %collective-permute-start.24) | collective-permute-done | bytes 102432 | tf_op jit(solution)/shard_map/ppermute | solution.py:266
  85.7 1.7 %collective-permute-done.28.refs_4_ = f32[80,320]{1,0:T(8,128)S(1)} collective-permute-done((f32[80,320]{1,0:T(8,128)S(1)}, f32[80,320]{1,0:T(8,128)S(1)}, u32[]{:S(2)}, u32[]{:S(2)}) %collective-permute-start.28) | collective-permute-done | bytes 102432 | tf_op jit(solution)/shard_map/ppermute | solution.py:266
  87.6 1.6 %collective-permute-start.32 = (f32[80,320]{1,0:T(8,128)S(1)}, f32[80,320]{1,0:T(8,128)S(1)}, u32[]{:S(2)}, u32[]{:S(2)}) collective-permute-start(f32[80,320]{1,0:T(8,128)S(1)} %get-tuple-element.65), channel_id=1, source_target_pairs={{0,2},{2,0},{4,6},{6,4},{8,10},{10,8},{12,14},{14,12},{16,18},{18,... | collective-permute-start | bytes 307208 | tf_op jit(solution)/shard_map/ppermute | solution.py:263
  89.7 2.4 %shard_map.143 = bf16[448,1280]{1,0:T(8,128)(2,1)} custom-call(bf16[448,320]{1,0:T(8,128)(2,1)S(1)} %get-tuple-element.67.ctx_own, bf16[1728,384]{1,0:T(8,128)(2,1)S(1)} %get-tuple-element.68.share, bf16[1728,384]{1,0:T(8,128)(2,1)S(1)} %collective-permute-done.35.got), custom_call_target="tpu_custom_call" | custom-call | flops 734003200 | bytes 4000000 | tf_op jit(solution)/shard_map/pallas_call | solution.py:360
  93.1 2.7 %collective-permute-done.33.keep_y = f32[80,320]{1,0:T(8,128)S(1)} collective-permute-done((f32[80,320]{1,0:T(8,128)S(1)}, f32[80,320]{1,0:T(8,128)S(1)}, u32[]{:S(2)}, u32[]{:S(2)}) %collective-permute-start.33) | collective-permute-done | bytes 102432 | tf_op jit(solution)/shard_map/ppermute | solution.py:344
  95.8 1.2 %shard_map.144 = (f32[80,640]{1,0:T(8,128)}, f32[80,640]{1,0:T(8,128)}, f32[80,640]{1,0:T(8,128)}, f32[80,640]{1,0:T(8,128)}) custom-call(s32[1]{0:T(128)} %bitcast.me.refs_0_, f32[80,320]{1,0:T(8,128)S(1)} %get-tuple-element.66.keep, f32[80,320]{1,0:T(8,128)S(1)} %collective-permute-done.33.keep_y, f32[80,320]{1,0:T(8,128)S(1)} %collective-permute-done.32.got, ...), custom_call_target="tpu_custom_call" | custom-call | tf_op jit(solution)/shard_map/pallas_call | solution.py:372
  (78 shorter events, 13.2 us)
Async XLA Ops:
  0.6 8.4 %collective-permute-start.2 = (bf16[512,1280]{1,0:T(8,128)(2,1)}, bf16[512,1280]{1,0:T(8,128)(2,1)}, u32[]{:S(2)}, u32[]{:S(2)}) collective-permute-start(bf16[512,1280]{1,0:T(8,128)(2,1)} %refs_19_.1), channel_id=1, source_target_pairs={{0,2},{2,0},{4,6},{6,4},{8,10},{10,8},{12,14},{14,12},{16,18},{18,... | collective-permute-start | bytes 3932168 | tf_op jit(solution)/shard_map/ppermute | solution.py:263
  3.3 5.7 %collective-permute-start.3 = (bf16[448,1280]{1,0:T(8,128)(2,1)S(1)}, bf16[448,1280]{1,0:T(8,128)(2,1)}, u32[]{:S(2)}, u32[]{:S(2)}) collective-permute-start(bf16[448,1280]{1,0:T(8,128)(2,1)S(1)} %broadcast_select_fusion.refs_21_), channel_id=1, source_target_pairs={{0,2},{2,0},{4,6},{6,4},{8,10},{10,8},{12,14},{14,12},{16,18},{18,... | collective-permute-start | bytes 3440648 | tf_op jit(solution)/shard_map/ppermute | solution.py:263
  3.5 5.5 %collective-permute-start.1 = (bf16[448,1280]{1,0:T(8,128)(2,1)S(1)}, bf16[448,1280]{1,0:T(8,128)(2,1)S(1)}, u32[]{:S(2)}, u32[]{:S(2)}) collective-permute-start(bf16[448,1280]{1,0:T(8,128)(2,1)S(1)} %copy-done), channel_id=1, source_target_pairs={{0,2},{2,0},{4,6},{6,4},{8,10},{10,8},{12,14},{14,12},{16,18},{18,... | collective-permute-start | bytes 3440648 | tf_op jit(solution)/shard_map/ppermute | solution.py:263
  9.1 8.6 %collective-permute-start.4 = (bf16[160,640]{1,0:T(8,128)(2,1)S(1)}, bf16[160,640]{1,0:T(8,128)(2,1)S(1)}, u32[]{:S(2)}, u32[]{:S(2)}) collective-permute-start(bf16[160,640]{1,0:T(8,128)(2,1)S(1)} %get-tuple-element.44.refs_1_), channel_id=1, source_target_pairs={{0,8},{2,10},{8,16},{10,18},{16,24},{18,26},{24,28},{26,30},{28,20... | collective-permute-start | bytes 614408 | tf_op jit(solution)/shard_map/ppermute | solution.py:265
  11.8 7.9 %collective-permute-start.12 = (bf16[160,640]{1,0:T(8,128)(2,1)S(1)}, bf16[160,640]{1,0:T(8,128)(2,1)S(1)}, u32[]{:S(2)}, u32[]{:S(2)}) collective-permute-start(bf16[160,640]{1,0:T(8,128)(2,1)S(1)} %get-tuple-element.45.refs_9_), channel_id=1, source_target_pairs={{0,4},{2,6},{8,0},{10,2},{16,8},{18,10},{24,16},{26,18},{28,24},{3... | collective-permute-start | bytes 614408 | tf_op jit(solution)/shard_map/ppermute | solution.py:266
  11.9 12.3 %collective-permute-start.5 = (bf16[160,640]{1,0:T(8,128)(2,1)S(1)}, bf16[160,640]{1,0:T(8,128)(2,1)S(1)}, u32[]{:S(2)}, u32[]{:S(2)}) collective-permute-start(bf16[160,640]{1,0:T(8,128)(2,1)S(1)} %get-tuple-element.44.refs_1_), channel_id=1, source_target_pairs={{0,4},{2,6},{8,0},{10,2},{16,8},{18,10},{24,16},{26,18},{28,24},{3... | collective-permute-start | bytes 614408 | tf_op jit(solution)/shard_map/ppermute | solution.py:266
  13.8 10.4 %collective-permute-start.11 = (bf16[160,640]{1,0:T(8,128)(2,1)S(1)}, bf16[160,640]{1,0:T(8,128)(2,1)S(1)}, u32[]{:S(2)}, u32[]{:S(2)}) collective-permute-start(bf16[160,640]{1,0:T(8,128)(2,1)S(1)} %get-tuple-element.45.refs_9_), channel_id=1, source_target_pairs={{0,8},{2,10},{8,16},{10,18},{16,24},{18,26},{24,28},{26,30},{28,20... | collective-permute-start | bytes 614408 | tf_op jit(solution)/shard_map/ppermute | solution.py:265
  17.7 8.8 %collective-permute-start.6 = (bf16[160,640]{1,0:T(8,128)(2,1)S(1)}, bf16[160,640]{1,0:T(8,128)(2,1)S(1)}, u32[]{:S(2)}, u32[]{:S(2)}) collective-permute-start(bf16[160,640]{1,0:T(8,128)(2,1)S(1)} %collective-permute-done.4.refs_2_), channel_id=1, source_target_pairs={{0,8},{2,10},{8,16},{10,18},{16,24},{18,26},{24,28},{26,30},{28,20... | collective-permute-start | bytes 614408 | tf_op jit(solution)/shard_map/ppermute | solution.py:265
  19.8 8.8 %collective-permute-start.14 = (bf16[160,640]{1,0:T(8,128)(2,1)S(1)}, bf16[160,640]{1,0:T(8,128)(2,1)S(1)}, u32[]{:S(2)}, u32[]{:S(2)}) collective-permute-start(bf16[160,640]{1,0:T(8,128)(2,1)S(1)} %collective-permute-done.12.refs_11_), channel_id=1, source_target_pairs={{0,4},{2,6},{8,0},{10,2},{16,8},{18,10},{24,16},{26,18},{28,24},{3... | collective-permute-start | bytes 614408 | tf_op jit(solution)/shard_map/ppermute | solution.py:266
  24.2 8.8 %collective-permute-start.7 = (bf16[160,640]{1,0:T(8,128)(2,1)S(1)}, bf16[160,640]{1,0:T(8,128)(2,1)S(1)}, u32[]{:S(2)}, u32[]{:S(2)}) collective-permute-start(bf16[160,640]{1,0:T(8,128)(2,1)S(1)} %collective-permute-done.5.refs_3_), channel_id=1, source_target_pairs={{0,4},{2,6},{8,0},{10,2},{16,8},{18,10},{24,16},{26,18},{28,24},{3... | collective-permute-start | bytes 614408 | tf_op jit(solution)/shard_map/ppermute | solution.py:266
  24.2 8.8 %collective-permute-start.13 = (bf16[160,640]{1,0:T(8,128)(2,1)S(1)}, bf16[160,640]{1,0:T(8,128)(2,1)S(1)}, u32[]{:S(2)}, u32[]{:S(2)}) collective-permute-start(bf16[160,640]{1,0:T(8,128)(2,1)S(1)} %collective-permute-done.11.refs_10_), channel_id=1, source_target_pairs={{0,8},{2,10},{8,16},{10,18},{16,24},{18,26},{24,28},{26,30},{28,20... | collective-permute-start | bytes 614408 | tf_op jit(solution)/shard_map/ppermute | solution.py:265
  26.5 9.1 %collective-permute-start.8 = (bf16[160,640]{1,0:T(8,128)(2,1)S(1)}, bf16[160,640]{1,0:T(8,128)(2,1)S(1)}, u32[]{:S(2)}, u32[]{:S(2)}) collective-permute-start(bf16[160,640]{1,0:T(8,128)(2,1)S(1)} %collective-permute-done.6.refs_4_), channel_id=1, source_target_pairs={{0,8},{2,10},{8,16},{10,18},{16,24},{18,26},{24,28},{26,30},{28,20... | collective-permute-start | bytes 614408 | tf_op jit(solution)/shard_map/ppermute | solution.py:265
  28.6 9.2 %collective-permute-start.16 = (bf16[160,640]{1,0:T(8,128)(2,1)S(1)}, bf16[160,640]{1,0:T(8,128)(2,1)S(1)}, u32[]{:S(2)}, u32[]{:S(2)}) collective-permute-start(bf16[160,640]{1,0:T(8,128)(2,1)S(1)} %collective-permute-done.14.refs_13_), channel_id=1, source_target_pairs={{0,4},{2,6},{8,0},{10,2},{16,8},{18,10},{24,16},{26,18},{28,24},{3... | collective-permute-start | bytes 614408 | tf_op jit(solution)/shard_map/ppermute | solution.py:266
  32.9 8.8 %collective-permute-start.9 = (bf16[160,640]{1,0:T(8,128)(2,1)S(1)}, bf16[160,640]{1,0:T(8,128)(2,1)S(1)}, u32[]{:S(2)}, u32[]{:S(2)}) collective-permute-start(bf16[160,640]{1,0:T(8,128)(2,1)S(1)} %collective-permute-done.7.refs_5_), channel_id=1, source_target_pairs={{0,4},{2,6},{8,0},{10,2},{16,8},{18,10},{24,16},{26,18},{28,24},{3... | collective-permute-start | bytes 614408 | tf_op jit(solution)/shard_map/ppermute | solution.py:266
  33.0 8.8 %collective-permute-start.15 = (bf16[160,640]{1,0:T(8,128)(2,1)S(1)}, bf16[160,640]{1,0:T(8,128)(2,1)S(1)}, u32[]{:S(2)}, u32[]{:S(2)}) collective-permute-start(bf16[160,640]{1,0:T(8,128)(2,1)S(1)} %collective-permute-done.13.refs_12_), channel_id=1, source_target_pairs={{0,8},{2,10},{8,16},{10,18},{16,24},{18,26},{24,28},{26,30},{28,20... | collective-permute-start | bytes 614408 | tf_op jit(solution)/shard_map/ppermute | solution.py:265
  35.5 8.2 %collective-permute-start.10 = (bf16[160,640]{1,0:T(8,128)(2,1)S(1)}, bf16[160,640]{1,0:T(8,128)(2,1)S(1)}, u32[]{:S(2)}, u32[]{:S(2)}) collective-permute-start(bf16[160,640]{1,0:T(8,128)(2,1)S(1)} %collective-permute-done.8.refs_6_), channel_id=1, source_target_pairs={{0,8},{2,10},{8,16},{10,18},{16,24},{18,26},{24,28},{26,30},{28,20... | collective-permute-start | bytes 614408 | tf_op jit(solution)/shard_map/ppermute | solution.py:265
  37.8 7.5 %collective-permute-start.17 = (bf16[160,640]{1,0:T(8,128)(2,1)S(1)}, bf16[160,640]{1,0:T(8,128)(2,1)S(1)}, u32[]{:S(2)}, u32[]{:S(2)}) collective-permute-start(bf16[160,640]{1,0:T(8,128)(2,1)S(1)} %collective-permute-done.16.refs_15_), channel_id=1, source_target_pairs={{0,4},{2,6},{8,0},{10,2},{16,8},{18,10},{24,16},{26,18},{28,24},{3... | collective-permute-start | bytes 614408 | tf_op jit(solution)/shard_map/ppermute | solution.py:266
  62.4 27.3 %collective-permute-start.35 = (bf16[1728,384]{1,0:T(8,128)(2,1)S(1)}, bf16[1728,384]{1,0:T(8,128)(2,1)S(1)}, u32[]{:S(2)}, u32[]{:S(2)}) collective-permute-start(bf16[1728,384]{1,0:T(8,128)(2,1)S(1)} %get-tuple-element.68.share), channel_id=1, source_target_pairs={{0,2},{2,0},{4,6},{6,4},{8,10},{10,8},{12,14},{14,12},{16,18},{18,... | collective-permute-start | bytes 3981320 | tf_op jit(solution)/shard_map/ppermute | solution.py:263
  62.5 6.2 %collective-permute-start.18 = (f32[80,320]{1,0:T(8,128)S(1)}, f32[80,320]{1,0:T(8,128)S(1)}, u32[]{:S(2)}, u32[]{:S(2)}) collective-permute-start(f32[80,320]{1,0:T(8,128)S(1)} %get-tuple-element.50), channel_id=1, source_target_pairs={{0,8},{2,10},{8,16},{10,18},{16,24},{18,26},{24,28},{26,30},{28,20... | collective-permute-start | bytes 307208 | tf_op jit(solution)/shard_map/ppermute | solution.py:265
  64.1 6.2 %collective-permute-start.25 = (f32[80,320]{1,0:T(8,128)S(1)}, f32[80,320]{1,0:T(8,128)S(1)}, u32[]{:S(2)}, u32[]{:S(2)}) collective-permute-start(f32[80,320]{1,0:T(8,128)S(1)} %get-tuple-element.58), channel_id=1, source_target_pairs={{0,4},{2,6},{8,0},{10,2},{16,8},{18,10},{24,16},{26,18},{28,24},{3... | collective-permute-start | bytes 307208 | tf_op jit(solution)/shard_map/ppermute | solution.py:266
  64.5 7.7 %collective-permute-start.22 = (f32[80,320]{1,0:T(8,128)S(1)}, f32[80,320]{1,0:T(8,128)S(1)}, u32[]{:S(2)}, u32[]{:S(2)}) collective-permute-start(f32[80,320]{1,0:T(8,128)S(1)} %get-tuple-element.54), channel_id=1, source_target_pairs={{0,4},{2,6},{8,0},{10,2},{16,8},{18,10},{24,16},{26,18},{28,24},{3... | collective-permute-start | bytes 307208 | tf_op jit(solution)/shard_map/ppermute | solution.py:266
  64.8 8.0 %collective-permute-start.29 = (f32[80,320]{1,0:T(8,128)S(1)}, f32[80,320]{1,0:T(8,128)S(1)}, u32[]{:S(2)}, u32[]{:S(2)}) collective-permute-start(f32[80,320]{1,0:T(8,128)S(1)} %get-tuple-element.62), channel_id=1, source_target_pairs={{0,8},{2,10},{8,16},{10,18},{16,24},{18,26},{24,28},{26,30},{28,20... | collective-permute-start | bytes 307208 | tf_op jit(solution)/shard_map/ppermute | solution.py:265
  68.7 5.8 %collective-permute-start.19 = (f32[80,320]{1,0:T(8,128)S(1)}, f32[80,320]{1,0:T(8,128)S(1)}, u32[]{:S(2)}, u32[]{:S(2)}) collective-permute-start(f32[80,320]{1,0:T(8,128)S(1)} %add.30), channel_id=1, source_target_pairs={{0,8},{2,10},{8,16},{10,18},{16,24},{18,26},{24,28},{26,30},{28,20... | collective-permute-start | bytes 307208 | tf_op jit(solution)/shard_map/ppermute | solution.py:265
  70.3 6.1 %collective-permute-start.26 = (f32[80,320]{1,0:T(8,128)S(1)}, f32[80,320]{1,0:T(8,128)S(1)}, u32[]{:S(2)}, u32[]{:S(2)}) collective-permute-start(f32[80,320]{1,0:T(8,128)S(1)} %add.35), channel_id=1, source_target_pairs={{0,4},{2,6},{8,0},{10,2},{16,8},{18,10},{24,16},{26,18},{28,24},{3... | collective-permute-start | bytes 307208 | tf_op jit(solution)/shard_map/ppermute | solution.py:266
  72.3 6.3 %collective-permute-start.23 = (f32[80,320]{1,0:T(8,128)S(1)}, f32[80,320]{1,0:T(8,128)S(1)}, u32[]{:S(2)}, u32[]{:S(2)}) collective-permute-start(f32[80,320]{1,0:T(8,128)S(1)} %add.33), channel_id=1, source_target_pairs={{0,4},{2,6},{8,0},{10,2},{16,8},{18,10},{24,16},{26,18},{28,24},{3... | collective-permute-start | bytes 307208 | tf_op jit(solution)/shard_map/ppermute | solution.py:266
  72.8 6.3 %collective-permute-start.30 = (f32[80,320]{1,0:T(8,128)S(1)}, f32[80,320]{1,0:T(8,128)S(1)}, u32[]{:S(2)}, u32[]{:S(2)}) collective-permute-start(f32[80,320]{1,0:T(8,128)S(1)} %add.38), channel_id=1, source_target_pairs={{0,8},{2,10},{8,16},{10,18},{16,24},{18,26},{24,28},{26,30},{28,20... | collective-permute-start | bytes 307208 | tf_op jit(solution)/shard_map/ppermute | solution.py:265
  74.5 6.3 %collective-permute-start.20 = (f32[80,320]{1,0:T(8,128)S(1)}, f32[80,320]{1,0:T(8,128)S(1)}, u32[]{:S(2)}, u32[]{:S(2)}) collective-permute-start(f32[80,320]{1,0:T(8,128)S(1)} %add.31), channel_id=1, source_target_pairs={{0,8},{2,10},{8,16},{10,18},{16,24},{18,26},{24,28},{26,30},{28,20... | collective-permute-start | bytes 307208 | tf_op jit(solution)/shard_map/ppermute | solution.py:265
  76.4 6.1 %collective-permute-start.27 = (f32[80,320]{1,0:T(8,128)S(1)}, f32[80,320]{1,0:T(8,128)S(1)}, u32[]{:S(2)}, u32[]{:S(2)}) collective-permute-start(f32[80,320]{1,0:T(8,128)S(1)} %add.36), channel_id=1, source_target_pairs={{0,4},{2,6},{8,0},{10,2},{16,8},{18,10},{24,16},{26,18},{28,24},{3... | collective-permute-start | bytes 307208 | tf_op jit(solution)/shard_map/ppermute | solution.py:266
  78.6 5.9 %collective-permute-start.24 = (f32[80,320]{1,0:T(8,128)S(1)}, f32[80,320]{1,0:T(8,128)S(1)}, u32[]{:S(2)}, u32[]{:S(2)}) collective-permute-start(f32[80,320]{1,0:T(8,128)S(1)} %add.34), channel_id=1, source_target_pairs={{0,4},{2,6},{8,0},{10,2},{16,8},{18,10},{24,16},{26,18},{28,24},{3... | collective-permute-start | bytes 307208 | tf_op jit(solution)/shard_map/ppermute | solution.py:266
  87.5 5.6 %collective-permute-start.34 = (f32[80,320]{1,0:T(8,128)S(1)}, f32[80,320]{1,0:T(8,128)S(1)}, u32[]{:S(2)}, u32[]{:S(2)}) collective-permute-start(f32[80,320]{1,0:T(8,128)S(1)} %get-tuple-element.65), channel_id=1, source_target_pairs={{0,3},{1,2},{2,1},{3,0},{4,7},{5,6},{6,5},{7,4},{8,11},{9,10},{10,... | collective-permute-start | bytes 307208 | tf_op jit(solution)/shard_map/ppermute | solution.py:345
  87.6 5.5 %collective-permute-start.32 = (f32[80,320]{1,0:T(8,128)S(1)}, f32[80,320]{1,0:T(8,128)S(1)}, u32[]{:S(2)}, u32[]{:S(2)}) collective-permute-start(f32[80,320]{1,0:T(8,128)S(1)} %get-tuple-element.65), channel_id=1, source_target_pairs={{0,2},{2,0},{4,6},{6,4},{8,10},{10,8},{12,14},{14,12},{16,18},{18,... | collective-permute-start | bytes 307208 | tf_op jit(solution)/shard_map/ppermute | solution.py:263
  89.2 6.6 %collective-permute-start.33 = (f32[80,320]{1,0:T(8,128)S(1)}, f32[80,320]{1,0:T(8,128)S(1)}, u32[]{:S(2)}, u32[]{:S(2)}) collective-permute-start(f32[80,320]{1,0:T(8,128)S(1)} %get-tuple-element.66.keep), channel_id=1, source_target_pairs={{0,1},{1,0},{2,3},{3,2},{4,5},{5,4},{6,7},{7,6},{8,9},{9,8},{10,11... | collective-permute-start | bytes 307208 | tf_op jit(solution)/shard_map/ppermute | solution.py:344
  (13 other events, 48.7 us)

commit v4 on v3

--- a/solution.py
+++ b/solution.py
@@ -23,6 +23,7 @@
 VM = pl.BlockSpec(memory_space=pltpu.VMEM)
 SM = pl.BlockSpec(memory_space=pltpu.SMEM)
 ANY = pl.BlockSpec(memory_space=pl.ANY)
+LARGE = pltpu.CompilerParams(vmem_limit_bytes=56 * 2**20)
 HBM = pl.BlockSpec(memory_space=pltpu.HBM)
 SMALL = pltpu.CompilerParams(vmem_limit_bytes=4 * 2**20)
 
@@ -65,10 +66,8 @@
 
 
 def pack_kernel(me, q, k, v, o, keep, send, qv, kv, vv, ov, sem):
-    copies = [
-        pltpu.make_async_copy(src, dst, sem.at[i])
-        for i, (src, dst) in enumerate(((q, qv), (k, kv), (v, vv), (o, ov)))
-    ]
+    moves = ((q, qv), (k, kv), (v, vv), (o, ov))
+    copies = [pltpu.make_async_copy(src, dst, sem.at[i]) for i, (src, dst) in enumerate(moves)]
     for c in copies:
         c.start()
     for c in copies:
@@ -88,19 +87,41 @@
         send[...] = halves[0]
 
 
-def turn_kernel(x, t):
-    t[...] = x[...].T
-
-
-def turn(x):
+def stage_kernel(length, x, e, g, _, acts, xv, ev, gv, sem):
+    parts = list(zip((x, e, g), (xv, ev, gv), act_rows(e.shape[0])))
+    loads = [pltpu.make_async_copy(a, v, sem.at[i]) for i, (a, v, _) in enumerate(parts)]
+    stores = [pltpu.make_async_copy(v, acts.at[at], sem.at[3 + i]) for i, (_, v, at) in enumerate(parts)]
+    for c in loads[::-1]:
+        c.start()
+    loads[2].wait()
+    in_use = lax.broadcasted_iota(jnp.int32, gv.shape, 0) < length[0]
+    gv[...] = jnp.where(in_use, gv[...].astype(F32), 0.0).astype(BF)
+    stores[2].start()
+    for i in (1, 0):
+        loads[i].wait()
+        stores[i].start()
+    for c in stores:
+        c.wait()
+
+
+def act_rows(frames):
+    return pl.ds(0, TOK), pl.ds(TOK, frames), pl.ds(TOK + frames, TOK)
+
+
+def turn_kernel(mine, other, t0, t1):
+    t0[...] = mine[:TOK, :].T
+    t1[...] = other[:TOK, :].T
+
+
+def turn(mine, other):
     return pl.pallas_call(
         turn_kernel,
-        out_shape=jax.ShapeDtypeStruct(x.shape[::-1], BF),
-        in_specs=[VM],
-        out_specs=VM,
+        out_shape=(jax.ShapeDtypeStruct((mine.shape[1], TOK), BF),) * 2,
+        in_specs=[VM] * 2,
+        out_specs=(VM,) * 2,
         compiler_params=pltpu.CompilerParams(vmem_limit_bytes=8 * 2**20),
         cost_estimate=pl.CostEstimate(flops=0, bytes_accessed=5 * 10**6, transcendentals=0),
-    )(x)
+    )(mine, other)
 
 
 def join_kernel(me, keep, got, *blocks):
@@ -121,10 +142,12 @@
     take = lambda n: [refs.pop(0) for _ in range(n)]
     (me,) = take(1)
     chains = [take(len(s)) for s in steps]
-    x0, x1, e0, e1, g0, g1, t0, t1 = take(8)
+    mine, other, t0, t1 = take(4)
     share, ctx_own = take(2)
     sums = take(len(pieces))
-    (w,) = take(1)
+    w, loaded, whole, sem = take(4)
+    load = pltpu.make_async_copy(other, loaded, sem)
+    load.start()
     number, width = CORE_HEADS, WIDE
     chip_rows = w.shape[0] // chips
     if len(steps[0]) == 1:
@@ -136,12 +159,16 @@
         for k, block in zip(steps[i], blocks):
             w[pl.ds(places[k], block.shape[0]), i * cols : (i + 1) * cols] = block[...]
 
-    acts = ((x0, e0, g0), (x1, e1, g1))
+    x_at, e_at, g_at = act_rows(mine.shape[0] - 2 * TOK)
     rows_of = []
-    for xs, es, gs in acts:
-        q = (dot(xs[...], w[:, :width]) * 0.125).astype(BF)
-        kv = dot(es[...], w[:, width : 3 * width]).astype(BF)
-        g = dot(gs[...], w[:, 3 * width :]).astype(BF)
+
+    def project(clip):
+        acts = (mine, loaded)[clip]
+        if clip == 1:
+            load.wait()
+        q = (dot(acts[x_at, :], w[:, :width]) * 0.125).astype(BF)
+        kv = dot(acts[e_at, :], w[:, width : 3 * width]).astype(BF)
+        g = dot(acts[g_at, :], w[:, 3 * width :]).astype(BF)
         k, v = kv[:, :width], kv[:, width:]
         rows_of.append((q, k, v, g, k.T, v.T, g.T))
 
@@ -161,10 +188,13 @@
         return ctx.astype(BF), (dot(kt[cols], grad_scores) * 0.125).astype(BF)
 
     items = [(clip, h) for clip in range(2) for h in range(number)]
+    project(0)
     begun = begin(*items[0])
     done = []
     for i, item in enumerate(items):
         now = begun
+        if i == 1:
+            project(1)
         if i + 1 < len(items):
             begun = begin(*items[i + 1])
         done.append(finish(*item, *now))
@@ -174,13 +204,16 @@
     grads = [
         jnp.concatenate([g for _, g in done[c * number : (c + 1) * number]], axis=0) for c in (0, 1)
     ]
+    whole[...] = dot(t0[...], grads[0].T) + dot(t1[...], grads[1].T)
     for out, (k, skip) in zip(sums, pieces):
-        rows = pl.ds(places[k] + skip, out.shape[0])
-        out[...] = dot(t0[rows, :], grads[0], ROWS) + dot(t1[rows, :], grads[1], ROWS)
-
-
-def heads(chips, me, chains, steps, acts, pieces, piece_rows):
-    depth = acts[6].shape[0]
+        fold = out.shape[1] // width
+        for i in range(fold):
+            rows = pl.ds(places[k] + skip + i * out.shape[0], out.shape[0])
+            out[:, i * width : (i + 1) * width] = whole[rows, :]
+
+
+def heads(chips, me, chains, steps, acts, pieces, piece_shape):
+    depth = acts[0].shape[1]
     width = WIDE
     blocks = [b for chain in chains for b in chain]
     return pl.pallas_call(
@@ -189,11 +222,12 @@
             jax.ShapeDtypeStruct((TOK + depth, padded(width)), BF),
             jax.ShapeDtypeStruct((TOK, width), BF),
         )
-        + (jax.ShapeDtypeStruct((piece_rows, width), F32),) * len(pieces),
-        in_specs=[SM] + [VM] * (len(blocks) + 8),
+        + (jax.ShapeDtypeStruct(piece_shape, F32),) * len(pieces),
+        in_specs=[SM] + [VM] * len(blocks) + [VM, ANY, VM, VM],
         out_specs=(VM,) * (2 + len(pieces)),
-        scratch_shapes=[pltpu.VMEM((depth, 4 * width), BF)],
-        compiler_params=pltpu.CompilerParams(vmem_limit_bytes=16 * 2**20),
+        scratch_shapes=[pltpu.VMEM((depth, 4 * width), BF)]
+        + [pltpu.VMEM(acts[1].shape, BF), pltpu.VMEM((depth, width), F32), pltpu.SemaphoreType.DMA],
+        compiler_params=pltpu.CompilerParams(vmem_limit_bytes=22 * 2**20),
         cost_estimate=pl.CostEstimate(
             flops=9 * 10**9, bytes_accessed=15 * 10**6, transcendentals=2 * 10**6
         ),
@@ -234,9 +268,14 @@
 
         @pl.when(core == c)
         def _():
-            summed = jnp.concatenate([mine, other] if c == 0 else [other, mine], axis=1)
-            for out, value in zip(outs, adam(master[...], moment[...], second[...], summed)):
-                out[...] = value
+            for i in range(2):
+                rows = slice(i * mine.shape[0], (i + 1) * mine.shape[0])
+                cols = slice(i * WIDE, (i + 1) * WIDE)
+                halves = (mine[:, cols], other[:, cols])
+                summed = jnp.concatenate([halves[c], halves[1 - c]], axis=1)
+                values = adam(master[rows, :], moment[rows, :], second[rows, :], summed)
+                for out, value in zip(outs, values):
+                    out[rows, :] = value
 
 
 def per_device(
@@ -254,7 +293,7 @@
     out_weight,
 ):
     rows, width = q_master.shape
-    depth = text_states.shape[1]
+    frames, depth = encoder_frames.shape
     chip_rows = CORES * rows
     index = lax.axis_index("dp")
     me = index.astype(jnp.int32).reshape(1)
@@ -266,23 +305,27 @@
     left = lambda a: lax.ppermute(a, "dp", ring_pairs(chips, -1))
     same_core = [[CORES * i + c for i in range(chips)] for c in range(CORES)]
 
-    in_use = jnp.arange(TOK, dtype=jnp.int32) < text_lengths[0]
-    grad_out = jnp.where(in_use[:, None], out_cotangent, jnp.zeros_like(out_cotangent))
-    x0, e0, g0 = text_states, encoder_frames, grad_out
-    x1, e1, g1 = swap(x0), swap(e0), swap(g0)
-
     if ring:
         keep, send = pl.pallas_call(
             pack_kernel,
             out_shape=(jax.ShapeDtypeStruct((rows, 4 * WIDE), BF),) * 2,
             in_specs=[SM] + [HBM] * 4,
-            out_specs=(VM, VM),
+            out_specs=(VM,) * 2,
             scratch_shapes=[pltpu.VMEM((rows, width), F32)]
             + [pltpu.VMEM((rows, width), BF)] * 3
             + [pltpu.SemaphoreType.DMA((4,))],
-            compiler_params=SMALL,
+            compiler_params=LARGE,
         )(me, q_master, key_weight, value_weight, out_weight.T)
-        got, x1, e1, g1 = lax.optimization_barrier((swap(send), x1, e1, g1))
+        got = swap(send)
+        mine = pl.pallas_call(
+            stage_kernel,
+            out_shape=jax.ShapeDtypeStruct((2 * TOK + frames, depth), BF),
+            in_specs=[SM] + [HBM] * 3 + [ANY],
+            out_specs=HBM,
+            scratch_shapes=[pltpu.VMEM((n, depth), BF) for n in (TOK, frames, TOK)]
+            + [pltpu.SemaphoreType.DMA((6,))],
+            compiler_params=LARGE,
+        )(text_lengths, text_states, encoder_frames, out_cotangent, keep)
         own_blocks = pl.pallas_call(
             join_kernel,
             out_shape=(jax.ShapeDtypeStruct((chip_rows, 4 * WIDE // CHAINS), BF),) * CHAINS,
@@ -299,8 +342,13 @@
             first, jnp.concatenate([keep, got], axis=0), jnp.concatenate([got, keep], axis=0)
         )
         own_blocks = [block]
-
-    acts = (x0, x1, e0, e1, g0, g1, turn(x0), turn(x1))
+        in_use = jnp.arange(TOK, dtype=jnp.int32) < text_lengths[0]
+        grad_out = jnp.where(in_use[:, None], out_cotangent, jnp.zeros_like(out_cotangent))
+        mine = jnp.concatenate([text_states, encoder_frames, grad_out], axis=0)
+
+    mine, *own_blocks = lax.optimization_barrier((mine, *own_blocks))
+    other = swap(mine)
+    acts = (mine, other, *turn(mine, other))
     far = chips // 2
     if ring:
         steps, chains = [], []
@@ -318,7 +366,7 @@
         pieces = [(k, h * rows) for k in range(far, 0, -1) for h in range(2)]
         pieces += [(chips - k, h * rows) for k in range(far - 1, 0, -1) for h in range(2)]
         pieces += [(0, h * rows) for h in range(2)]
-        share, ctx_own, *sums = heads(chips, me, chains, steps, acts, pieces, rows)
+        share, ctx_own, *sums = heads(chips, me, chains, steps, acts, pieces, (rows // 2, 2 * WIDE))
         got_share = swap(share)
         totals = []
         for h in range(2):
@@ -332,7 +380,7 @@
             totals += [term[0], a, b]
         keep, send = pl.pallas_call(
             total_kernel,
-            out_shape=(jax.ShapeDtypeStruct((rows, WIDE), F32),) * 2,
+            out_shape=(jax.ShapeDtypeStruct((rows // 2, 2 * WIDE), F32),) * 2,
             in_specs=[SM] + [VM] * len(totals),
             out_specs=(VM, VM),
             compiler_params=SMALL,
@@ -345,7 +393,7 @@
         got_y = lax.ppermute(send, both, cross)
     else:
         block = lax.all_gather(own_blocks[0], "dp", axis=0, tiled=True, axis_index_groups=same_core)
-        share, ctx_own, total = heads(chips, me, [[block]], [[0]], acts, [(0, 0)], depth)
+        share, ctx_own, total = heads(chips, me, [[block]], [[0]], acts, [(0, 0)], (depth, WIDE))
         got_share = swap(share)
         total = lax.psum_scatter(
             total, "dp", scatter_dimension=0, tiled=True, axis_index_groups=same_core

time: 97.3 us -> 90.7 us (0.932)
  waiting for transfers between devices: 35.2 us -> 28.8 us
  Pallas kernels: 22.4 us -> 24.7 us
  other arithmetic: 1.67 us -> 0.15 us
    ppermute x14, waiting for transfers between devices: 20.3 us -> 16.7 us  [per_device(): left = lambda a: lax.ppermute(a, 'dp', ring_pairs(chips, -1))]
    pallas_call x3, Pallas kernels: 0.85 us -> 4.12 us  [the longest x1 3.33 us: per_device(): pl.pallas_call(stage_kernel, out_shape=jax.ShapeDtypeStruct((2 * TOK + fr...]
    pallas_call x1, Pallas kernels: 17.1 us -> 15 us  [heads(): pl.pallas_call(functools.partial(head_kernel, chips, steps, pieces), out_...]
    select_n x1 -> x0, other arithmetic: 1.5 us -> none  [per_device(): jnp.where(in_use[:, None], out_cotangent, jnp.zeros_like(out_cotangent))]
    ppermute x6 -> x4, waiting for transfers between devices: 1.38 us -> 0.01 us  [per_device(): swap = lambda a: lax.ppermute(a, 'dp', mates)]
    pallas_call x1, Pallas kernels: 0.83 us -> 2.04 us  [per_device(): pl.pallas_call(pack_kernel, out_shape=(jax.ShapeDtypeStruct((rows, 4 * WI...]
    unnamed x18 -> x12, local copies, waits for them, and re-layouts: 2.75 us -> 2.03 us
    ppermute x6 -> x4, starting transfers between devices: 2.93 us -> 2.33 us  [per_device(): swap = lambda a: lax.ppermute(a, 'dp', mates)]
  transfers between devices with their start and end apart: 36 -> 34, of which waited for: 18 -> 17; matrix products, arithmetic and copies ran while one was open for 2% -> 0% of each run, Pallas kernels for 4% -> 7%
where the time goes in v4:
time: 90.7 us; the launch traced here: 90.5 us
  starting transfers between devices  33.3 us (37%)
  waiting for transfers between devices  28.8 us (32%)
  Pallas kernels  24.7 us (27%)
  local copies, waits for them, and re-layouts  2.03 us (2%)
  between operations  1.45 us (2%)
    ppermute x14, starting transfers between devices, per_device(): right = lambda a: lax.ppermute(a, 'dp', ring_pairs(chips, 1))  25.6 us
    ppermute x14, waiting for transfers between devices, per_device(): left = lambda a: lax.ppermute(a, 'dp', ring_pairs(chips, -1))  16.7 us
    pallas_call x1, Pallas kernels, heads(): pl.pallas_call(functools.partial(head_kernel, chips, steps, pieces), out_...  15 us
    ppermute x14, waiting for transfers between devices, per_device(): right = lambda a: lax.ppermute(a, 'dp', ring_pairs(chips, 1))  9.3 us
    ppermute x14, starting transfers between devices, per_device(): left = lambda a: lax.ppermute(a, 'dp', ring_pairs(chips, -1))  4.8 us
    pallas_call x1, Pallas kernels, per_device(): pl.pallas_call(stage_kernel, out_shape=jax.ShapeDtypeStruct((2 * TOK + fr...  3.33 us
    pallas_call x1, Pallas kernels, per_device(): pl.pallas_call(out_kernel, out_shape=jax.ShapeDtypeStruct((TOK, depth), B...  2.37 us
    ppermute x4, starting transfers between devices, per_device(): swap = lambda a: lax.ppermute(a, 'dp', mates)  2.33 us
  transfers between devices with their start and end apart: 34, of which 17 were waited for; matrix products, arithmetic and copies ran while one was open for 0% of the time, Pallas kernels for 7%

profile of v4, /device:TPU:0, one launch (start us, length us, event | category | flops | bytes accessed | tf_op | source)
XLA Modules:
  0.0 90.5 jit_solution(5623216061550127242)
XLA Ops:
  0.6 2.0 %shard_map.137 = (bf16[80,1280]{1,0:T(8,128)(2,1)}, bf16[80,1280]{1,0:T(8,128)(2,1)}) custom-call(s32[1]{0:T(128)} %bitcast.me.refs_0_, f32[80,640]{1,0:T(8,128)} %master.1, bf16[80,640]{1,0:T(8,128)(2,1)} %k.1, bf16[80,640]{1,0:T(8,128)(2,1)} %v.1, bf16[80,640]{1,0:T(8,128)(2,1)} %bitcast.2), custom_call_target="tpu_custom_call" | custom-call | tf_op jit(solution)/shard_map/pallas_call | solution.py:309
  3.9 3.3 %shard_map.138.mine.refs_17_ = bf16[1408,1280]{1,0:T(8,128)(2,1)} custom-call(s32[1]{0:T(128)S(6)} %copy.15.length, bf16[448,1280]{1,0:T(8,128)(2,1)} %x.1, bf16[512,1280]{1,0:T(8,128)(2,1)} %e.1, bf16[448,1280]{1,0:T(8,128)(2,1)} %g.1, bf16[80,1280]{1,0:T(8,128)(2,1)} %get-tuple-element.42._.keep), custom_call_target="tpu_custom_call" | custom-call | tf_op jit(solution)/shard_map/pallas_call | solution.py:320
  7.4 3.0 %collective-permute-start.1 = (bf16[160,640]{1,0:T(8,128)(2,1)S(1)}, bf16[160,640]{1,0:T(8,128)(2,1)S(1)}, u32[]{:S(2)}, u32[]{:S(2)}) collective-permute-start(bf16[160,640]{1,0:T(8,128)(2,1)S(1)} %get-tuple-element.46.refs_1_), channel_id=1, source_target_pairs={{0,8},{2,10},{8,16},{10,18},{16,24},{18,26},{24,28},{26,30},{28,20... | collective-permute-start | bytes 614408 | tf_op jit(solution)/shard_map/ppermute | solution.py:304
  10.4 1.9 %collective-permute-start.2 = (bf16[160,640]{1,0:T(8,128)(2,1)S(1)}, bf16[160,640]{1,0:T(8,128)(2,1)S(1)}, u32[]{:S(2)}, u32[]{:S(2)}) collective-permute-start(bf16[160,640]{1,0:T(8,128)(2,1)S(1)} %get-tuple-element.46.refs_1_), channel_id=1, source_target_pairs={{0,4},{2,6},{8,0},{10,2},{16,8},{18,10},{24,16},{26,18},{28,24},{3... | collective-permute-start | bytes 614408 | tf_op jit(solution)/shard_map/ppermute | solution.py:305
  12.5 3.7 %collective-permute-done.1.refs_2_ = bf16[160,640]{1,0:T(8,128)(2,1)S(1)} collective-permute-done((bf16[160,640]{1,0:T(8,128)(2,1)S(1)}, bf16[160,640]{1,0:T(8,128)(2,1)S(1)}, u32[]{:S(2)}, u32[]{:S(2)}) %collective-permute-start.1) | collective-permute-done | bytes 204832 | tf_op jit(solution)/shard_map/ppermute | solution.py:304
  16.2 2.1 %collective-permute-start.3 = (bf16[160,640]{1,0:T(8,128)(2,1)S(1)}, bf16[160,640]{1,0:T(8,128)(2,1)S(1)}, u32[]{:S(2)}, u32[]{:S(2)}) collective-permute-start(bf16[160,640]{1,0:T(8,128)(2,1)S(1)} %collective-permute-done.1.refs_2_), channel_id=1, source_target_pairs={{0,8},{2,10},{8,16},{10,18},{16,24},{18,26},{24,28},{26,30},{28,20... | collective-permute-start | bytes 614408 | tf_op jit(solution)/shard_map/ppermute | solution.py:304
  18.4 4.4 %collective-permute-done.2.refs_3_ = bf16[160,640]{1,0:T(8,128)(2,1)S(1)} collective-permute-done((bf16[160,640]{1,0:T(8,128)(2,1)S(1)}, bf16[160,640]{1,0:T(8,128)(2,1)S(1)}, u32[]{:S(2)}, u32[]{:S(2)}) %collective-permute-start.2) | collective-permute-done | bytes 204832 | tf_op jit(solution)/shard_map/ppermute | solution.py:305
  22.8 2.0 %collective-permute-start.10 = (bf16[160,640]{1,0:T(8,128)(2,1)S(1)}, bf16[160,640]{1,0:T(8,128)(2,1)S(1)}, u32[]{:S(2)}, u32[]{:S(2)}) collective-permute-start(bf16[160,640]{1,0:T(8,128)(2,1)S(1)} %collective-permute-done.8.refs_10_), channel_id=1, source_target_pairs={{0,8},{2,10},{8,16},{10,18},{16,24},{18,26},{24,28},{26,30},{28,20... | collective-permute-start | bytes 614408 | tf_op jit(solution)/shard_map/ppermute | solution.py:304
  25.0 2.1 %collective-permute-start.5 = (bf16[160,640]{1,0:T(8,128)(2,1)S(1)}, bf16[160,640]{1,0:T(8,128)(2,1)S(1)}, u32[]{:S(2)}, u32[]{:S(2)}) collective-permute-start(bf16[160,640]{1,0:T(8,128)(2,1)S(1)} %collective-permute-done.3.refs_4_), channel_id=1, source_target_pairs={{0,8},{2,10},{8,16},{10,18},{16,24},{18,26},{24,28},{26,30},{28,20... | collective-permute-start | bytes 614408 | tf_op jit(solution)/shard_map/ppermute | solution.py:304
  27.2 4.4 %collective-permute-done.4.refs_5_ = bf16[160,640]{1,0:T(8,128)(2,1)S(1)} collective-permute-done((bf16[160,640]{1,0:T(8,128)(2,1)S(1)}, bf16[160,640]{1,0:T(8,128)(2,1)S(1)}, u32[]{:S(2)}, u32[]{:S(2)}) %collective-permute-start.4) | collective-permute-done | bytes 204832 | tf_op jit(solution)/shard_map/ppermute | solution.py:305
  31.6 2.0 %collective-permute-start.12 = (bf16[160,640]{1,0:T(8,128)(2,1)S(1)}, bf16[160,640]{1,0:T(8,128)(2,1)S(1)}, u32[]{:S(2)}, u32[]{:S(2)}) collective-permute-start(bf16[160,640]{1,0:T(8,128)(2,1)S(1)} %collective-permute-done.10.refs_12_), channel_id=1, source_target_pairs={{0,8},{2,10},{8,16},{10,18},{16,24},{18,26},{24,28},{26,30},{28,20... | collective-permute-start | bytes 614408 | tf_op jit(solution)/shard_map/ppermute | solution.py:304
  34.2 2.2 %collective-permute-start.7 = (bf16[160,640]{1,0:T(8,128)(2,1)S(1)}, bf16[160,640]{1,0:T(8,128)(2,1)S(1)}, u32[]{:S(2)}, u32[]{:S(2)}) collective-permute-start(bf16[160,640]{1,0:T(8,128)(2,1)S(1)} %collective-permute-done.5.refs_6_), channel_id=1, source_target_pairs={{0,8},{2,10},{8,16},{10,18},{16,24},{18,26},{24,28},{26,30},{28,20... | collective-permute-start | bytes 614408 | tf_op jit(solution)/shard_map/ppermute | solution.py:304
  36.4 2.0 %copy-done = bf16[1408,1280]{1,0:T(8,128)(2,1)S(1)} copy-done((bf16[1408,1280]{1,0:T(8,128)(2,1)S(1)}, bf16[1408,1280]{1,0:T(8,128)(2,1)}, u32[]{:S(2)}) %copy-start) | copy-done | bytes 3604504
  39.2 1.2 %collective-permute-done.6.refs_7_ = bf16[160,640]{1,0:T(8,128)(2,1)S(1)} collective-permute-done((bf16[160,640]{1,0:T(8,128)(2,1)S(1)}, bf16[160,640]{1,0:T(8,128)(2,1)S(1)}, u32[]{:S(2)}, u32[]{:S(2)}) %collective-permute-start.6) | collective-permute-done | bytes 204832 | tf_op jit(solution)/shard_map/ppermute | solution.py:305
  40.3 1.6 %collective-permute-done.7.refs_8_ = bf16[160,640]{1,0:T(8,128)(2,1)S(1)} collective-permute-done((bf16[160,640]{1,0:T(8,128)(2,1)S(1)}, bf16[160,640]{1,0:T(8,128)(2,1)S(1)}, u32[]{:S(2)}, u32[]{:S(2)}) %collective-permute-start.7) | collective-permute-done | bytes 204832 | tf_op jit(solution)/shard_map/ppermute | solution.py:304
  42.0 1.5 %collective-permute-done.14.refs_16_ = bf16[160,640]{1,0:T(8,128)(2,1)S(1)} collective-permute-done((bf16[160,640]{1,0:T(8,128)(2,1)S(1)}, bf16[160,640]{1,0:T(8,128)(2,1)S(1)}, u32[]{:S(2)}, u32[]{:S(2)}) %collective-permute-start.14) | collective-permute-done | bytes 204832 | tf_op jit(solution)/shard_map/ppermute | solution.py:305
  43.5 15.0 %shard_map.141 = (bf16[1728,384]{1,0:T(8,128)(2,1)S(1)}, bf16[448,320]{1,0:T(8,128)(2,1)S(1)}, f32[40,640]{1,0:T(8,128)S(1)}, f32[40,640]{1,0:T(8,128)S(1)}, f32...) custom-call(s32[1]{0:T(128)} %bitcast.me.refs_0_, ...), custom_call_target="tpu_custom_call" | custom-call | flops 8999999488 | bytes 15000000 | tf_op jit(solution)/shard_map/pallas_call | solution.py:219
  58.6 1.6 %collective-permute-start.16 = (f32[40,640]{1,0:T(8,128)S(1)}, f32[40,640]{1,0:T(8,128)S(1)}, u32[]{:S(2)}, u32[]{:S(2)}) collective-permute-start(f32[40,640]{1,0:T(8,128)S(1)} %get-tuple-element.52), channel_id=1, source_target_pairs={{0,8},{2,10},{8,16},{10,18},{16,24},{18,26},{24,28},{26,30},{28,20... | collective-permute-start | bytes 307208 | tf_op jit(solution)/shard_map/ppermute | solution.py:304
  61.0 1.7 %collective-permute-start.27 = (f32[40,640]{1,0:T(8,128)S(1)}, f32[40,640]{1,0:T(8,128)S(1)}, u32[]{:S(2)}, u32[]{:S(2)}) collective-permute-start(f32[40,640]{1,0:T(8,128)S(1)} %get-tuple-element.64), channel_id=1, source_target_pairs={{0,8},{2,10},{8,16},{10,18},{16,24},{18,26},{24,28},{26,30},{28,20... | collective-permute-start | bytes 307208 | tf_op jit(solution)/shard_map/ppermute | solution.py:304
  62.7 1.6 %collective-permute-done.16 = f32[40,640]{1,0:T(8,128)S(1)} collective-permute-done((f32[40,640]{1,0:T(8,128)S(1)}, f32[40,640]{1,0:T(8,128)S(1)}, u32[]{:S(2)}, u32[]{:S(2)}) %collective-permute-start.16) | collective-permute-done | bytes 102432 | tf_op jit(solution)/shard_map/ppermute | solution.py:304
  64.3 1.6 %collective-permute-start.17 = (f32[40,640]{1,0:T(8,128)S(1)}, f32[40,640]{1,0:T(8,128)S(1)}, u32[]{:S(2)}, u32[]{:S(2)}) collective-permute-start(f32[40,640]{1,0:T(8,128)S(1)} %add.30), channel_id=1, source_target_pairs={{0,8},{2,10},{8,16},{10,18},{16,24},{18,26},{24,28},{26,30},{28,20... | collective-permute-start | bytes 307208 | tf_op jit(solution)/shard_map/ppermute | solution.py:304
  67.9 1.6 %collective-permute-start.28 = (f32[40,640]{1,0:T(8,128)S(1)}, f32[40,640]{1,0:T(8,128)S(1)}, u32[]{:S(2)}, u32[]{:S(2)}) collective-permute-start(f32[40,640]{1,0:T(8,128)S(1)} %add.38), channel_id=1, source_target_pairs={{0,8},{2,10},{8,16},{10,18},{16,24},{18,26},{24,28},{26,30},{28,20... | collective-permute-start | bytes 307208 | tf_op jit(solution)/shard_map/ppermute | solution.py:304
  69.6 1.6 %collective-permute-start.18 = (f32[40,640]{1,0:T(8,128)S(1)}, f32[40,640]{1,0:T(8,128)S(1)}, u32[]{:S(2)}, u32[]{:S(2)}) collective-permute-start(f32[40,640]{1,0:T(8,128)S(1)} %add.31), channel_id=1, source_target_pairs={{0,8},{2,10},{8,16},{10,18},{16,24},{18,26},{24,28},{26,30},{28,20... | collective-permute-start | bytes 307208 | tf_op jit(solution)/shard_map/ppermute | solution.py:304
  73.4 1.6 %collective-permute-start.29 = (f32[40,640]{1,0:T(8,128)S(1)}, f32[40,640]{1,0:T(8,128)S(1)}, u32[]{:S(2)}, u32[]{:S(2)}) collective-permute-start(f32[40,640]{1,0:T(8,128)S(1)} %add.39), channel_id=1, source_target_pairs={{0,8},{2,10},{8,16},{10,18},{16,24},{18,26},{24,28},{26,30},{28,20... | collective-permute-start | bytes 307208 | tf_op jit(solution)/shard_map/ppermute | solution.py:304
  75.1 2.0 %collective-permute-start.19 = (f32[40,640]{1,0:T(8,128)S(1)}, f32[40,640]{1,0:T(8,128)S(1)}, u32[]{:S(2)}, u32[]{:S(2)}) collective-permute-start(f32[40,640]{1,0:T(8,128)S(1)} %add.32), channel_id=1, source_target_pairs={{0,8},{2,10},{8,16},{10,18},{16,24},{18,26},{24,28},{26,30},{28,20... | collective-permute-start | bytes 307208 | tf_op jit(solution)/shard_map/ppermute | solution.py:304
  77.2 1.0 %collective-permute-done.22.refs_2_ = f32[40,640]{1,0:T(8,128)S(1)} collective-permute-done((f32[40,640]{1,0:T(8,128)S(1)}, f32[40,640]{1,0:T(8,128)S(1)}, u32[]{:S(2)}, u32[]{:S(2)}) %collective-permute-start.22) | collective-permute-done | bytes 102432 | tf_op jit(solution)/shard_map/ppermute | solution.py:305
  78.2 1.6 %collective-permute-done.19.refs_1_ = f32[40,640]{1,0:T(8,128)S(1)} collective-permute-done((f32[40,640]{1,0:T(8,128)S(1)}, f32[40,640]{1,0:T(8,128)S(1)}, u32[]{:S(2)}, u32[]{:S(2)}) %collective-permute-start.19) | collective-permute-done | bytes 102432 | tf_op jit(solution)/shard_map/ppermute | solution.py:304
  79.8 2.0 %collective-permute-done.26.refs_4_ = f32[40,640]{1,0:T(8,128)S(1)} collective-permute-done((f32[40,640]{1,0:T(8,128)S(1)}, f32[40,640]{1,0:T(8,128)S(1)}, u32[]{:S(2)}, u32[]{:S(2)}) %collective-permute-start.26) | collective-permute-done | bytes 102432 | tf_op jit(solution)/shard_map/ppermute | solution.py:305
  81.9 1.6 %collective-permute-start.30 = (f32[40,640]{1,0:T(8,128)S(1)}, f32[40,640]{1,0:T(8,128)S(1)}, u32[]{:S(2)}, u32[]{:S(2)}) collective-permute-start(f32[40,640]{1,0:T(8,128)S(1)} %get-tuple-element.67), channel_id=1, source_target_pairs={{0,2},{2,0},{4,6},{6,4},{8,10},{10,8},{12,14},{14,12},{16,18},{18,... | collective-permute-start | bytes 307208 | tf_op jit(solution)/shard_map/ppermute | solution.py:302
  84.1 2.4 %shard_map.143 = bf16[448,1280]{1,0:T(8,128)(2,1)} custom-call(bf16[448,320]{1,0:T(8,128)(2,1)S(1)} %get-tuple-element.69.ctx_own, bf16[1728,384]{1,0:T(8,128)(2,1)S(1)} %get-tuple-element.70.share, bf16[1728,384]{1,0:T(8,128)(2,1)S(1)} %collective-permute-done.33.got), custom_call_target="tpu_custom_call" | custom-call | flops 734003200 | bytes 4000000 | tf_op jit(solution)/shard_map/pallas_call | solution.py:408
  87.0 2.3 %collective-permute-done.31.keep_y = f32[40,640]{1,0:T(8,128)S(1)} collective-permute-done((f32[40,640]{1,0:T(8,128)S(1)}, f32[40,640]{1,0:T(8,128)S(1)}, u32[]{:S(2)}, u32[]{:S(2)}) %collective-permute-start.31) | collective-permute-done | bytes 102432 | tf_op jit(solution)/shard_map/ppermute | solution.py:392
  89.3 1.2 %shard_map.144 = (f32[80,640]{1,0:T(8,128)}, f32[80,640]{1,0:T(8,128)}, f32[80,640]{1,0:T(8,128)}, f32[80,640]{1,0:T(8,128)}) custom-call(s32[1]{0:T(128)} %bitcast.me.refs_0_, f32[40,640]{1,0:T(8,128)S(1)} %get-tuple-element.68.keep, f32[40,640]{1,0:T(8,128)S(1)} %collective-permute-done.31.keep_y, f32[40,640]{1,0:T(8,128)S(1)} %collective-permute-done.30.got, ...), custom_call_target="tpu_custom_call" | custom-call | tf_op jit(solution)/shard_map/pallas_call | solution.py:420
  (66 shorter events, 8.8 us)
Async XLA Ops:
  7.3 29.1 %collective-permute-start.15 = (bf16[1408,1280]{1,0:T(8,128)(2,1)}, bf16[1408,1280]{1,0:T(8,128)(2,1)S(1)}, u32[]{:S(2)}, u32[]{:S(2)}) collective-permute-start(bf16[1408,1280]{1,0:T(8,128)(2,1)} %shard_map.138.mine.refs_17_), channel_id=1, source_target_pairs={{0,2},{2,0},{4,6},{6,4},{8,10},{10,8},{12,14},{14,12},{16,18},{18,... | collective-permute-start | bytes 10813448 | tf_op jit(solution)/shard_map/ppermute | solution.py:302
  7.4 8.8 %collective-permute-start.1 = (bf16[160,640]{1,0:T(8,128)(2,1)S(1)}, bf16[160,640]{1,0:T(8,128)(2,1)S(1)}, u32[]{:S(2)}, u32[]{:S(2)}) collective-permute-start(bf16[160,640]{1,0:T(8,128)(2,1)S(1)} %get-tuple-element.46.refs_1_), channel_id=1, source_target_pairs={{0,8},{2,10},{8,16},{10,18},{16,24},{18,26},{24,28},{26,30},{28,20... | collective-permute-start | bytes 614408 | tf_op jit(solution)/shard_map/ppermute | solution.py:304
  10.4 8.0 %collective-permute-start.9 = (bf16[160,640]{1,0:T(8,128)(2,1)S(1)}, bf16[160,640]{1,0:T(8,128)(2,1)S(1)}, u32[]{:S(2)}, u32[]{:S(2)}) collective-permute-start(bf16[160,640]{1,0:T(8,128)(2,1)S(1)} %get-tuple-element.47.refs_9_), channel_id=1, source_target_pairs={{0,4},{2,6},{8,0},{10,2},{16,8},{18,10},{24,16},{26,18},{28,24},{3... | collective-permute-start | bytes 614408 | tf_op jit(solution)/shard_map/ppermute | solution.py:305
  10.4 12.4 %collective-permute-start.2 = (bf16[160,640]{1,0:T(8,128)(2,1)S(1)}, bf16[160,640]{1,0:T(8,128)(2,1)S(1)}, u32[]{:S(2)}, u32[]{:S(2)}) collective-permute-start(bf16[160,640]{1,0:T(8,128)(2,1)S(1)} %get-tuple-element.46.refs_1_), channel_id=1, source_target_pairs={{0,4},{2,6},{8,0},{10,2},{16,8},{18,10},{24,16},{26,18},{28,24},{3... | collective-permute-start | bytes 614408 | tf_op jit(solution)/shard_map/ppermute | solution.py:305
  12.4 10.4 %collective-permute-start.8 = (bf16[160,640]{1,0:T(8,128)(2,1)S(1)}, bf16[160,640]{1,0:T(8,128)(2,1)S(1)}, u32[]{:S(2)}, u32[]{:S(2)}) collective-permute-start(bf16[160,640]{1,0:T(8,128)(2,1)S(1)} %get-tuple-element.47.refs_9_), channel_id=1, source_target_pairs={{0,8},{2,10},{8,16},{10,18},{16,24},{18,26},{24,28},{26,30},{28,20... | collective-permute-start | bytes 614408 | tf_op jit(solution)/shard_map/ppermute | solution.py:304
  16.2 8.8 %collective-permute-start.3 = (bf16[160,640]{1,0:T(8,128)(2,1)S(1)}, bf16[160,640]{1,0:T(8,128)(2,1)S(1)}, u32[]{:S(2)}, u32[]{:S(2)}) collective-permute-start(bf16[160,640]{1,0:T(8,128)(2,1)S(1)} %collective-permute-done.1.refs_2_), channel_id=1, source_target_pairs={{0,8},{2,10},{8,16},{10,18},{16,24},{18,26},{24,28},{26,30},{28,20... | collective-permute-start | bytes 614408 | tf_op jit(solution)/shard_map/ppermute | solution.py:304
  18.4 8.8 %collective-permute-start.11 = (bf16[160,640]{1,0:T(8,128)(2,1)S(1)}, bf16[160,640]{1,0:T(8,128)(2,1)S(1)}, u32[]{:S(2)}, u32[]{:S(2)}) collective-permute-start(bf16[160,640]{1,0:T(8,128)(2,1)S(1)} %collective-permute-done.9.refs_11_), channel_id=1, source_target_pairs={{0,4},{2,6},{8,0},{10,2},{16,8},{18,10},{24,16},{26,18},{28,24},{3... | collective-permute-start | bytes 614408 | tf_op jit(solution)/shard_map/ppermute | solution.py:305
  22.8 8.8 %collective-permute-start.4 = (bf16[160,640]{1,0:T(8,128)(2,1)S(1)}, bf16[160,640]{1,0:T(8,128)(2,1)S(1)}, u32[]{:S(2)}, u32[]{:S(2)}) collective-permute-start(bf16[160,640]{1,0:T(8,128)(2,1)S(1)} %collective-permute-done.2.refs_3_), channel_id=1, source_target_pairs={{0,4},{2,6},{8,0},{10,2},{16,8},{18,10},{24,16},{26,18},{28,24},{3... | collective-permute-start | bytes 614408 | tf_op jit(solution)/shard_map/ppermute | solution.py:305
  22.8 8.8 %collective-permute-start.10 = (bf16[160,640]{1,0:T(8,128)(2,1)S(1)}, bf16[160,640]{1,0:T(8,128)(2,1)S(1)}, u32[]{:S(2)}, u32[]{:S(2)}) collective-permute-start(bf16[160,640]{1,0:T(8,128)(2,1)S(1)} %collective-permute-done.8.refs_10_), channel_id=1, source_target_pairs={{0,8},{2,10},{8,16},{10,18},{16,24},{18,26},{24,28},{26,30},{28,20... | collective-permute-start | bytes 614408 | tf_op jit(solution)/shard_map/ppermute | solution.py:304
  25.0 9.2 %collective-permute-start.5 = (bf16[160,640]{1,0:T(8,128)(2,1)S(1)}, bf16[160,640]{1,0:T(8,128)(2,1)S(1)}, u32[]{:S(2)}, u32[]{:S(2)}) collective-permute-start(bf16[160,640]{1,0:T(8,128)(2,1)S(1)} %collective-permute-done.3.refs_4_), channel_id=1, source_target_pairs={{0,8},{2,10},{8,16},{10,18},{16,24},{18,26},{24,28},{26,30},{28,20... | collective-permute-start | bytes 614408 | tf_op jit(solution)/shard_map/ppermute | solution.py:304
  27.2 9.2 %collective-permute-start.13 = (bf16[160,640]{1,0:T(8,128)(2,1)S(1)}, bf16[160,640]{1,0:T(8,128)(2,1)S(1)}, u32[]{:S(2)}, u32[]{:S(2)}) collective-permute-start(bf16[160,640]{1,0:T(8,128)(2,1)S(1)} %collective-permute-done.11.refs_13_), channel_id=1, source_target_pairs={{0,4},{2,6},{8,0},{10,2},{16,8},{18,10},{24,16},{26,18},{28,24},{3... | collective-permute-start | bytes 614408 | tf_op jit(solution)/shard_map/ppermute | solution.py:305
  31.6 8.8 %collective-permute-start.6 = (bf16[160,640]{1,0:T(8,128)(2,1)S(1)}, bf16[160,640]{1,0:T(8,128)(2,1)S(1)}, u32[]{:S(2)}, u32[]{:S(2)}) collective-permute-start(bf16[160,640]{1,0:T(8,128)(2,1)S(1)} %collective-permute-done.4.refs_5_), channel_id=1, source_target_pairs={{0,4},{2,6},{8,0},{10,2},{16,8},{18,10},{24,16},{26,18},{28,24},{3... | collective-permute-start | bytes 614408 | tf_op jit(solution)/shard_map/ppermute | solution.py:305
  31.6 8.8 %collective-permute-start.12 = (bf16[160,640]{1,0:T(8,128)(2,1)S(1)}, bf16[160,640]{1,0:T(8,128)(2,1)S(1)}, u32[]{:S(2)}, u32[]{:S(2)}) collective-permute-start(bf16[160,640]{1,0:T(8,128)(2,1)S(1)} %collective-permute-done.10.refs_12_), channel_id=1, source_target_pairs={{0,8},{2,10},{8,16},{10,18},{16,24},{18,26},{24,28},{26,30},{28,20... | collective-permute-start | bytes 614408 | tf_op jit(solution)/shard_map/ppermute | solution.py:304
  34.2 7.8 %collective-permute-start.7 = (bf16[160,640]{1,0:T(8,128)(2,1)S(1)}, bf16[160,640]{1,0:T(8,128)(2,1)S(1)}, u32[]{:S(2)}, u32[]{:S(2)}) collective-permute-start(bf16[160,640]{1,0:T(8,128)(2,1)S(1)} %collective-permute-done.5.refs_6_), channel_id=1, source_target_pairs={{0,8},{2,10},{8,16},{10,18},{16,24},{18,26},{24,28},{26,30},{28,20... | collective-permute-start | bytes 614408 | tf_op jit(solution)/shard_map/ppermute | solution.py:304
  36.4 7.1 %collective-permute-start.14 = (bf16[160,640]{1,0:T(8,128)(2,1)S(1)}, bf16[160,640]{1,0:T(8,128)(2,1)S(1)}, u32[]{:S(2)}, u32[]{:S(2)}) collective-permute-start(bf16[160,640]{1,0:T(8,128)(2,1)S(1)} %collective-permute-done.13.refs_15_), channel_id=1, source_target_pairs={{0,4},{2,6},{8,0},{10,2},{16,8},{18,10},{24,16},{26,18},{28,24},{3... | collective-permute-start | bytes 614408 | tf_op jit(solution)/shard_map/ppermute | solution.py:305
  58.5 25.6 %collective-permute-start.33 = (bf16[1728,384]{1,0:T(8,128)(2,1)S(1)}, bf16[1728,384]{1,0:T(8,128)(2,1)S(1)}, u32[]{:S(2)}, u32[]{:S(2)}) collective-permute-start(bf16[1728,384]{1,0:T(8,128)(2,1)S(1)} %get-tuple-element.70.share), channel_id=1, source_target_pairs={{0,2},{2,0},{4,6},{6,4},{8,10},{10,8},{12,14},{14,12},{16,18},{18,... | collective-permute-start | bytes 3981320 | tf_op jit(solution)/shard_map/ppermute | solution.py:302
  58.6 5.7 %collective-permute-start.16 = (f32[40,640]{1,0:T(8,128)S(1)}, f32[40,640]{1,0:T(8,128)S(1)}, u32[]{:S(2)}, u32[]{:S(2)}) collective-permute-start(f32[40,640]{1,0:T(8,128)S(1)} %get-tuple-element.52), channel_id=1, source_target_pairs={{0,8},{2,10},{8,16},{10,18},{16,24},{18,26},{24,28},{26,30},{28,20... | collective-permute-start | bytes 307208 | tf_op jit(solution)/shard_map/ppermute | solution.py:304
  60.2 5.8 %collective-permute-start.23 = (f32[40,640]{1,0:T(8,128)S(1)}, f32[40,640]{1,0:T(8,128)S(1)}, u32[]{:S(2)}, u32[]{:S(2)}) collective-permute-start(f32[40,640]{1,0:T(8,128)S(1)} %get-tuple-element.60), channel_id=1, source_target_pairs={{0,4},{2,6},{8,0},{10,2},{16,8},{18,10},{24,16},{26,18},{28,24},{3... | collective-permute-start | bytes 307208 | tf_op jit(solution)/shard_map/ppermute | solution.py:305
  60.7 6.7 %collective-permute-start.20 = (f32[40,640]{1,0:T(8,128)S(1)}, f32[40,640]{1,0:T(8,128)S(1)}, u32[]{:S(2)}, u32[]{:S(2)}) collective-permute-start(f32[40,640]{1,0:T(8,128)S(1)} %get-tuple-element.56), channel_id=1, source_target_pairs={{0,4},{2,6},{8,0},{10,2},{16,8},{18,10},{24,16},{26,18},{28,24},{3... | collective-permute-start | bytes 307208 | tf_op jit(solution)/shard_map/ppermute | solution.py:305
  61.0 6.9 %collective-permute-start.27 = (f32[40,640]{1,0:T(8,128)S(1)}, f32[40,640]{1,0:T(8,128)S(1)}, u32[]{:S(2)}, u32[]{:S(2)}) collective-permute-start(f32[40,640]{1,0:T(8,128)S(1)} %get-tuple-element.64), channel_id=1, source_target_pairs={{0,8},{2,10},{8,16},{10,18},{16,24},{18,26},{24,28},{26,30},{28,20... | collective-permute-start | bytes 307208 | tf_op jit(solution)/shard_map/ppermute | solution.py:304
  64.3 5.2 %collective-permute-start.17 = (f32[40,640]{1,0:T(8,128)S(1)}, f32[40,640]{1,0:T(8,128)S(1)}, u32[]{:S(2)}, u32[]{:S(2)}) collective-permute-start(f32[40,640]{1,0:T(8,128)S(1)} %add.30), channel_id=1, source_target_pairs={{0,8},{2,10},{8,16},{10,18},{16,24},{18,26},{24,28},{26,30},{28,20... | collective-permute-start | bytes 307208 | tf_op jit(solution)/shard_map/ppermute | solution.py:304
  66.0 5.6 %collective-permute-start.24 = (f32[40,640]{1,0:T(8,128)S(1)}, f32[40,640]{1,0:T(8,128)S(1)}, u32[]{:S(2)}, u32[]{:S(2)}) collective-permute-start(f32[40,640]{1,0:T(8,128)S(1)} %add.35), channel_id=1, source_target_pairs={{0,4},{2,6},{8,0},{10,2},{16,8},{18,10},{24,16},{26,18},{28,24},{3... | collective-permute-start | bytes 307208 | tf_op jit(solution)/shard_map/ppermute | solution.py:305
  67.4 5.5 %collective-permute-start.21 = (f32[40,640]{1,0:T(8,128)S(1)}, f32[40,640]{1,0:T(8,128)S(1)}, u32[]{:S(2)}, u32[]{:S(2)}) collective-permute-start(f32[40,640]{1,0:T(8,128)S(1)} %add.33), channel_id=1, source_target_pairs={{0,4},{2,6},{8,0},{10,2},{16,8},{18,10},{24,16},{26,18},{28,24},{3... | collective-permute-start | bytes 307208 | tf_op jit(solution)/shard_map/ppermute | solution.py:305
  67.9 5.5 %collective-permute-start.28 = (f32[40,640]{1,0:T(8,128)S(1)}, f32[40,640]{1,0:T(8,128)S(1)}, u32[]{:S(2)}, u32[]{:S(2)}) collective-permute-start(f32[40,640]{1,0:T(8,128)S(1)} %add.38), channel_id=1, source_target_pairs={{0,8},{2,10},{8,16},{10,18},{16,24},{18,26},{24,28},{26,30},{28,20... | collective-permute-start | bytes 307208 | tf_op jit(solution)/shard_map/ppermute | solution.py:304
  69.6 5.5 %collective-permute-start.18 = (f32[40,640]{1,0:T(8,128)S(1)}, f32[40,640]{1,0:T(8,128)S(1)}, u32[]{:S(2)}, u32[]{:S(2)}) collective-permute-start(f32[40,640]{1,0:T(8,128)S(1)} %add.31), channel_id=1, source_target_pairs={{0,8},{2,10},{8,16},{10,18},{16,24},{18,26},{24,28},{26,30},{28,20... | collective-permute-start | bytes 307208 | tf_op jit(solution)/shard_map/ppermute | solution.py:304
  71.6 5.5 %collective-permute-start.25 = (f32[40,640]{1,0:T(8,128)S(1)}, f32[40,640]{1,0:T(8,128)S(1)}, u32[]{:S(2)}, u32[]{:S(2)}) collective-permute-start(f32[40,640]{1,0:T(8,128)S(1)} %add.36), channel_id=1, source_target_pairs={{0,4},{2,6},{8,0},{10,2},{16,8},{18,10},{24,16},{26,18},{28,24},{3... | collective-permute-start | bytes 307208 | tf_op jit(solution)/shard_map/ppermute | solution.py:305
  72.9 5.3 %collective-permute-start.22 = (f32[40,640]{1,0:T(8,128)S(1)}, f32[40,640]{1,0:T(8,128)S(1)}, u32[]{:S(2)}, u32[]{:S(2)}) collective-permute-start(f32[40,640]{1,0:T(8,128)S(1)} %add.34), channel_id=1, source_target_pairs={{0,4},{2,6},{8,0},{10,2},{16,8},{18,10},{24,16},{26,18},{28,24},{3... | collective-permute-start | bytes 307208 | tf_op jit(solution)/shard_map/ppermute | solution.py:305
  73.4 4.8 %collective-permute-start.29 = (f32[40,640]{1,0:T(8,128)S(1)}, f32[40,640]{1,0:T(8,128)S(1)}, u32[]{:S(2)}, u32[]{:S(2)}) collective-permute-start(f32[40,640]{1,0:T(8,128)S(1)} %add.39), channel_id=1, source_target_pairs={{0,8},{2,10},{8,16},{10,18},{16,24},{18,26},{24,28},{26,30},{28,20... | collective-permute-start | bytes 307208 | tf_op jit(solution)/shard_map/ppermute | solution.py:304
  75.1 4.7 %collective-permute-start.19 = (f32[40,640]{1,0:T(8,128)S(1)}, f32[40,640]{1,0:T(8,128)S(1)}, u32[]{:S(2)}, u32[]{:S(2)}) collective-permute-start(f32[40,640]{1,0:T(8,128)S(1)} %add.32), channel_id=1, source_target_pairs={{0,8},{2,10},{8,16},{10,18},{16,24},{18,26},{24,28},{26,30},{28,20... | collective-permute-start | bytes 307208 | tf_op jit(solution)/shard_map/ppermute | solution.py:304
  81.9 5.2 %collective-permute-start.32 = (f32[40,640]{1,0:T(8,128)S(1)}, f32[40,640]{1,0:T(8,128)S(1)}, u32[]{:S(2)}, u32[]{:S(2)}) collective-permute-start(f32[40,640]{1,0:T(8,128)S(1)} %get-tuple-element.67), channel_id=1, source_target_pairs={{0,3},{1,2},{2,1},{3,0},{4,7},{5,6},{6,5},{7,4},{8,11},{9,10},{10,... | collective-permute-start | bytes 307208 | tf_op jit(solution)/shard_map/ppermute | solution.py:393
  81.9 5.1 %collective-permute-start.30 = (f32[40,640]{1,0:T(8,128)S(1)}, f32[40,640]{1,0:T(8,128)S(1)}, u32[]{:S(2)}, u32[]{:S(2)}) collective-permute-start(f32[40,640]{1,0:T(8,128)S(1)} %get-tuple-element.67), channel_id=1, source_target_pairs={{0,2},{2,0},{4,6},{6,4},{8,10},{10,8},{12,14},{14,12},{16,18},{18,... | collective-permute-start | bytes 307208 | tf_op jit(solution)/shard_map/ppermute | solution.py:302
  83.6 5.7 %collective-permute-start.31 = (f32[40,640]{1,0:T(8,128)S(1)}, f32[40,640]{1,0:T(8,128)S(1)}, u32[]{:S(2)}, u32[]{:S(2)}) collective-permute-start(f32[40,640]{1,0:T(8,128)S(1)} %get-tuple-element.68.keep), channel_id=1, source_target_pairs={{0,1},{1,0},{2,3},{3,2},{4,5},{5,4},{6,7},{7,6},{8,9},{9,8},{10,11... | collective-permute-start | bytes 307208 | tf_op jit(solution)/shard_map/ppermute | solution.py:392
  (8 other events, 35.4 us)

commit v5 on v4

--- a/solution.py
+++ b/solution.py
@@ -145,9 +145,7 @@
     mine, other, t0, t1 = take(4)
     share, ctx_own = take(2)
     sums = take(len(pieces))
-    w, loaded, whole, sem = take(4)
-    load = pltpu.make_async_copy(other, loaded, sem)
-    load.start()
+    w, whole = take(2)
     number, width = CORE_HEADS, WIDE
     chip_rows = w.shape[0] // chips
     if len(steps[0]) == 1:
@@ -163,48 +161,56 @@
     rows_of = []
 
     def project(clip):
-        acts = (mine, loaded)[clip]
-        if clip == 1:
-            load.wait()
+        acts = (mine, other)[clip]
         q = (dot(acts[x_at, :], w[:, :width]) * 0.125).astype(BF)
         kv = dot(acts[e_at, :], w[:, width : 3 * width]).astype(BF)
         g = dot(acts[g_at, :], w[:, 3 * width :]).astype(BF)
         k, v = kv[:, :width], kv[:, width:]
         rows_of.append((q, k, v, g, k.T, v.T, g.T))
 
-    def begin(clip, h):
+    def begin(clip, h, tokens):
         q, k, v, g, _, _, _ = rows_of[clip]
         cols = slice(h * HEAD_DIM, (h + 1) * HEAD_DIM)
-        return dot(k[:, cols], q[:, cols], ROWS), dot(v[:, cols], g[:, cols], ROWS)
-
-    def finish(clip, h, scores, grad_attention):
+        return dot(k[:, cols], q[tokens, cols], ROWS), dot(v[:, cols], g[tokens, cols], ROWS)
+
+    def finish(clip, h, tokens, scores, grad_attention):
         _, _, _, _, kt, vt, gt = rows_of[clip]
         cols = slice(h * HEAD_DIM, (h + 1) * HEAD_DIM)
         e = jnp.exp(scores - jnp.max(scores, axis=0, keepdims=True))
         attention = (e * (1.0 / jnp.sum(e, axis=0, keepdims=True))).astype(BF)
         ctx = dot(vt[cols], attention)
-        inner = jnp.sum(gt[cols].astype(F32) * ctx, axis=0, keepdims=True)
+        inner = jnp.sum(gt[cols, tokens].astype(F32) * ctx, axis=0, keepdims=True)
         grad_scores = (attention.astype(F32) * (grad_attention - inner)).astype(BF)
         return ctx.astype(BF), (dot(kt[cols], grad_scores) * 0.125).astype(BF)
 
-    items = [(clip, h) for clip in range(2) for h in range(number)]
+    halves = (slice(0, 256), slice(256, TOK))
+    items = [(clip, h, t) for clip in range(2) for h in range(number) for t in halves]
     project(0)
-    begun = begin(*items[0])
+    begun = [begin(*item) for item in items[:2]]
     done = []
     for i, item in enumerate(items):
-        now = begun
-        if i == 1:
+        if i == 6:
             project(1)
-        if i + 1 < len(items):
-            begun = begin(*items[i + 1])
-        done.append(finish(*item, *now))
-    ctx_own[...] = jnp.concatenate([c for c, _ in done[:number]], axis=0).T
-    share[:TOK, :width] = jnp.concatenate([c for c, _ in done[number:]], axis=0).T
+        if i + 2 < len(items):
+            begun.append(begin(*items[i + 2]))
+        done.append(finish(*item, *begun[i]))
+    ctxs, grads = [
+        [
+            jnp.concatenate(
+                [
+                    jnp.concatenate([done[(c * number + h) * 2 + t][which] for t in (0, 1)], axis=1)
+                    for h in range(number)
+                ],
+                axis=0,
+            ).T
+            for c in (0, 1)
+        ]
+        for which in (0, 1)
+    ]
+    ctx_own[...] = ctxs[0]
+    share[:TOK, :width] = ctxs[1]
     share[TOK:, :width] = w[:, 3 * width :]
-    grads = [
-        jnp.concatenate([g for _, g in done[c * number : (c + 1) * number]], axis=0) for c in (0, 1)
-    ]
-    whole[...] = dot(t0[...], grads[0].T) + dot(t1[...], grads[1].T)
+    whole[...] = dot(t0[...], grads[0]) + dot(t1[...], grads[1])
     for out, (k, skip) in zip(sums, pieces):
         fold = out.shape[1] // width
         for i in range(fold):
@@ -223,10 +229,10 @@
             jax.ShapeDtypeStruct((TOK, width), BF),
         )
         + (jax.ShapeDtypeStruct(piece_shape, F32),) * len(pieces),
-        in_specs=[SM] + [VM] * len(blocks) + [VM, ANY, VM, VM],
+        in_specs=[SM] + [VM] * (len(blocks) + 4),
         out_specs=(VM,) * (2 + len(pieces)),
         scratch_shapes=[pltpu.VMEM((depth, 4 * width), BF)]
-        + [pltpu.VMEM(acts[1].shape, BF), pltpu.VMEM((depth, width), F32), pltpu.SemaphoreType.DMA],
+        + [pltpu.VMEM((depth, width), F32)],
         compiler_params=pltpu.CompilerParams(vmem_limit_bytes=22 * 2**20),
         cost_estimate=pl.CostEstimate(
             flops=9 * 10**9, bytes_accessed=15 * 10**6, transcendentals=2 * 10**6

time: 90.7 us -> 88.9 us (0.980)
  Pallas kernels: 24.7 us -> 23 us
    pallas_call x1, Pallas kernels: 15 us -> 13.2 us  [heads(): pl.pallas_call(functools.partial(head_kernel, chips, steps, pieces), out_...]
where the time goes in v5:
time: 88.9 us; the launch traced here: 88.7 us
  starting transfers between devices  33.3 us (37%)
  waiting for transfers between devices  28.8 us (32%)
  Pallas kernels  23 us (26%)
  local copies, waits for them, and re-layouts  2.03 us (2%)
  between operations  1.45 us (2%)
    ppermute x14, starting transfers between devices, per_device(): right = lambda a: lax.ppermute(a, 'dp', ring_pairs(chips, 1))  25.6 us
    ppermute x14, waiting for transfers between devices, per_device(): left = lambda a: lax.ppermute(a, 'dp', ring_pairs(chips, -1))  16.7 us
    pallas_call x1, Pallas kernels, heads(): pl.pallas_call(functools.partial(head_kernel, chips, steps, pieces), out_...  13.2 us
    ppermute x14, waiting for transfers between devices, per_device(): right = lambda a: lax.ppermute(a, 'dp', ring_pairs(chips, 1))  9.29 us
    ppermute x14, starting transfers between devices, per_device(): left = lambda a: lax.ppermute(a, 'dp', ring_pairs(chips, -1))  4.83 us
    pallas_call x1, Pallas kernels, per_device(): pl.pallas_call(stage_kernel, out_shape=jax.ShapeDtypeStruct((2 * TOK + fr...  3.33 us
    pallas_call x1, Pallas kernels, per_device(): pl.pallas_call(out_kernel, out_shape=jax.ShapeDtypeStruct((TOK, depth), B...  2.37 us
    ppermute x4, starting transfers between devices, per_device(): swap = lambda a: lax.ppermute(a, 'dp', mates)  2.34 us
  transfers between devices with their start and end apart: 34, of which 17 were waited for; matrix products, arithmetic and copies ran while one was open for 0% of the time, Pallas kernels for 7%

profile of v5, /device:TPU:0, one launch (start us, length us, event | category | flops | bytes accessed | tf_op | source)
XLA Modules:
  0.0 88.7 jit_solution(9672324986247099130)
XLA Ops:
  0.6 2.0 %shard_map.137 = (bf16[80,1280]{1,0:T(8,128)(2,1)}, bf16[80,1280]{1,0:T(8,128)(2,1)}) custom-call(s32[1]{0:T(128)} %bitcast.me.refs_0_, f32[80,640]{1,0:T(8,128)} %master.1, bf16[80,640]{1,0:T(8,128)(2,1)} %k.1, bf16[80,640]{1,0:T(8,128)(2,1)} %v.1, bf16[80,640]{1,0:T(8,128)(2,1)} %bitcast.2), custom_call_target="tpu_custom_call" | custom-call | tf_op jit(solution)/shard_map/pallas_call | solution.py:315
  3.9 3.3 %shard_map.138.mine.refs_17_ = bf16[1408,1280]{1,0:T(8,128)(2,1)} custom-call(s32[1]{0:T(128)S(6)} %copy.15.length, bf16[448,1280]{1,0:T(8,128)(2,1)} %x.1, bf16[512,1280]{1,0:T(8,128)(2,1)} %e.1, bf16[448,1280]{1,0:T(8,128)(2,1)} %g.1, bf16[80,1280]{1,0:T(8,128)(2,1)} %get-tuple-element.42._.keep), custom_call_target="tpu_custom_call" | custom-call | tf_op jit(solution)/shard_map/pallas_call | solution.py:326
  7.4 3.0 %collective-permute-start.1 = (bf16[160,640]{1,0:T(8,128)(2,1)S(1)}, bf16[160,640]{1,0:T(8,128)(2,1)S(1)}, u32[]{:S(2)}, u32[]{:S(2)}) collective-permute-start(bf16[160,640]{1,0:T(8,128)(2,1)S(1)} %get-tuple-element.46.refs_1_), channel_id=1, source_target_pairs={{0,8},{2,10},{8,16},{10,18},{16,24},{18,26},{24,28},{26,30},{28,20... | collective-permute-start | bytes 614408 | tf_op jit(solution)/shard_map/ppermute | solution.py:310
  10.4 1.9 %collective-permute-start.2 = (bf16[160,640]{1,0:T(8,128)(2,1)S(1)}, bf16[160,640]{1,0:T(8,128)(2,1)S(1)}, u32[]{:S(2)}, u32[]{:S(2)}) collective-permute-start(bf16[160,640]{1,0:T(8,128)(2,1)S(1)} %get-tuple-element.46.refs_1_), channel_id=1, source_target_pairs={{0,4},{2,6},{8,0},{10,2},{16,8},{18,10},{24,16},{26,18},{28,24},{3... | collective-permute-start | bytes 614408 | tf_op jit(solution)/shard_map/ppermute | solution.py:311
  12.5 3.7 %collective-permute-done.1.refs_2_ = bf16[160,640]{1,0:T(8,128)(2,1)S(1)} collective-permute-done((bf16[160,640]{1,0:T(8,128)(2,1)S(1)}, bf16[160,640]{1,0:T(8,128)(2,1)S(1)}, u32[]{:S(2)}, u32[]{:S(2)}) %collective-permute-start.1) | collective-permute-done | bytes 204832 | tf_op jit(solution)/shard_map/ppermute | solution.py:310
  16.2 2.1 %collective-permute-start.3 = (bf16[160,640]{1,0:T(8,128)(2,1)S(1)}, bf16[160,640]{1,0:T(8,128)(2,1)S(1)}, u32[]{:S(2)}, u32[]{:S(2)}) collective-permute-start(bf16[160,640]{1,0:T(8,128)(2,1)S(1)} %collective-permute-done.1.refs_2_), channel_id=1, source_target_pairs={{0,8},{2,10},{8,16},{10,18},{16,24},{18,26},{24,28},{26,30},{28,20... | collective-permute-start | bytes 614408 | tf_op jit(solution)/shard_map/ppermute | solution.py:310
  18.4 4.4 %collective-permute-done.2.refs_3_ = bf16[160,640]{1,0:T(8,128)(2,1)S(1)} collective-permute-done((bf16[160,640]{1,0:T(8,128)(2,1)S(1)}, bf16[160,640]{1,0:T(8,128)(2,1)S(1)}, u32[]{:S(2)}, u32[]{:S(2)}) %collective-permute-start.2) | collective-permute-done | bytes 204832 | tf_op jit(solution)/shard_map/ppermute | solution.py:311
  22.8 2.0 %collective-permute-start.10 = (bf16[160,640]{1,0:T(8,128)(2,1)S(1)}, bf16[160,640]{1,0:T(8,128)(2,1)S(1)}, u32[]{:S(2)}, u32[]{:S(2)}) collective-permute-start(bf16[160,640]{1,0:T(8,128)(2,1)S(1)} %collective-permute-done.8.refs_10_), channel_id=1, source_target_pairs={{0,8},{2,10},{8,16},{10,18},{16,24},{18,26},{24,28},{26,30},{28,20... | collective-permute-start | bytes 614408 | tf_op jit(solution)/shard_map/ppermute | solution.py:310
  25.0 2.1 %collective-permute-start.5 = (bf16[160,640]{1,0:T(8,128)(2,1)S(1)}, bf16[160,640]{1,0:T(8,128)(2,1)S(1)}, u32[]{:S(2)}, u32[]{:S(2)}) collective-permute-start(bf16[160,640]{1,0:T(8,128)(2,1)S(1)} %collective-permute-done.3.refs_4_), channel_id=1, source_target_pairs={{0,8},{2,10},{8,16},{10,18},{16,24},{18,26},{24,28},{26,30},{28,20... | collective-permute-start | bytes 614408 | tf_op jit(solution)/shard_map/ppermute | solution.py:310
  27.2 4.4 %collective-permute-done.4.refs_5_ = bf16[160,640]{1,0:T(8,128)(2,1)S(1)} collective-permute-done((bf16[160,640]{1,0:T(8,128)(2,1)S(1)}, bf16[160,640]{1,0:T(8,128)(2,1)S(1)}, u32[]{:S(2)}, u32[]{:S(2)}) %collective-permute-start.4) | collective-permute-done | bytes 204832 | tf_op jit(solution)/shard_map/ppermute | solution.py:311
  31.6 2.0 %collective-permute-start.12 = (bf16[160,640]{1,0:T(8,128)(2,1)S(1)}, bf16[160,640]{1,0:T(8,128)(2,1)S(1)}, u32[]{:S(2)}, u32[]{:S(2)}) collective-permute-start(bf16[160,640]{1,0:T(8,128)(2,1)S(1)} %collective-permute-done.10.refs_12_), channel_id=1, source_target_pairs={{0,8},{2,10},{8,16},{10,18},{16,24},{18,26},{24,28},{26,30},{28,20... | collective-permute-start | bytes 614408 | tf_op jit(solution)/shard_map/ppermute | solution.py:310
  34.2 2.2 %collective-permute-start.7 = (bf16[160,640]{1,0:T(8,128)(2,1)S(1)}, bf16[160,640]{1,0:T(8,128)(2,1)S(1)}, u32[]{:S(2)}, u32[]{:S(2)}) collective-permute-start(bf16[160,640]{1,0:T(8,128)(2,1)S(1)} %collective-permute-done.5.refs_6_), channel_id=1, source_target_pairs={{0,8},{2,10},{8,16},{10,18},{16,24},{18,26},{24,28},{26,30},{28,20... | collective-permute-start | bytes 614408 | tf_op jit(solution)/shard_map/ppermute | solution.py:310
  36.4 2.0 %copy-done = bf16[1408,1280]{1,0:T(8,128)(2,1)S(1)} copy-done((bf16[1408,1280]{1,0:T(8,128)(2,1)S(1)}, bf16[1408,1280]{1,0:T(8,128)(2,1)}, u32[]{:S(2)}) %copy-start) | copy-done | bytes 3604504
  39.2 1.2 %collective-permute-done.6.refs_7_ = bf16[160,640]{1,0:T(8,128)(2,1)S(1)} collective-permute-done((bf16[160,640]{1,0:T(8,128)(2,1)S(1)}, bf16[160,640]{1,0:T(8,128)(2,1)S(1)}, u32[]{:S(2)}, u32[]{:S(2)}) %collective-permute-start.6) | collective-permute-done | bytes 204832 | tf_op jit(solution)/shard_map/ppermute | solution.py:311
  40.3 1.6 %collective-permute-done.7.refs_8_ = bf16[160,640]{1,0:T(8,128)(2,1)S(1)} collective-permute-done((bf16[160,640]{1,0:T(8,128)(2,1)S(1)}, bf16[160,640]{1,0:T(8,128)(2,1)S(1)}, u32[]{:S(2)}, u32[]{:S(2)}) %collective-permute-start.7) | collective-permute-done | bytes 204832 | tf_op jit(solution)/shard_map/ppermute | solution.py:310
  42.0 1.5 %collective-permute-done.14.refs_16_ = bf16[160,640]{1,0:T(8,128)(2,1)S(1)} collective-permute-done((bf16[160,640]{1,0:T(8,128)(2,1)S(1)}, bf16[160,640]{1,0:T(8,128)(2,1)S(1)}, u32[]{:S(2)}, u32[]{:S(2)}) %collective-permute-start.14) | collective-permute-done | bytes 204832 | tf_op jit(solution)/shard_map/ppermute | solution.py:311
  43.5 13.2 %shard_map.141 = (bf16[1728,384]{1,0:T(8,128)(2,1)S(1)}, bf16[448,320]{1,0:T(8,128)(2,1)S(1)}, f32[40,640]{1,0:T(8,128)S(1)}, f32[40,640]{1,0:T(8,128)S(1)}, f32...) custom-call(s32[1]{0:T(128)} %bitcast.me.refs_0_, ...), custom_call_target="tpu_custom_call" | custom-call | flops 8999999488 | bytes 15000000 | tf_op jit(solution)/shard_map/pallas_call | solution.py:225
  56.8 1.6 %collective-permute-start.16 = (f32[40,640]{1,0:T(8,128)S(1)}, f32[40,640]{1,0:T(8,128)S(1)}, u32[]{:S(2)}, u32[]{:S(2)}) collective-permute-start(f32[40,640]{1,0:T(8,128)S(1)} %get-tuple-element.52), channel_id=1, source_target_pairs={{0,8},{2,10},{8,16},{10,18},{16,24},{18,26},{24,28},{26,30},{28,20... | collective-permute-start | bytes 307208 | tf_op jit(solution)/shard_map/ppermute | solution.py:310
  59.2 1.7 %collective-permute-start.27 = (f32[40,640]{1,0:T(8,128)S(1)}, f32[40,640]{1,0:T(8,128)S(1)}, u32[]{:S(2)}, u32[]{:S(2)}) collective-permute-start(f32[40,640]{1,0:T(8,128)S(1)} %get-tuple-element.64), channel_id=1, source_target_pairs={{0,8},{2,10},{8,16},{10,18},{16,24},{18,26},{24,28},{26,30},{28,20... | collective-permute-start | bytes 307208 | tf_op jit(solution)/shard_map/ppermute | solution.py:310
  60.9 1.6 %collective-permute-done.16 = f32[40,640]{1,0:T(8,128)S(1)} collective-permute-done((f32[40,640]{1,0:T(8,128)S(1)}, f32[40,640]{1,0:T(8,128)S(1)}, u32[]{:S(2)}, u32[]{:S(2)}) %collective-permute-start.16) | collective-permute-done | bytes 102432 | tf_op jit(solution)/shard_map/ppermute | solution.py:310
  62.6 1.6 %collective-permute-start.17 = (f32[40,640]{1,0:T(8,128)S(1)}, f32[40,640]{1,0:T(8,128)S(1)}, u32[]{:S(2)}, u32[]{:S(2)}) collective-permute-start(f32[40,640]{1,0:T(8,128)S(1)} %add.30), channel_id=1, source_target_pairs={{0,8},{2,10},{8,16},{10,18},{16,24},{18,26},{24,28},{26,30},{28,20... | collective-permute-start | bytes 307208 | tf_op jit(solution)/shard_map/ppermute | solution.py:310
  66.1 1.6 %collective-permute-start.28 = (f32[40,640]{1,0:T(8,128)S(1)}, f32[40,640]{1,0:T(8,128)S(1)}, u32[]{:S(2)}, u32[]{:S(2)}) collective-permute-start(f32[40,640]{1,0:T(8,128)S(1)} %add.38), channel_id=1, source_target_pairs={{0,8},{2,10},{8,16},{10,18},{16,24},{18,26},{24,28},{26,30},{28,20... | collective-permute-start | bytes 307208 | tf_op jit(solution)/shard_map/ppermute | solution.py:310
  67.8 1.6 %collective-permute-start.18 = (f32[40,640]{1,0:T(8,128)S(1)}, f32[40,640]{1,0:T(8,128)S(1)}, u32[]{:S(2)}, u32[]{:S(2)}) collective-permute-start(f32[40,640]{1,0:T(8,128)S(1)} %add.31), channel_id=1, source_target_pairs={{0,8},{2,10},{8,16},{10,18},{16,24},{18,26},{24,28},{26,30},{28,20... | collective-permute-start | bytes 307208 | tf_op jit(solution)/shard_map/ppermute | solution.py:310
  71.7 1.6 %collective-permute-start.29 = (f32[40,640]{1,0:T(8,128)S(1)}, f32[40,640]{1,0:T(8,128)S(1)}, u32[]{:S(2)}, u32[]{:S(2)}) collective-permute-start(f32[40,640]{1,0:T(8,128)S(1)} %add.39), channel_id=1, source_target_pairs={{0,8},{2,10},{8,16},{10,18},{16,24},{18,26},{24,28},{26,30},{28,20... | collective-permute-start | bytes 307208 | tf_op jit(solution)/shard_map/ppermute | solution.py:310
  73.3 2.0 %collective-permute-start.19 = (f32[40,640]{1,0:T(8,128)S(1)}, f32[40,640]{1,0:T(8,128)S(1)}, u32[]{:S(2)}, u32[]{:S(2)}) collective-permute-start(f32[40,640]{1,0:T(8,128)S(1)} %add.32), channel_id=1, source_target_pairs={{0,8},{2,10},{8,16},{10,18},{16,24},{18,26},{24,28},{26,30},{28,20... | collective-permute-start | bytes 307208 | tf_op jit(solution)/shard_map/ppermute | solution.py:310
  75.5 1.0 %collective-permute-done.22.refs_2_ = f32[40,640]{1,0:T(8,128)S(1)} collective-permute-done((f32[40,640]{1,0:T(8,128)S(1)}, f32[40,640]{1,0:T(8,128)S(1)}, u32[]{:S(2)}, u32[]{:S(2)}) %collective-permute-start.22) | collective-permute-done | bytes 102432 | tf_op jit(solution)/shard_map/ppermute | solution.py:311
  76.5 1.5 %collective-permute-done.19.refs_1_ = f32[40,640]{1,0:T(8,128)S(1)} collective-permute-done((f32[40,640]{1,0:T(8,128)S(1)}, f32[40,640]{1,0:T(8,128)S(1)}, u32[]{:S(2)}, u32[]{:S(2)}) %collective-permute-start.19) | collective-permute-done | bytes 102432 | tf_op jit(solution)/shard_map/ppermute | solution.py:310
  78.0 2.0 %collective-permute-done.26.refs_4_ = f32[40,640]{1,0:T(8,128)S(1)} collective-permute-done((f32[40,640]{1,0:T(8,128)S(1)}, f32[40,640]{1,0:T(8,128)S(1)}, u32[]{:S(2)}, u32[]{:S(2)}) %collective-permute-start.26) | collective-permute-done | bytes 102432 | tf_op jit(solution)/shard_map/ppermute | solution.py:311
  80.2 1.6 %collective-permute-start.30 = (f32[40,640]{1,0:T(8,128)S(1)}, f32[40,640]{1,0:T(8,128)S(1)}, u32[]{:S(2)}, u32[]{:S(2)}) collective-permute-start(f32[40,640]{1,0:T(8,128)S(1)} %get-tuple-element.67), channel_id=1, source_target_pairs={{0,2},{2,0},{4,6},{6,4},{8,10},{10,8},{12,14},{14,12},{16,18},{18,... | collective-permute-start | bytes 307208 | tf_op jit(solution)/shard_map/ppermute | solution.py:308
  82.3 2.4 %shard_map.143 = bf16[448,1280]{1,0:T(8,128)(2,1)} custom-call(bf16[448,320]{1,0:T(8,128)(2,1)S(1)} %get-tuple-element.69.ctx_own, bf16[1728,384]{1,0:T(8,128)(2,1)S(1)} %get-tuple-element.70.share, bf16[1728,384]{1,0:T(8,128)(2,1)S(1)} %collective-permute-done.33.got), custom_call_target="tpu_custom_call" | custom-call | flops 734003200 | bytes 4000000 | tf_op jit(solution)/shard_map/pallas_call | solution.py:414
  85.2 2.3 %collective-permute-done.31.keep_y = f32[40,640]{1,0:T(8,128)S(1)} collective-permute-done((f32[40,640]{1,0:T(8,128)S(1)}, f32[40,640]{1,0:T(8,128)S(1)}, u32[]{:S(2)}, u32[]{:S(2)}) %collective-permute-start.31) | collective-permute-done | bytes 102432 | tf_op jit(solution)/shard_map/ppermute | solution.py:398
  87.5 1.2 %shard_map.144 = (f32[80,640]{1,0:T(8,128)}, f32[80,640]{1,0:T(8,128)}, f32[80,640]{1,0:T(8,128)}, f32[80,640]{1,0:T(8,128)}) custom-call(s32[1]{0:T(128)} %bitcast.me.refs_0_, f32[40,640]{1,0:T(8,128)S(1)} %get-tuple-element.68.keep, f32[40,640]{1,0:T(8,128)S(1)} %collective-permute-done.31.keep_y, f32[40,640]{1,0:T(8,128)S(1)} %collective-permute-done.30.got, ...), custom_call_target="tpu_custom_call" | custom-call | tf_op jit(solution)/shard_map/pallas_call | solution.py:426
  (66 shorter events, 8.8 us)
Async XLA Ops:
  7.3 29.1 %collective-permute-start.15 = (bf16[1408,1280]{1,0:T(8,128)(2,1)}, bf16[1408,1280]{1,0:T(8,128)(2,1)S(1)}, u32[]{:S(2)}, u32[]{:S(2)}) collective-permute-start(bf16[1408,1280]{1,0:T(8,128)(2,1)} %shard_map.138.mine.refs_17_), channel_id=1, source_target_pairs={{0,2},{2,0},{4,6},{6,4},{8,10},{10,8},{12,14},{14,12},{16,18},{18,... | collective-permute-start | bytes 10813448 | tf_op jit(solution)/shard_map/ppermute | solution.py:308
  7.4 8.8 %collective-permute-start.1 = (bf16[160,640]{1,0:T(8,128)(2,1)S(1)}, bf16[160,640]{1,0:T(8,128)(2,1)S(1)}, u32[]{:S(2)}, u32[]{:S(2)}) collective-permute-start(bf16[160,640]{1,0:T(8,128)(2,1)S(1)} %get-tuple-element.46.refs_1_), channel_id=1, source_target_pairs={{0,8},{2,10},{8,16},{10,18},{16,24},{18,26},{24,28},{26,30},{28,20... | collective-permute-start | bytes 614408 | tf_op jit(solution)/shard_map/ppermute | solution.py:310
  10.4 8.0 %collective-permute-start.9 = (bf16[160,640]{1,0:T(8,128)(2,1)S(1)}, bf16[160,640]{1,0:T(8,128)(2,1)S(1)}, u32[]{:S(2)}, u32[]{:S(2)}) collective-permute-start(bf16[160,640]{1,0:T(8,128)(2,1)S(1)} %get-tuple-element.47.refs_9_), channel_id=1, source_target_pairs={{0,4},{2,6},{8,0},{10,2},{16,8},{18,10},{24,16},{26,18},{28,24},{3... | collective-permute-start | bytes 614408 | tf_op jit(solution)/shard_map/ppermute | solution.py:311
  10.4 12.4 %collective-permute-start.2 = (bf16[160,640]{1,0:T(8,128)(2,1)S(1)}, bf16[160,640]{1,0:T(8,128)(2,1)S(1)}, u32[]{:S(2)}, u32[]{:S(2)}) collective-permute-start(bf16[160,640]{1,0:T(8,128)(2,1)S(1)} %get-tuple-element.46.refs_1_), channel_id=1, source_target_pairs={{0,4},{2,6},{8,0},{10,2},{16,8},{18,10},{24,16},{26,18},{28,24},{3... | collective-permute-start | bytes 614408 | tf_op jit(solution)/shard_map/ppermute | solution.py:311
  12.4 10.4 %collective-permute-start.8 = (bf16[160,640]{1,0:T(8,128)(2,1)S(1)}, bf16[160,640]{1,0:T(8,128)(2,1)S(1)}, u32[]{:S(2)}, u32[]{:S(2)}) collective-permute-start(bf16[160,640]{1,0:T(8,128)(2,1)S(1)} %get-tuple-element.47.refs_9_), channel_id=1, source_target_pairs={{0,8},{2,10},{8,16},{10,18},{16,24},{18,26},{24,28},{26,30},{28,20... | collective-permute-start | bytes 614408 | tf_op jit(solution)/shard_map/ppermute | solution.py:310
  16.2 8.8 %collective-permute-start.3 = (bf16[160,640]{1,0:T(8,128)(2,1)S(1)}, bf16[160,640]{1,0:T(8,128)(2,1)S(1)}, u32[]{:S(2)}, u32[]{:S(2)}) collective-permute-start(bf16[160,640]{1,0:T(8,128)(2,1)S(1)} %collective-permute-done.1.refs_2_), channel_id=1, source_target_pairs={{0,8},{2,10},{8,16},{10,18},{16,24},{18,26},{24,28},{26,30},{28,20... | collective-permute-start | bytes 614408 | tf_op jit(solution)/shard_map/ppermute | solution.py:310
  18.4 8.8 %collective-permute-start.11 = (bf16[160,640]{1,0:T(8,128)(2,1)S(1)}, bf16[160,640]{1,0:T(8,128)(2,1)S(1)}, u32[]{:S(2)}, u32[]{:S(2)}) collective-permute-start(bf16[160,640]{1,0:T(8,128)(2,1)S(1)} %collective-permute-done.9.refs_11_), channel_id=1, source_target_pairs={{0,4},{2,6},{8,0},{10,2},{16,8},{18,10},{24,16},{26,18},{28,24},{3... | collective-permute-start | bytes 614408 | tf_op jit(solution)/shard_map/ppermute | solution.py:311
  22.8 8.8 %collective-permute-start.4 = (bf16[160,640]{1,0:T(8,128)(2,1)S(1)}, bf16[160,640]{1,0:T(8,128)(2,1)S(1)}, u32[]{:S(2)}, u32[]{:S(2)}) collective-permute-start(bf16[160,640]{1,0:T(8,128)(2,1)S(1)} %collective-permute-done.2.refs_3_), channel_id=1, source_target_pairs={{0,4},{2,6},{8,0},{10,2},{16,8},{18,10},{24,16},{26,18},{28,24},{3... | collective-permute-start | bytes 614408 | tf_op jit(solution)/shard_map/ppermute | solution.py:311
  22.8 8.8 %collective-permute-start.10 = (bf16[160,640]{1,0:T(8,128)(2,1)S(1)}, bf16[160,640]{1,0:T(8,128)(2,1)S(1)}, u32[]{:S(2)}, u32[]{:S(2)}) collective-permute-start(bf16[160,640]{1,0:T(8,128)(2,1)S(1)} %collective-permute-done.8.refs_10_), channel_id=1, source_target_pairs={{0,8},{2,10},{8,16},{10,18},{16,24},{18,26},{24,28},{26,30},{28,20... | collective-permute-start | bytes 614408 | tf_op jit(solution)/shard_map/ppermute | solution.py:310
  25.0 9.2 %collective-permute-start.5 = (bf16[160,640]{1,0:T(8,128)(2,1)S(1)}, bf16[160,640]{1,0:T(8,128)(2,1)S(1)}, u32[]{:S(2)}, u32[]{:S(2)}) collective-permute-start(bf16[160,640]{1,0:T(8,128)(2,1)S(1)} %collective-permute-done.3.refs_4_), channel_id=1, source_target_pairs={{0,8},{2,10},{8,16},{10,18},{16,24},{18,26},{24,28},{26,30},{28,20... | collective-permute-start | bytes 614408 | tf_op jit(solution)/shard_map/ppermute | solution.py:310
  27.2 9.2 %collective-permute-start.13 = (bf16[160,640]{1,0:T(8,128)(2,1)S(1)}, bf16[160,640]{1,0:T(8,128)(2,1)S(1)}, u32[]{:S(2)}, u32[]{:S(2)}) collective-permute-start(bf16[160,640]{1,0:T(8,128)(2,1)S(1)} %collective-permute-done.11.refs_13_), channel_id=1, source_target_pairs={{0,4},{2,6},{8,0},{10,2},{16,8},{18,10},{24,16},{26,18},{28,24},{3... | collective-permute-start | bytes 614408 | tf_op jit(solution)/shard_map/ppermute | solution.py:311
  31.6 8.8 %collective-permute-start.6 = (bf16[160,640]{1,0:T(8,128)(2,1)S(1)}, bf16[160,640]{1,0:T(8,128)(2,1)S(1)}, u32[]{:S(2)}, u32[]{:S(2)}) collective-permute-start(bf16[160,640]{1,0:T(8,128)(2,1)S(1)} %collective-permute-done.4.refs_5_), channel_id=1, source_target_pairs={{0,4},{2,6},{8,0},{10,2},{16,8},{18,10},{24,16},{26,18},{28,24},{3... | collective-permute-start | bytes 614408 | tf_op jit(solution)/shard_map/ppermute | solution.py:311
  31.6 8.8 %collective-permute-start.12 = (bf16[160,640]{1,0:T(8,128)(2,1)S(1)}, bf16[160,640]{1,0:T(8,128)(2,1)S(1)}, u32[]{:S(2)}, u32[]{:S(2)}) collective-permute-start(bf16[160,640]{1,0:T(8,128)(2,1)S(1)} %collective-permute-done.10.refs_12_), channel_id=1, source_target_pairs={{0,8},{2,10},{8,16},{10,18},{16,24},{18,26},{24,28},{26,30},{28,20... | collective-permute-start | bytes 614408 | tf_op jit(solution)/shard_map/ppermute | solution.py:310
  34.2 7.8 %collective-permute-start.7 = (bf16[160,640]{1,0:T(8,128)(2,1)S(1)}, bf16[160,640]{1,0:T(8,128)(2,1)S(1)}, u32[]{:S(2)}, u32[]{:S(2)}) collective-permute-start(bf16[160,640]{1,0:T(8,128)(2,1)S(1)} %collective-permute-done.5.refs_6_), channel_id=1, source_target_pairs={{0,8},{2,10},{8,16},{10,18},{16,24},{18,26},{24,28},{26,30},{28,20... | collective-permute-start | bytes 614408 | tf_op jit(solution)/shard_map/ppermute | solution.py:310
  36.4 7.1 %collective-permute-start.14 = (bf16[160,640]{1,0:T(8,128)(2,1)S(1)}, bf16[160,640]{1,0:T(8,128)(2,1)S(1)}, u32[]{:S(2)}, u32[]{:S(2)}) collective-permute-start(bf16[160,640]{1,0:T(8,128)(2,1)S(1)} %collective-permute-done.13.refs_15_), channel_id=1, source_target_pairs={{0,4},{2,6},{8,0},{10,2},{16,8},{18,10},{24,16},{26,18},{28,24},{3... | collective-permute-start | bytes 614408 | tf_op jit(solution)/shard_map/ppermute | solution.py:311
  56.7 25.5 %collective-permute-start.33 = (bf16[1728,384]{1,0:T(8,128)(2,1)S(1)}, bf16[1728,384]{1,0:T(8,128)(2,1)S(1)}, u32[]{:S(2)}, u32[]{:S(2)}) collective-permute-start(bf16[1728,384]{1,0:T(8,128)(2,1)S(1)} %get-tuple-element.70.share), channel_id=1, source_target_pairs={{0,2},{2,0},{4,6},{6,4},{8,10},{10,8},{12,14},{14,12},{16,18},{18,... | collective-permute-start | bytes 3981320 | tf_op jit(solution)/shard_map/ppermute | solution.py:308
  56.8 5.7 %collective-permute-start.16 = (f32[40,640]{1,0:T(8,128)S(1)}, f32[40,640]{1,0:T(8,128)S(1)}, u32[]{:S(2)}, u32[]{:S(2)}) collective-permute-start(f32[40,640]{1,0:T(8,128)S(1)} %get-tuple-element.52), channel_id=1, source_target_pairs={{0,8},{2,10},{8,16},{10,18},{16,24},{18,26},{24,28},{26,30},{28,20... | collective-permute-start | bytes 307208 | tf_op jit(solution)/shard_map/ppermute | solution.py:310
  58.5 5.8 %collective-permute-start.23 = (f32[40,640]{1,0:T(8,128)S(1)}, f32[40,640]{1,0:T(8,128)S(1)}, u32[]{:S(2)}, u32[]{:S(2)}) collective-permute-start(f32[40,640]{1,0:T(8,128)S(1)} %get-tuple-element.60), channel_id=1, source_target_pairs={{0,4},{2,6},{8,0},{10,2},{16,8},{18,10},{24,16},{26,18},{28,24},{3... | collective-permute-start | bytes 307208 | tf_op jit(solution)/shard_map/ppermute | solution.py:311
  58.9 6.7 %collective-permute-start.20 = (f32[40,640]{1,0:T(8,128)S(1)}, f32[40,640]{1,0:T(8,128)S(1)}, u32[]{:S(2)}, u32[]{:S(2)}) collective-permute-start(f32[40,640]{1,0:T(8,128)S(1)} %get-tuple-element.56), channel_id=1, source_target_pairs={{0,4},{2,6},{8,0},{10,2},{16,8},{18,10},{24,16},{26,18},{28,24},{3... | collective-permute-start | bytes 307208 | tf_op jit(solution)/shard_map/ppermute | solution.py:311
  59.2 6.9 %collective-permute-start.27 = (f32[40,640]{1,0:T(8,128)S(1)}, f32[40,640]{1,0:T(8,128)S(1)}, u32[]{:S(2)}, u32[]{:S(2)}) collective-permute-start(f32[40,640]{1,0:T(8,128)S(1)} %get-tuple-element.64), channel_id=1, source_target_pairs={{0,8},{2,10},{8,16},{10,18},{16,24},{18,26},{24,28},{26,30},{28,20... | collective-permute-start | bytes 307208 | tf_op jit(solution)/shard_map/ppermute | solution.py:310
  62.6 5.2 %collective-permute-start.17 = (f32[40,640]{1,0:T(8,128)S(1)}, f32[40,640]{1,0:T(8,128)S(1)}, u32[]{:S(2)}, u32[]{:S(2)}) collective-permute-start(f32[40,640]{1,0:T(8,128)S(1)} %add.30), channel_id=1, source_target_pairs={{0,8},{2,10},{8,16},{10,18},{16,24},{18,26},{24,28},{26,30},{28,20... | collective-permute-start | bytes 307208 | tf_op jit(solution)/shard_map/ppermute | solution.py:310
  64.2 5.6 %collective-permute-start.24 = (f32[40,640]{1,0:T(8,128)S(1)}, f32[40,640]{1,0:T(8,128)S(1)}, u32[]{:S(2)}, u32[]{:S(2)}) collective-permute-start(f32[40,640]{1,0:T(8,128)S(1)} %add.35), channel_id=1, source_target_pairs={{0,4},{2,6},{8,0},{10,2},{16,8},{18,10},{24,16},{26,18},{28,24},{3... | collective-permute-start | bytes 307208 | tf_op jit(solution)/shard_map/ppermute | solution.py:311
  65.6 5.5 %collective-permute-start.21 = (f32[40,640]{1,0:T(8,128)S(1)}, f32[40,640]{1,0:T(8,128)S(1)}, u32[]{:S(2)}, u32[]{:S(2)}) collective-permute-start(f32[40,640]{1,0:T(8,128)S(1)} %add.33), channel_id=1, source_target_pairs={{0,4},{2,6},{8,0},{10,2},{16,8},{18,10},{24,16},{26,18},{28,24},{3... | collective-permute-start | bytes 307208 | tf_op jit(solution)/shard_map/ppermute | solution.py:311
  66.1 5.5 %collective-permute-start.28 = (f32[40,640]{1,0:T(8,128)S(1)}, f32[40,640]{1,0:T(8,128)S(1)}, u32[]{:S(2)}, u32[]{:S(2)}) collective-permute-start(f32[40,640]{1,0:T(8,128)S(1)} %add.38), channel_id=1, source_target_pairs={{0,8},{2,10},{8,16},{10,18},{16,24},{18,26},{24,28},{26,30},{28,20... | collective-permute-start | bytes 307208 | tf_op jit(solution)/shard_map/ppermute | solution.py:310
  67.8 5.5 %collective-permute-start.18 = (f32[40,640]{1,0:T(8,128)S(1)}, f32[40,640]{1,0:T(8,128)S(1)}, u32[]{:S(2)}, u32[]{:S(2)}) collective-permute-start(f32[40,640]{1,0:T(8,128)S(1)} %add.31), channel_id=1, source_target_pairs={{0,8},{2,10},{8,16},{10,18},{16,24},{18,26},{24,28},{26,30},{28,20... | collective-permute-start | bytes 307208 | tf_op jit(solution)/shard_map/ppermute | solution.py:310
  69.8 5.5 %collective-permute-start.25 = (f32[40,640]{1,0:T(8,128)S(1)}, f32[40,640]{1,0:T(8,128)S(1)}, u32[]{:S(2)}, u32[]{:S(2)}) collective-permute-start(f32[40,640]{1,0:T(8,128)S(1)} %add.36), channel_id=1, source_target_pairs={{0,4},{2,6},{8,0},{10,2},{16,8},{18,10},{24,16},{26,18},{28,24},{3... | collective-permute-start | bytes 307208 | tf_op jit(solution)/shard_map/ppermute | solution.py:311
  71.2 5.3 %collective-permute-start.22 = (f32[40,640]{1,0:T(8,128)S(1)}, f32[40,640]{1,0:T(8,128)S(1)}, u32[]{:S(2)}, u32[]{:S(2)}) collective-permute-start(f32[40,640]{1,0:T(8,128)S(1)} %add.34), channel_id=1, source_target_pairs={{0,4},{2,6},{8,0},{10,2},{16,8},{18,10},{24,16},{26,18},{28,24},{3... | collective-permute-start | bytes 307208 | tf_op jit(solution)/shard_map/ppermute | solution.py:311
  71.7 4.8 %collective-permute-start.29 = (f32[40,640]{1,0:T(8,128)S(1)}, f32[40,640]{1,0:T(8,128)S(1)}, u32[]{:S(2)}, u32[]{:S(2)}) collective-permute-start(f32[40,640]{1,0:T(8,128)S(1)} %add.39), channel_id=1, source_target_pairs={{0,8},{2,10},{8,16},{10,18},{16,24},{18,26},{24,28},{26,30},{28,20... | collective-permute-start | bytes 307208 | tf_op jit(solution)/shard_map/ppermute | solution.py:310
  73.3 4.7 %collective-permute-start.19 = (f32[40,640]{1,0:T(8,128)S(1)}, f32[40,640]{1,0:T(8,128)S(1)}, u32[]{:S(2)}, u32[]{:S(2)}) collective-permute-start(f32[40,640]{1,0:T(8,128)S(1)} %add.32), channel_id=1, source_target_pairs={{0,8},{2,10},{8,16},{10,18},{16,24},{18,26},{24,28},{26,30},{28,20... | collective-permute-start | bytes 307208 | tf_op jit(solution)/shard_map/ppermute | solution.py:310
  80.1 5.2 %collective-permute-start.32 = (f32[40,640]{1,0:T(8,128)S(1)}, f32[40,640]{1,0:T(8,128)S(1)}, u32[]{:S(2)}, u32[]{:S(2)}) collective-permute-start(f32[40,640]{1,0:T(8,128)S(1)} %get-tuple-element.67), channel_id=1, source_target_pairs={{0,3},{1,2},{2,1},{3,0},{4,7},{5,6},{6,5},{7,4},{8,11},{9,10},{10,... | collective-permute-start | bytes 307208 | tf_op jit(solution)/shard_map/ppermute | solution.py:399
  80.2 5.1 %collective-permute-start.30 = (f32[40,640]{1,0:T(8,128)S(1)}, f32[40,640]{1,0:T(8,128)S(1)}, u32[]{:S(2)}, u32[]{:S(2)}) collective-permute-start(f32[40,640]{1,0:T(8,128)S(1)} %get-tuple-element.67), channel_id=1, source_target_pairs={{0,2},{2,0},{4,6},{6,4},{8,10},{10,8},{12,14},{14,12},{16,18},{18,... | collective-permute-start | bytes 307208 | tf_op jit(solution)/shard_map/ppermute | solution.py:308
  81.8 5.7 %collective-permute-start.31 = (f32[40,640]{1,0:T(8,128)S(1)}, f32[40,640]{1,0:T(8,128)S(1)}, u32[]{:S(2)}, u32[]{:S(2)}) collective-permute-start(f32[40,640]{1,0:T(8,128)S(1)} %get-tuple-element.68.keep), channel_id=1, source_target_pairs={{0,1},{1,0},{2,3},{3,2},{4,5},{5,4},{6,7},{7,6},{8,9},{9,8},{10,11... | collective-permute-start | bytes 307208 | tf_op jit(solution)/shard_map/ppermute | solution.py:398
  (8 other events, 35.4 us)

commit v6 on v5

--- a/solution.py
+++ b/solution.py
@@ -157,24 +157,26 @@
         for k, block in zip(steps[i], blocks):
             w[pl.ds(places[k], block.shape[0]), i * cols : (i + 1) * cols] = block[...]
 
-    x_at, e_at, g_at = act_rows(mine.shape[0] - 2 * TOK)
+    _, e_at, g_at = act_rows(mine.shape[0] - 2 * TOK)
     rows_of = []
+
+    wq_t, wo_t = w[:, :width].T, w[:, 3 * width :].T
 
     def project(clip):
         acts = (mine, other)[clip]
-        q = (dot(acts[x_at, :], w[:, :width]) * 0.125).astype(BF)
+        qt = (dot(wq_t, (t0, t1)[clip][...]) * 0.125).astype(BF)
         kv = dot(acts[e_at, :], w[:, width : 3 * width]).astype(BF)
-        g = dot(acts[g_at, :], w[:, 3 * width :]).astype(BF)
+        gt = dot(wo_t, acts[g_at, :], ROWS).astype(BF)
         k, v = kv[:, :width], kv[:, width:]
-        rows_of.append((q, k, v, g, k.T, v.T, g.T))
+        rows_of.append((qt, k, v, gt, k.T, v.T))
 
     def begin(clip, h, tokens):
-        q, k, v, g, _, _, _ = rows_of[clip]
+        qt, k, v, gt, _, _ = rows_of[clip]
         cols = slice(h * HEAD_DIM, (h + 1) * HEAD_DIM)
-        return dot(k[:, cols], q[tokens, cols], ROWS), dot(v[:, cols], g[tokens, cols], ROWS)
+        return dot(k[:, cols], qt[cols, tokens]), dot(v[:, cols], gt[cols, tokens])
 
     def finish(clip, h, tokens, scores, grad_attention):
-        _, _, _, _, kt, vt, gt = rows_of[clip]
+        _, _, _, gt, kt, vt = rows_of[clip]
         cols = slice(h * HEAD_DIM, (h + 1) * HEAD_DIM)
         e = jnp.exp(scores - jnp.max(scores, axis=0, keepdims=True))
         attention = (e * (1.0 / jnp.sum(e, axis=0, keepdims=True))).astype(BF)

time: 88.9 us -> 87.9 us (0.989)
  Pallas kernels: 23 us -> 21.9 us
    pallas_call x1, Pallas kernels: 13.2 us -> 12.1 us  [heads(): pl.pallas_call(functools.partial(head_kernel, chips, steps, pieces), out_...]
where the time goes in v6:
time: 87.9 us; the launch traced here: 87.7 us
  starting transfers between devices  33.3 us (38%)
  waiting for transfers between devices  28.8 us (33%)
  Pallas kernels  21.9 us (25%)
  local copies, waits for them, and re-layouts  2.03 us (2%)
  between operations  1.45 us (2%)
    ppermute x14, starting transfers between devices, per_device(): right = lambda a: lax.ppermute(a, 'dp', ring_pairs(chips, 1))  25.6 us
    ppermute x14, waiting for transfers between devices, per_device(): left = lambda a: lax.ppermute(a, 'dp', ring_pairs(chips, -1))  16.6 us
    pallas_call x1, Pallas kernels, heads(): pl.pallas_call(functools.partial(head_kernel, chips, steps, pieces), out_...  12.1 us
    ppermute x14, waiting for transfers between devices, per_device(): right = lambda a: lax.ppermute(a, 'dp', ring_pairs(chips, 1))  9.3 us
    ppermute x14, starting transfers between devices, per_device(): left = lambda a: lax.ppermute(a, 'dp', ring_pairs(chips, -1))  4.83 us
    pallas_call x1, Pallas kernels, per_device(): pl.pallas_call(stage_kernel, out_shape=jax.ShapeDtypeStruct((2 * TOK + fr...  3.33 us
    pallas_call x1, Pallas kernels, per_device(): pl.pallas_call(out_kernel, out_shape=jax.ShapeDtypeStruct((TOK, depth), B...  2.37 us
    ppermute x4, starting transfers between devices, per_device(): swap = lambda a: lax.ppermute(a, 'dp', mates)  2.33 us
  transfers between devices with their start and end apart: 34, of which 17 were waited for; matrix products, arithmetic and copies ran while one was open for 0% of the time, Pallas kernels for 7%

profile of v6, /device:TPU:0, one launch (start us, length us, event | category | flops | bytes accessed | tf_op | source)
XLA Modules:
  0.0 87.7 jit_solution(3909307867643350828)
XLA Ops:
  0.6 2.0 %shard_map.137 = (bf16[80,1280]{1,0:T(8,128)(2,1)}, bf16[80,1280]{1,0:T(8,128)(2,1)}) custom-call(s32[1]{0:T(128)} %bitcast.me.refs_0_, f32[80,640]{1,0:T(8,128)} %master.1, bf16[80,640]{1,0:T(8,128)(2,1)} %k.1, bf16[80,640]{1,0:T(8,128)(2,1)} %v.1, bf16[80,640]{1,0:T(8,128)(2,1)} %bitcast.2), custom_call_target="tpu_custom_call" | custom-call | tf_op jit(solution)/shard_map/pallas_call | solution.py:317
  3.9 3.3 %shard_map.138.mine.refs_17_ = bf16[1408,1280]{1,0:T(8,128)(2,1)} custom-call(s32[1]{0:T(128)S(6)} %copy.15.length, bf16[448,1280]{1,0:T(8,128)(2,1)} %x.1, bf16[512,1280]{1,0:T(8,128)(2,1)} %e.1, bf16[448,1280]{1,0:T(8,128)(2,1)} %g.1, bf16[80,1280]{1,0:T(8,128)(2,1)} %get-tuple-element.42._.keep), custom_call_target="tpu_custom_call" | custom-call | tf_op jit(solution)/shard_map/pallas_call | solution.py:328
  7.4 3.0 %collective-permute-start.1 = (bf16[160,640]{1,0:T(8,128)(2,1)S(1)}, bf16[160,640]{1,0:T(8,128)(2,1)S(1)}, u32[]{:S(2)}, u32[]{:S(2)}) collective-permute-start(bf16[160,640]{1,0:T(8,128)(2,1)S(1)} %get-tuple-element.46.refs_1_), channel_id=1, source_target_pairs={{0,8},{2,10},{8,16},{10,18},{16,24},{18,26},{24,28},{26,30},{28,20... | collective-permute-start | bytes 614408 | tf_op jit(solution)/shard_map/ppermute | solution.py:312
  10.4 1.9 %collective-permute-start.2 = (bf16[160,640]{1,0:T(8,128)(2,1)S(1)}, bf16[160,640]{1,0:T(8,128)(2,1)S(1)}, u32[]{:S(2)}, u32[]{:S(2)}) collective-permute-start(bf16[160,640]{1,0:T(8,128)(2,1)S(1)} %get-tuple-element.46.refs_1_), channel_id=1, source_target_pairs={{0,4},{2,6},{8,0},{10,2},{16,8},{18,10},{24,16},{26,18},{28,24},{3... | collective-permute-start | bytes 614408 | tf_op jit(solution)/shard_map/ppermute | solution.py:313
  12.5 3.7 %collective-permute-done.1.refs_2_ = bf16[160,640]{1,0:T(8,128)(2,1)S(1)} collective-permute-done((bf16[160,640]{1,0:T(8,128)(2,1)S(1)}, bf16[160,640]{1,0:T(8,128)(2,1)S(1)}, u32[]{:S(2)}, u32[]{:S(2)}) %collective-permute-start.1) | collective-permute-done | bytes 204832 | tf_op jit(solution)/shard_map/ppermute | solution.py:312
  16.2 2.1 %collective-permute-start.3 = (bf16[160,640]{1,0:T(8,128)(2,1)S(1)}, bf16[160,640]{1,0:T(8,128)(2,1)S(1)}, u32[]{:S(2)}, u32[]{:S(2)}) collective-permute-start(bf16[160,640]{1,0:T(8,128)(2,1)S(1)} %collective-permute-done.1.refs_2_), channel_id=1, source_target_pairs={{0,8},{2,10},{8,16},{10,18},{16,24},{18,26},{24,28},{26,30},{28,20... | collective-permute-start | bytes 614408 | tf_op jit(solution)/shard_map/ppermute | solution.py:312
  18.4 4.4 %collective-permute-done.2.refs_3_ = bf16[160,640]{1,0:T(8,128)(2,1)S(1)} collective-permute-done((bf16[160,640]{1,0:T(8,128)(2,1)S(1)}, bf16[160,640]{1,0:T(8,128)(2,1)S(1)}, u32[]{:S(2)}, u32[]{:S(2)}) %collective-permute-start.2) | collective-permute-done | bytes 204832 | tf_op jit(solution)/shard_map/ppermute | solution.py:313
  22.8 2.0 %collective-permute-start.10 = (bf16[160,640]{1,0:T(8,128)(2,1)S(1)}, bf16[160,640]{1,0:T(8,128)(2,1)S(1)}, u32[]{:S(2)}, u32[]{:S(2)}) collective-permute-start(bf16[160,640]{1,0:T(8,128)(2,1)S(1)} %collective-permute-done.8.refs_10_), channel_id=1, source_target_pairs={{0,8},{2,10},{8,16},{10,18},{16,24},{18,26},{24,28},{26,30},{28,20... | collective-permute-start | bytes 614408 | tf_op jit(solution)/shard_map/ppermute | solution.py:312
  25.0 2.1 %collective-permute-start.5 = (bf16[160,640]{1,0:T(8,128)(2,1)S(1)}, bf16[160,640]{1,0:T(8,128)(2,1)S(1)}, u32[]{:S(2)}, u32[]{:S(2)}) collective-permute-start(bf16[160,640]{1,0:T(8,128)(2,1)S(1)} %collective-permute-done.3.refs_4_), channel_id=1, source_target_pairs={{0,8},{2,10},{8,16},{10,18},{16,24},{18,26},{24,28},{26,30},{28,20... | collective-permute-start | bytes 614408 | tf_op jit(solution)/shard_map/ppermute | solution.py:312
  27.2 4.4 %collective-permute-done.4.refs_5_ = bf16[160,640]{1,0:T(8,128)(2,1)S(1)} collective-permute-done((bf16[160,640]{1,0:T(8,128)(2,1)S(1)}, bf16[160,640]{1,0:T(8,128)(2,1)S(1)}, u32[]{:S(2)}, u32[]{:S(2)}) %collective-permute-start.4) | collective-permute-done | bytes 204832 | tf_op jit(solution)/shard_map/ppermute | solution.py:313
  31.6 2.0 %collective-permute-start.12 = (bf16[160,640]{1,0:T(8,128)(2,1)S(1)}, bf16[160,640]{1,0:T(8,128)(2,1)S(1)}, u32[]{:S(2)}, u32[]{:S(2)}) collective-permute-start(bf16[160,640]{1,0:T(8,128)(2,1)S(1)} %collective-permute-done.10.refs_12_), channel_id=1, source_target_pairs={{0,8},{2,10},{8,16},{10,18},{16,24},{18,26},{24,28},{26,30},{28,20... | collective-permute-start | bytes 614408 | tf_op jit(solution)/shard_map/ppermute | solution.py:312
  34.2 2.2 %collective-permute-start.7 = (bf16[160,640]{1,0:T(8,128)(2,1)S(1)}, bf16[160,640]{1,0:T(8,128)(2,1)S(1)}, u32[]{:S(2)}, u32[]{:S(2)}) collective-permute-start(bf16[160,640]{1,0:T(8,128)(2,1)S(1)} %collective-permute-done.5.refs_6_), channel_id=1, source_target_pairs={{0,8},{2,10},{8,16},{10,18},{16,24},{18,26},{24,28},{26,30},{28,20... | collective-permute-start | bytes 614408 | tf_op jit(solution)/shard_map/ppermute | solution.py:312
  36.4 2.0 %copy-done = bf16[1408,1280]{1,0:T(8,128)(2,1)S(1)} copy-done((bf16[1408,1280]{1,0:T(8,128)(2,1)S(1)}, bf16[1408,1280]{1,0:T(8,128)(2,1)}, u32[]{:S(2)}) %copy-start) | copy-done | bytes 3604504
  39.2 1.2 %collective-permute-done.6.refs_7_ = bf16[160,640]{1,0:T(8,128)(2,1)S(1)} collective-permute-done((bf16[160,640]{1,0:T(8,128)(2,1)S(1)}, bf16[160,640]{1,0:T(8,128)(2,1)S(1)}, u32[]{:S(2)}, u32[]{:S(2)}) %collective-permute-start.6) | collective-permute-done | bytes 204832 | tf_op jit(solution)/shard_map/ppermute | solution.py:313
  40.3 1.6 %collective-permute-done.7.refs_8_ = bf16[160,640]{1,0:T(8,128)(2,1)S(1)} collective-permute-done((bf16[160,640]{1,0:T(8,128)(2,1)S(1)}, bf16[160,640]{1,0:T(8,128)(2,1)S(1)}, u32[]{:S(2)}, u32[]{:S(2)}) %collective-permute-start.7) | collective-permute-done | bytes 204832 | tf_op jit(solution)/shard_map/ppermute | solution.py:312
  42.0 1.5 %collective-permute-done.14.refs_16_ = bf16[160,640]{1,0:T(8,128)(2,1)S(1)} collective-permute-done((bf16[160,640]{1,0:T(8,128)(2,1)S(1)}, bf16[160,640]{1,0:T(8,128)(2,1)S(1)}, u32[]{:S(2)}, u32[]{:S(2)}) %collective-permute-start.14) | collective-permute-done | bytes 204832 | tf_op jit(solution)/shard_map/ppermute | solution.py:313
  43.5 12.1 %shard_map.141 = (bf16[1728,384]{1,0:T(8,128)(2,1)S(1)}, bf16[448,320]{1,0:T(8,128)(2,1)S(1)}, f32[40,640]{1,0:T(8,128)S(1)}, f32[40,640]{1,0:T(8,128)S(1)}, f32...) custom-call(s32[1]{0:T(128)} %bitcast.me.refs_0_, ...), custom_call_target="tpu_custom_call" | custom-call | flops 8999999488 | bytes 15000000 | tf_op jit(solution)/shard_map/pallas_call | solution.py:227
  55.8 1.6 %collective-permute-start.16 = (f32[40,640]{1,0:T(8,128)S(1)}, f32[40,640]{1,0:T(8,128)S(1)}, u32[]{:S(2)}, u32[]{:S(2)}) collective-permute-start(f32[40,640]{1,0:T(8,128)S(1)} %get-tuple-element.52), channel_id=1, source_target_pairs={{0,8},{2,10},{8,16},{10,18},{16,24},{18,26},{24,28},{26,30},{28,20... | collective-permute-start | bytes 307208 | tf_op jit(solution)/shard_map/ppermute | solution.py:312
  58.1 1.7 %collective-permute-start.27 = (f32[40,640]{1,0:T(8,128)S(1)}, f32[40,640]{1,0:T(8,128)S(1)}, u32[]{:S(2)}, u32[]{:S(2)}) collective-permute-start(f32[40,640]{1,0:T(8,128)S(1)} %get-tuple-element.64), channel_id=1, source_target_pairs={{0,8},{2,10},{8,16},{10,18},{16,24},{18,26},{24,28},{26,30},{28,20... | collective-permute-start | bytes 307208 | tf_op jit(solution)/shard_map/ppermute | solution.py:312
  59.9 1.6 %collective-permute-done.16 = f32[40,640]{1,0:T(8,128)S(1)} collective-permute-done((f32[40,640]{1,0:T(8,128)S(1)}, f32[40,640]{1,0:T(8,128)S(1)}, u32[]{:S(2)}, u32[]{:S(2)}) %collective-permute-start.16) | collective-permute-done | bytes 102432 | tf_op jit(solution)/shard_map/ppermute | solution.py:312
  61.5 1.6 %collective-permute-start.17 = (f32[40,640]{1,0:T(8,128)S(1)}, f32[40,640]{1,0:T(8,128)S(1)}, u32[]{:S(2)}, u32[]{:S(2)}) collective-permute-start(f32[40,640]{1,0:T(8,128)S(1)} %add.30), channel_id=1, source_target_pairs={{0,8},{2,10},{8,16},{10,18},{16,24},{18,26},{24,28},{26,30},{28,20... | collective-permute-start | bytes 307208 | tf_op jit(solution)/shard_map/ppermute | solution.py:312
  65.1 1.6 %collective-permute-start.28 = (f32[40,640]{1,0:T(8,128)S(1)}, f32[40,640]{1,0:T(8,128)S(1)}, u32[]{:S(2)}, u32[]{:S(2)}) collective-permute-start(f32[40,640]{1,0:T(8,128)S(1)} %add.38), channel_id=1, source_target_pairs={{0,8},{2,10},{8,16},{10,18},{16,24},{18,26},{24,28},{26,30},{28,20... | collective-permute-start | bytes 307208 | tf_op jit(solution)/shard_map/ppermute | solution.py:312
  66.7 1.6 %collective-permute-start.18 = (f32[40,640]{1,0:T(8,128)S(1)}, f32[40,640]{1,0:T(8,128)S(1)}, u32[]{:S(2)}, u32[]{:S(2)}) collective-permute-start(f32[40,640]{1,0:T(8,128)S(1)} %add.31), channel_id=1, source_target_pairs={{0,8},{2,10},{8,16},{10,18},{16,24},{18,26},{24,28},{26,30},{28,20... | collective-permute-start | bytes 307208 | tf_op jit(solution)/shard_map/ppermute | solution.py:312
  70.6 1.6 %collective-permute-start.29 = (f32[40,640]{1,0:T(8,128)S(1)}, f32[40,640]{1,0:T(8,128)S(1)}, u32[]{:S(2)}, u32[]{:S(2)}) collective-permute-start(f32[40,640]{1,0:T(8,128)S(1)} %add.39), channel_id=1, source_target_pairs={{0,8},{2,10},{8,16},{10,18},{16,24},{18,26},{24,28},{26,30},{28,20... | collective-permute-start | bytes 307208 | tf_op jit(solution)/shard_map/ppermute | solution.py:312
  72.2 2.0 %collective-permute-start.19 = (f32[40,640]{1,0:T(8,128)S(1)}, f32[40,640]{1,0:T(8,128)S(1)}, u32[]{:S(2)}, u32[]{:S(2)}) collective-permute-start(f32[40,640]{1,0:T(8,128)S(1)} %add.32), channel_id=1, source_target_pairs={{0,8},{2,10},{8,16},{10,18},{16,24},{18,26},{24,28},{26,30},{28,20... | collective-permute-start | bytes 307208 | tf_op jit(solution)/shard_map/ppermute | solution.py:312
  74.4 1.0 %collective-permute-done.22.refs_2_ = f32[40,640]{1,0:T(8,128)S(1)} collective-permute-done((f32[40,640]{1,0:T(8,128)S(1)}, f32[40,640]{1,0:T(8,128)S(1)}, u32[]{:S(2)}, u32[]{:S(2)}) %collective-permute-start.22) | collective-permute-done | bytes 102432 | tf_op jit(solution)/shard_map/ppermute | solution.py:313
  75.4 1.6 %collective-permute-done.19.refs_1_ = f32[40,640]{1,0:T(8,128)S(1)} collective-permute-done((f32[40,640]{1,0:T(8,128)S(1)}, f32[40,640]{1,0:T(8,128)S(1)}, u32[]{:S(2)}, u32[]{:S(2)}) %collective-permute-start.19) | collective-permute-done | bytes 102432 | tf_op jit(solution)/shard_map/ppermute | solution.py:312
  76.9 2.0 %collective-permute-done.26.refs_4_ = f32[40,640]{1,0:T(8,128)S(1)} collective-permute-done((f32[40,640]{1,0:T(8,128)S(1)}, f32[40,640]{1,0:T(8,128)S(1)}, u32[]{:S(2)}, u32[]{:S(2)}) %collective-permute-start.26) | collective-permute-done | bytes 102432 | tf_op jit(solution)/shard_map/ppermute | solution.py:313
  79.1 1.6 %collective-permute-start.30 = (f32[40,640]{1,0:T(8,128)S(1)}, f32[40,640]{1,0:T(8,128)S(1)}, u32[]{:S(2)}, u32[]{:S(2)}) collective-permute-start(f32[40,640]{1,0:T(8,128)S(1)} %get-tuple-element.67), channel_id=1, source_target_pairs={{0,2},{2,0},{4,6},{6,4},{8,10},{10,8},{12,14},{14,12},{16,18},{18,... | collective-permute-start | bytes 307208 | tf_op jit(solution)/shard_map/ppermute | solution.py:310
  81.2 2.4 %shard_map.143 = bf16[448,1280]{1,0:T(8,128)(2,1)} custom-call(bf16[448,320]{1,0:T(8,128)(2,1)S(1)} %get-tuple-element.69.ctx_own, bf16[1728,384]{1,0:T(8,128)(2,1)S(1)} %get-tuple-element.70.share, bf16[1728,384]{1,0:T(8,128)(2,1)S(1)} %collective-permute-done.33.got), custom_call_target="tpu_custom_call" | custom-call | flops 734003200 | bytes 4000000 | tf_op jit(solution)/shard_map/pallas_call | solution.py:416
  84.2 2.3 %collective-permute-done.31.keep_y = f32[40,640]{1,0:T(8,128)S(1)} collective-permute-done((f32[40,640]{1,0:T(8,128)S(1)}, f32[40,640]{1,0:T(8,128)S(1)}, u32[]{:S(2)}, u32[]{:S(2)}) %collective-permute-start.31) | collective-permute-done | bytes 102432 | tf_op jit(solution)/shard_map/ppermute | solution.py:400
  86.5 1.2 %shard_map.144 = (f32[80,640]{1,0:T(8,128)}, f32[80,640]{1,0:T(8,128)}, f32[80,640]{1,0:T(8,128)}, f32[80,640]{1,0:T(8,128)}) custom-call(s32[1]{0:T(128)} %bitcast.me.refs_0_, f32[40,640]{1,0:T(8,128)S(1)} %get-tuple-element.68.keep, f32[40,640]{1,0:T(8,128)S(1)} %collective-permute-done.31.keep_y, f32[40,640]{1,0:T(8,128)S(1)} %collective-permute-done.30.got, ...), custom_call_target="tpu_custom_call" | custom-call | tf_op jit(solution)/shard_map/pallas_call | solution.py:428
  (66 shorter events, 8.8 us)
Async XLA Ops:
  7.3 29.1 %collective-permute-start.15 = (bf16[1408,1280]{1,0:T(8,128)(2,1)}, bf16[1408,1280]{1,0:T(8,128)(2,1)S(1)}, u32[]{:S(2)}, u32[]{:S(2)}) collective-permute-start(bf16[1408,1280]{1,0:T(8,128)(2,1)} %shard_map.138.mine.refs_17_), channel_id=1, source_target_pairs={{0,2},{2,0},{4,6},{6,4},{8,10},{10,8},{12,14},{14,12},{16,18},{18,... | collective-permute-start | bytes 10813448 | tf_op jit(solution)/shard_map/ppermute | solution.py:310
  7.4 8.8 %collective-permute-start.1 = (bf16[160,640]{1,0:T(8,128)(2,1)S(1)}, bf16[160,640]{1,0:T(8,128)(2,1)S(1)}, u32[]{:S(2)}, u32[]{:S(2)}) collective-permute-start(bf16[160,640]{1,0:T(8,128)(2,1)S(1)} %get-tuple-element.46.refs_1_), channel_id=1, source_target_pairs={{0,8},{2,10},{8,16},{10,18},{16,24},{18,26},{24,28},{26,30},{28,20... | collective-permute-start | bytes 614408 | tf_op jit(solution)/shard_map/ppermute | solution.py:312
  10.4 8.0 %collective-permute-start.9 = (bf16[160,640]{1,0:T(8,128)(2,1)S(1)}, bf16[160,640]{1,0:T(8,128)(2,1)S(1)}, u32[]{:S(2)}, u32[]{:S(2)}) collective-permute-start(bf16[160,640]{1,0:T(8,128)(2,1)S(1)} %get-tuple-element.47.refs_9_), channel_id=1, source_target_pairs={{0,4},{2,6},{8,0},{10,2},{16,8},{18,10},{24,16},{26,18},{28,24},{3... | collective-permute-start | bytes 614408 | tf_op jit(solution)/shard_map/ppermute | solution.py:313
  10.4 12.4 %collective-permute-start.2 = (bf16[160,640]{1,0:T(8,128)(2,1)S(1)}, bf16[160,640]{1,0:T(8,128)(2,1)S(1)}, u32[]{:S(2)}, u32[]{:S(2)}) collective-permute-start(bf16[160,640]{1,0:T(8,128)(2,1)S(1)} %get-tuple-element.46.refs_1_), channel_id=1, source_target_pairs={{0,4},{2,6},{8,0},{10,2},{16,8},{18,10},{24,16},{26,18},{28,24},{3... | collective-permute-start | bytes 614408 | tf_op jit(solution)/shard_map/ppermute | solution.py:313
  12.4 10.4 %collective-permute-start.8 = (bf16[160,640]{1,0:T(8,128)(2,1)S(1)}, bf16[160,640]{1,0:T(8,128)(2,1)S(1)}, u32[]{:S(2)}, u32[]{:S(2)}) collective-permute-start(bf16[160,640]{1,0:T(8,128)(2,1)S(1)} %get-tuple-element.47.refs_9_), channel_id=1, source_target_pairs={{0,8},{2,10},{8,16},{10,18},{16,24},{18,26},{24,28},{26,30},{28,20... | collective-permute-start | bytes 614408 | tf_op jit(solution)/shard_map/ppermute | solution.py:312
  16.2 8.8 %collective-permute-start.3 = (bf16[160,640]{1,0:T(8,128)(2,1)S(1)}, bf16[160,640]{1,0:T(8,128)(2,1)S(1)}, u32[]{:S(2)}, u32[]{:S(2)}) collective-permute-start(bf16[160,640]{1,0:T(8,128)(2,1)S(1)} %collective-permute-done.1.refs_2_), channel_id=1, source_target_pairs={{0,8},{2,10},{8,16},{10,18},{16,24},{18,26},{24,28},{26,30},{28,20... | collective-permute-start | bytes 614408 | tf_op jit(solution)/shard_map/ppermute | solution.py:312
  18.4 8.8 %collective-permute-start.11 = (bf16[160,640]{1,0:T(8,128)(2,1)S(1)}, bf16[160,640]{1,0:T(8,128)(2,1)S(1)}, u32[]{:S(2)}, u32[]{:S(2)}) collective-permute-start(bf16[160,640]{1,0:T(8,128)(2,1)S(1)} %collective-permute-done.9.refs_11_), channel_id=1, source_target_pairs={{0,4},{2,6},{8,0},{10,2},{16,8},{18,10},{24,16},{26,18},{28,24},{3... | collective-permute-start | bytes 614408 | tf_op jit(solution)/shard_map/ppermute | solution.py:313
  22.8 8.8 %collective-permute-start.4 = (bf16[160,640]{1,0:T(8,128)(2,1)S(1)}, bf16[160,640]{1,0:T(8,128)(2,1)S(1)}, u32[]{:S(2)}, u32[]{:S(2)}) collective-permute-start(bf16[160,640]{1,0:T(8,128)(2,1)S(1)} %collective-permute-done.2.refs_3_), channel_id=1, source_target_pairs={{0,4},{2,6},{8,0},{10,2},{16,8},{18,10},{24,16},{26,18},{28,24},{3... | collective-permute-start | bytes 614408 | tf_op jit(solution)/shard_map/ppermute | solution.py:313
  22.8 8.8 %collective-permute-start.10 = (bf16[160,640]{1,0:T(8,128)(2,1)S(1)}, bf16[160,640]{1,0:T(8,128)(2,1)S(1)}, u32[]{:S(2)}, u32[]{:S(2)}) collective-permute-start(bf16[160,640]{1,0:T(8,128)(2,1)S(1)} %collective-permute-done.8.refs_10_), channel_id=1, source_target_pairs={{0,8},{2,10},{8,16},{10,18},{16,24},{18,26},{24,28},{26,30},{28,20... | collective-permute-start | bytes 614408 | tf_op jit(solution)/shard_map/ppermute | solution.py:312
  25.0 9.2 %collective-permute-start.5 = (bf16[160,640]{1,0:T(8,128)(2,1)S(1)}, bf16[160,640]{1,0:T(8,128)(2,1)S(1)}, u32[]{:S(2)}, u32[]{:S(2)}) collective-permute-start(bf16[160,640]{1,0:T(8,128)(2,1)S(1)} %collective-permute-done.3.refs_4_), channel_id=1, source_target_pairs={{0,8},{2,10},{8,16},{10,18},{16,24},{18,26},{24,28},{26,30},{28,20... | collective-permute-start | bytes 614408 | tf_op jit(solution)/shard_map/ppermute | solution.py:312
  27.2 9.2 %collective-permute-start.13 = (bf16[160,640]{1,0:T(8,128)(2,1)S(1)}, bf16[160,640]{1,0:T(8,128)(2,1)S(1)}, u32[]{:S(2)}, u32[]{:S(2)}) collective-permute-start(bf16[160,640]{1,0:T(8,128)(2,1)S(1)} %collective-permute-done.11.refs_13_), channel_id=1, source_target_pairs={{0,4},{2,6},{8,0},{10,2},{16,8},{18,10},{24,16},{26,18},{28,24},{3... | collective-permute-start | bytes 614408 | tf_op jit(solution)/shard_map/ppermute | solution.py:313
  31.6 8.8 %collective-permute-start.6 = (bf16[160,640]{1,0:T(8,128)(2,1)S(1)}, bf16[160,640]{1,0:T(8,128)(2,1)S(1)}, u32[]{:S(2)}, u32[]{:S(2)}) collective-permute-start(bf16[160,640]{1,0:T(8,128)(2,1)S(1)} %collective-permute-done.4.refs_5_), channel_id=1, source_target_pairs={{0,4},{2,6},{8,0},{10,2},{16,8},{18,10},{24,16},{26,18},{28,24},{3... | collective-permute-start | bytes 614408 | tf_op jit(solution)/shard_map/ppermute | solution.py:313
  31.6 8.8 %collective-permute-start.12 = (bf16[160,640]{1,0:T(8,128)(2,1)S(1)}, bf16[160,640]{1,0:T(8,128)(2,1)S(1)}, u32[]{:S(2)}, u32[]{:S(2)}) collective-permute-start(bf16[160,640]{1,0:T(8,128)(2,1)S(1)} %collective-permute-done.10.refs_12_), channel_id=1, source_target_pairs={{0,8},{2,10},{8,16},{10,18},{16,24},{18,26},{24,28},{26,30},{28,20... | collective-permute-start | bytes 614408 | tf_op jit(solution)/shard_map/ppermute | solution.py:312
  34.2 7.8 %collective-permute-start.7 = (bf16[160,640]{1,0:T(8,128)(2,1)S(1)}, bf16[160,640]{1,0:T(8,128)(2,1)S(1)}, u32[]{:S(2)}, u32[]{:S(2)}) collective-permute-start(bf16[160,640]{1,0:T(8,128)(2,1)S(1)} %collective-permute-done.5.refs_6_), channel_id=1, source_target_pairs={{0,8},{2,10},{8,16},{10,18},{16,24},{18,26},{24,28},{26,30},{28,20... | collective-permute-start | bytes 614408 | tf_op jit(solution)/shard_map/ppermute | solution.py:312
  36.4 7.1 %collective-permute-start.14 = (bf16[160,640]{1,0:T(8,128)(2,1)S(1)}, bf16[160,640]{1,0:T(8,128)(2,1)S(1)}, u32[]{:S(2)}, u32[]{:S(2)}) collective-permute-start(bf16[160,640]{1,0:T(8,128)(2,1)S(1)} %collective-permute-done.13.refs_15_), channel_id=1, source_target_pairs={{0,4},{2,6},{8,0},{10,2},{16,8},{18,10},{24,16},{26,18},{28,24},{3... | collective-permute-start | bytes 614408 | tf_op jit(solution)/shard_map/ppermute | solution.py:313
  55.7 25.6 %collective-permute-start.33 = (bf16[1728,384]{1,0:T(8,128)(2,1)S(1)}, bf16[1728,384]{1,0:T(8,128)(2,1)S(1)}, u32[]{:S(2)}, u32[]{:S(2)}) collective-permute-start(bf16[1728,384]{1,0:T(8,128)(2,1)S(1)} %get-tuple-element.70.share), channel_id=1, source_target_pairs={{0,2},{2,0},{4,6},{6,4},{8,10},{10,8},{12,14},{14,12},{16,18},{18,... | collective-permute-start | bytes 3981320 | tf_op jit(solution)/shard_map/ppermute | solution.py:310
  55.8 5.7 %collective-permute-start.16 = (f32[40,640]{1,0:T(8,128)S(1)}, f32[40,640]{1,0:T(8,128)S(1)}, u32[]{:S(2)}, u32[]{:S(2)}) collective-permute-start(f32[40,640]{1,0:T(8,128)S(1)} %get-tuple-element.52), channel_id=1, source_target_pairs={{0,8},{2,10},{8,16},{10,18},{16,24},{18,26},{24,28},{26,30},{28,20... | collective-permute-start | bytes 307208 | tf_op jit(solution)/shard_map/ppermute | solution.py:312
  57.4 5.8 %collective-permute-start.23 = (f32[40,640]{1,0:T(8,128)S(1)}, f32[40,640]{1,0:T(8,128)S(1)}, u32[]{:S(2)}, u32[]{:S(2)}) collective-permute-start(f32[40,640]{1,0:T(8,128)S(1)} %get-tuple-element.60), channel_id=1, source_target_pairs={{0,4},{2,6},{8,0},{10,2},{16,8},{18,10},{24,16},{26,18},{28,24},{3... | collective-permute-start | bytes 307208 | tf_op jit(solution)/shard_map/ppermute | solution.py:313
  57.8 6.7 %collective-permute-start.20 = (f32[40,640]{1,0:T(8,128)S(1)}, f32[40,640]{1,0:T(8,128)S(1)}, u32[]{:S(2)}, u32[]{:S(2)}) collective-permute-start(f32[40,640]{1,0:T(8,128)S(1)} %get-tuple-element.56), channel_id=1, source_target_pairs={{0,4},{2,6},{8,0},{10,2},{16,8},{18,10},{24,16},{26,18},{28,24},{3... | collective-permute-start | bytes 307208 | tf_op jit(solution)/shard_map/ppermute | solution.py:313
  58.1 6.9 %collective-permute-start.27 = (f32[40,640]{1,0:T(8,128)S(1)}, f32[40,640]{1,0:T(8,128)S(1)}, u32[]{:S(2)}, u32[]{:S(2)}) collective-permute-start(f32[40,640]{1,0:T(8,128)S(1)} %get-tuple-element.64), channel_id=1, source_target_pairs={{0,8},{2,10},{8,16},{10,18},{16,24},{18,26},{24,28},{26,30},{28,20... | collective-permute-start | bytes 307208 | tf_op jit(solution)/shard_map/ppermute | solution.py:312
  61.5 5.2 %collective-permute-start.17 = (f32[40,640]{1,0:T(8,128)S(1)}, f32[40,640]{1,0:T(8,128)S(1)}, u32[]{:S(2)}, u32[]{:S(2)}) collective-permute-start(f32[40,640]{1,0:T(8,128)S(1)} %add.30), channel_id=1, source_target_pairs={{0,8},{2,10},{8,16},{10,18},{16,24},{18,26},{24,28},{26,30},{28,20... | collective-permute-start | bytes 307208 | tf_op jit(solution)/shard_map/ppermute | solution.py:312
  63.2 5.6 %collective-permute-start.24 = (f32[40,640]{1,0:T(8,128)S(1)}, f32[40,640]{1,0:T(8,128)S(1)}, u32[]{:S(2)}, u32[]{:S(2)}) collective-permute-start(f32[40,640]{1,0:T(8,128)S(1)} %add.35), channel_id=1, source_target_pairs={{0,4},{2,6},{8,0},{10,2},{16,8},{18,10},{24,16},{26,18},{28,24},{3... | collective-permute-start | bytes 307208 | tf_op jit(solution)/shard_map/ppermute | solution.py:313
  64.5 5.5 %collective-permute-start.21 = (f32[40,640]{1,0:T(8,128)S(1)}, f32[40,640]{1,0:T(8,128)S(1)}, u32[]{:S(2)}, u32[]{:S(2)}) collective-permute-start(f32[40,640]{1,0:T(8,128)S(1)} %add.33), channel_id=1, source_target_pairs={{0,4},{2,6},{8,0},{10,2},{16,8},{18,10},{24,16},{26,18},{28,24},{3... | collective-permute-start | bytes 307208 | tf_op jit(solution)/shard_map/ppermute | solution.py:313
  65.1 5.5 %collective-permute-start.28 = (f32[40,640]{1,0:T(8,128)S(1)}, f32[40,640]{1,0:T(8,128)S(1)}, u32[]{:S(2)}, u32[]{:S(2)}) collective-permute-start(f32[40,640]{1,0:T(8,128)S(1)} %add.38), channel_id=1, source_target_pairs={{0,8},{2,10},{8,16},{10,18},{16,24},{18,26},{24,28},{26,30},{28,20... | collective-permute-start | bytes 307208 | tf_op jit(solution)/shard_map/ppermute | solution.py:312
  66.7 5.5 %collective-permute-start.18 = (f32[40,640]{1,0:T(8,128)S(1)}, f32[40,640]{1,0:T(8,128)S(1)}, u32[]{:S(2)}, u32[]{:S(2)}) collective-permute-start(f32[40,640]{1,0:T(8,128)S(1)} %add.31), channel_id=1, source_target_pairs={{0,8},{2,10},{8,16},{10,18},{16,24},{18,26},{24,28},{26,30},{28,20... | collective-permute-start | bytes 307208 | tf_op jit(solution)/shard_map/ppermute | solution.py:312
  68.7 5.5 %collective-permute-start.25 = (f32[40,640]{1,0:T(8,128)S(1)}, f32[40,640]{1,0:T(8,128)S(1)}, u32[]{:S(2)}, u32[]{:S(2)}) collective-permute-start(f32[40,640]{1,0:T(8,128)S(1)} %add.36), channel_id=1, source_target_pairs={{0,4},{2,6},{8,0},{10,2},{16,8},{18,10},{24,16},{26,18},{28,24},{3... | collective-permute-start | bytes 307208 | tf_op jit(solution)/shard_map/ppermute | solution.py:313
  70.1 5.3 %collective-permute-start.22 = (f32[40,640]{1,0:T(8,128)S(1)}, f32[40,640]{1,0:T(8,128)S(1)}, u32[]{:S(2)}, u32[]{:S(2)}) collective-permute-start(f32[40,640]{1,0:T(8,128)S(1)} %add.34), channel_id=1, source_target_pairs={{0,4},{2,6},{8,0},{10,2},{16,8},{18,10},{24,16},{26,18},{28,24},{3... | collective-permute-start | bytes 307208 | tf_op jit(solution)/shard_map/ppermute | solution.py:313
  70.6 4.8 %collective-permute-start.29 = (f32[40,640]{1,0:T(8,128)S(1)}, f32[40,640]{1,0:T(8,128)S(1)}, u32[]{:S(2)}, u32[]{:S(2)}) collective-permute-start(f32[40,640]{1,0:T(8,128)S(1)} %add.39), channel_id=1, source_target_pairs={{0,8},{2,10},{8,16},{10,18},{16,24},{18,26},{24,28},{26,30},{28,20... | collective-permute-start | bytes 307208 | tf_op jit(solution)/shard_map/ppermute | solution.py:312
  72.2 4.7 %collective-permute-start.19 = (f32[40,640]{1,0:T(8,128)S(1)}, f32[40,640]{1,0:T(8,128)S(1)}, u32[]{:S(2)}, u32[]{:S(2)}) collective-permute-start(f32[40,640]{1,0:T(8,128)S(1)} %add.32), channel_id=1, source_target_pairs={{0,8},{2,10},{8,16},{10,18},{16,24},{18,26},{24,28},{26,30},{28,20... | collective-permute-start | bytes 307208 | tf_op jit(solution)/shard_map/ppermute | solution.py:312
  79.0 5.2 %collective-permute-start.32 = (f32[40,640]{1,0:T(8,128)S(1)}, f32[40,640]{1,0:T(8,128)S(1)}, u32[]{:S(2)}, u32[]{:S(2)}) collective-permute-start(f32[40,640]{1,0:T(8,128)S(1)} %get-tuple-element.67), channel_id=1, source_target_pairs={{0,3},{1,2},{2,1},{3,0},{4,7},{5,6},{6,5},{7,4},{8,11},{9,10},{10,... | collective-permute-start | bytes 307208 | tf_op jit(solution)/shard_map/ppermute | solution.py:401
  79.1 5.1 %collective-permute-start.30 = (f32[40,640]{1,0:T(8,128)S(1)}, f32[40,640]{1,0:T(8,128)S(1)}, u32[]{:S(2)}, u32[]{:S(2)}) collective-permute-start(f32[40,640]{1,0:T(8,128)S(1)} %get-tuple-element.67), channel_id=1, source_target_pairs={{0,2},{2,0},{4,6},{6,4},{8,10},{10,8},{12,14},{14,12},{16,18},{18,... | collective-permute-start | bytes 307208 | tf_op jit(solution)/shard_map/ppermute | solution.py:310
  80.7 5.7 %collective-permute-start.31 = (f32[40,640]{1,0:T(8,128)S(1)}, f32[40,640]{1,0:T(8,128)S(1)}, u32[]{:S(2)}, u32[]{:S(2)}) collective-permute-start(f32[40,640]{1,0:T(8,128)S(1)} %get-tuple-element.68.keep), channel_id=1, source_target_pairs={{0,1},{1,0},{2,3},{3,2},{4,5},{5,4},{6,7},{7,6},{8,9},{9,8},{10,11... | collective-permute-start | bytes 307208 | tf_op jit(solution)/shard_map/ppermute | solution.py:400
  (8 other events, 35.4 us)

commit v7 on v6

--- a/solution.py
+++ b/solution.py
@@ -95,7 +95,7 @@
         c.start()
     loads[2].wait()
     in_use = lax.broadcasted_iota(jnp.int32, gv.shape, 0) < length[0]
-    gv[...] = jnp.where(in_use, gv[...].astype(F32), 0.0).astype(BF)
+    gv[...] = jnp.where(in_use, gv[...], jnp.zeros_like(gv))
     stores[2].start()
     for i in (1, 0):
         loads[i].wait()
@@ -188,13 +188,13 @@
     halves = (slice(0, 256), slice(256, TOK))
     items = [(clip, h, t) for clip in range(2) for h in range(number) for t in halves]
     project(0)
-    begun = [begin(*item) for item in items[:2]]
+    begun = [begin(*item) for item in items[:3]]
     done = []
     for i, item in enumerate(items):
         if i == 6:
             project(1)
-        if i + 2 < len(items):
-            begun.append(begin(*items[i + 2]))
+        if i + 3 < len(items):
+            begun.append(begin(*items[i + 3]))
         done.append(finish(*item, *begun[i]))
     ctxs, grads = [
         [

time: 87.9 us -> 87.5 us (level)
  no operation moved by 1% of the time
where the time goes in v7:
time: 87.5 us; the launch traced here: 87.3 us
  starting transfers between devices  33.3 us (38%)
  waiting for transfers between devices  28.8 us (33%)
  Pallas kernels  21.6 us (25%)
  local copies, waits for them, and re-layouts  2.03 us (2%)
  between operations  1.45 us (2%)
    ppermute x14, starting transfers between devices, per_device(): right = lambda a: lax.ppermute(a, 'dp', ring_pairs(chips, 1))  25.6 us
    ppermute x14, waiting for transfers between devices, per_device(): left = lambda a: lax.ppermute(a, 'dp', ring_pairs(chips, -1))  16.6 us
    pallas_call x1, Pallas kernels, heads(): pl.pallas_call(functools.partial(head_kernel, chips, steps, pieces), out_...  11.9 us
    ppermute x14, waiting for transfers between devices, per_device(): right = lambda a: lax.ppermute(a, 'dp', ring_pairs(chips, 1))  9.3 us
    ppermute x14, starting transfers between devices, per_device(): left = lambda a: lax.ppermute(a, 'dp', ring_pairs(chips, -1))  4.83 us
    pallas_call x1, Pallas kernels, per_device(): pl.pallas_call(stage_kernel, out_shape=jax.ShapeDtypeStruct((2 * TOK + fr...  3.22 us
    pallas_call x1, Pallas kernels, per_device(): pl.pallas_call(out_kernel, out_shape=jax.ShapeDtypeStruct((TOK, depth), B...  2.37 us
    ppermute x4, starting transfers between devices, per_device(): swap = lambda a: lax.ppermute(a, 'dp', mates)  2.33 us
  transfers between devices with their start and end apart: 34, of which 17 were waited for; matrix products, arithmetic and copies ran while one was open for 0% of the time, Pallas kernels for 7%

profile of v7, /device:TPU:0, one launch (start us, length us, event | category | flops | bytes accessed | tf_op | source)
XLA Modules:
  0.0 87.3 jit_solution(12193813611724241460)
XLA Ops:
  0.6 2.0 %shard_map.137 = (bf16[80,1280]{1,0:T(8,128)(2,1)}, bf16[80,1280]{1,0:T(8,128)(2,1)}) custom-call(s32[1]{0:T(128)} %bitcast.me.refs_0_, f32[80,640]{1,0:T(8,128)} %master.1, bf16[80,640]{1,0:T(8,128)(2,1)} %k.1, bf16[80,640]{1,0:T(8,128)(2,1)} %v.1, bf16[80,640]{1,0:T(8,128)(2,1)} %bitcast.2), custom_call_target="tpu_custom_call" | custom-call | tf_op jit(solution)/shard_map/pallas_call | solution.py:317
  3.9 3.2 %shard_map.138.mine.refs_17_ = bf16[1408,1280]{1,0:T(8,128)(2,1)} custom-call(s32[1]{0:T(128)S(6)} %copy.15.length, bf16[448,1280]{1,0:T(8,128)(2,1)} %x.1, bf16[512,1280]{1,0:T(8,128)(2,1)} %e.1, bf16[448,1280]{1,0:T(8,128)(2,1)} %g.1, bf16[80,1280]{1,0:T(8,128)(2,1)} %get-tuple-element.42._.keep), custom_call_target="tpu_custom_call" | custom-call | tf_op jit(solution)/shard_map/pallas_call | solution.py:328
  7.3 3.0 %collective-permute-start.1 = (bf16[160,640]{1,0:T(8,128)(2,1)S(1)}, bf16[160,640]{1,0:T(8,128)(2,1)S(1)}, u32[]{:S(2)}, u32[]{:S(2)}) collective-permute-start(bf16[160,640]{1,0:T(8,128)(2,1)S(1)} %get-tuple-element.46.refs_1_), channel_id=1, source_target_pairs={{0,8},{2,10},{8,16},{10,18},{16,24},{18,26},{24,28},{26,30},{28,20... | collective-permute-start | bytes 614408 | tf_op jit(solution)/shard_map/ppermute | solution.py:312
  10.3 1.9 %collective-permute-start.2 = (bf16[160,640]{1,0:T(8,128)(2,1)S(1)}, bf16[160,640]{1,0:T(8,128)(2,1)S(1)}, u32[]{:S(2)}, u32[]{:S(2)}) collective-permute-start(bf16[160,640]{1,0:T(8,128)(2,1)S(1)} %get-tuple-element.46.refs_1_), channel_id=1, source_target_pairs={{0,4},{2,6},{8,0},{10,2},{16,8},{18,10},{24,16},{26,18},{28,24},{3... | collective-permute-start | bytes 614408 | tf_op jit(solution)/shard_map/ppermute | solution.py:313
  12.4 3.7 %collective-permute-done.1.refs_2_ = bf16[160,640]{1,0:T(8,128)(2,1)S(1)} collective-permute-done((bf16[160,640]{1,0:T(8,128)(2,1)S(1)}, bf16[160,640]{1,0:T(8,128)(2,1)S(1)}, u32[]{:S(2)}, u32[]{:S(2)}) %collective-permute-start.1) | collective-permute-done | bytes 204832 | tf_op jit(solution)/shard_map/ppermute | solution.py:312
  16.1 2.1 %collective-permute-start.3 = (bf16[160,640]{1,0:T(8,128)(2,1)S(1)}, bf16[160,640]{1,0:T(8,128)(2,1)S(1)}, u32[]{:S(2)}, u32[]{:S(2)}) collective-permute-start(bf16[160,640]{1,0:T(8,128)(2,1)S(1)} %collective-permute-done.1.refs_2_), channel_id=1, source_target_pairs={{0,8},{2,10},{8,16},{10,18},{16,24},{18,26},{24,28},{26,30},{28,20... | collective-permute-start | bytes 614408 | tf_op jit(solution)/shard_map/ppermute | solution.py:312
  18.3 4.4 %collective-permute-done.2.refs_3_ = bf16[160,640]{1,0:T(8,128)(2,1)S(1)} collective-permute-done((bf16[160,640]{1,0:T(8,128)(2,1)S(1)}, bf16[160,640]{1,0:T(8,128)(2,1)S(1)}, u32[]{:S(2)}, u32[]{:S(2)}) %collective-permute-start.2) | collective-permute-done | bytes 204832 | tf_op jit(solution)/shard_map/ppermute | solution.py:313
  22.7 2.0 %collective-permute-start.10 = (bf16[160,640]{1,0:T(8,128)(2,1)S(1)}, bf16[160,640]{1,0:T(8,128)(2,1)S(1)}, u32[]{:S(2)}, u32[]{:S(2)}) collective-permute-start(bf16[160,640]{1,0:T(8,128)(2,1)S(1)} %collective-permute-done.8.refs_10_), channel_id=1, source_target_pairs={{0,8},{2,10},{8,16},{10,18},{16,24},{18,26},{24,28},{26,30},{28,20... | collective-permute-start | bytes 614408 | tf_op jit(solution)/shard_map/ppermute | solution.py:312
  24.9 2.1 %collective-permute-start.5 = (bf16[160,640]{1,0:T(8,128)(2,1)S(1)}, bf16[160,640]{1,0:T(8,128)(2,1)S(1)}, u32[]{:S(2)}, u32[]{:S(2)}) collective-permute-start(bf16[160,640]{1,0:T(8,128)(2,1)S(1)} %collective-permute-done.3.refs_4_), channel_id=1, source_target_pairs={{0,8},{2,10},{8,16},{10,18},{16,24},{18,26},{24,28},{26,30},{28,20... | collective-permute-start | bytes 614408 | tf_op jit(solution)/shard_map/ppermute | solution.py:312
  27.1 4.4 %collective-permute-done.4.refs_5_ = bf16[160,640]{1,0:T(8,128)(2,1)S(1)} collective-permute-done((bf16[160,640]{1,0:T(8,128)(2,1)S(1)}, bf16[160,640]{1,0:T(8,128)(2,1)S(1)}, u32[]{:S(2)}, u32[]{:S(2)}) %collective-permute-start.4) | collective-permute-done | bytes 204832 | tf_op jit(solution)/shard_map/ppermute | solution.py:313
  31.5 2.0 %collective-permute-start.12 = (bf16[160,640]{1,0:T(8,128)(2,1)S(1)}, bf16[160,640]{1,0:T(8,128)(2,1)S(1)}, u32[]{:S(2)}, u32[]{:S(2)}) collective-permute-start(bf16[160,640]{1,0:T(8,128)(2,1)S(1)} %collective-permute-done.10.refs_12_), channel_id=1, source_target_pairs={{0,8},{2,10},{8,16},{10,18},{16,24},{18,26},{24,28},{26,30},{28,20... | collective-permute-start | bytes 614408 | tf_op jit(solution)/shard_map/ppermute | solution.py:312
  34.0 2.2 %collective-permute-start.7 = (bf16[160,640]{1,0:T(8,128)(2,1)S(1)}, bf16[160,640]{1,0:T(8,128)(2,1)S(1)}, u32[]{:S(2)}, u32[]{:S(2)}) collective-permute-start(bf16[160,640]{1,0:T(8,128)(2,1)S(1)} %collective-permute-done.5.refs_6_), channel_id=1, source_target_pairs={{0,8},{2,10},{8,16},{10,18},{16,24},{18,26},{24,28},{26,30},{28,20... | collective-permute-start | bytes 614408 | tf_op jit(solution)/shard_map/ppermute | solution.py:312
  36.3 2.0 %copy-done = bf16[1408,1280]{1,0:T(8,128)(2,1)S(1)} copy-done((bf16[1408,1280]{1,0:T(8,128)(2,1)S(1)}, bf16[1408,1280]{1,0:T(8,128)(2,1)}, u32[]{:S(2)}) %copy-start) | copy-done | bytes 3604504
  39.0 1.2 %collective-permute-done.6.refs_7_ = bf16[160,640]{1,0:T(8,128)(2,1)S(1)} collective-permute-done((bf16[160,640]{1,0:T(8,128)(2,1)S(1)}, bf16[160,640]{1,0:T(8,128)(2,1)S(1)}, u32[]{:S(2)}, u32[]{:S(2)}) %collective-permute-start.6) | collective-permute-done | bytes 204832 | tf_op jit(solution)/shard_map/ppermute | solution.py:313
  40.2 1.6 %collective-permute-done.7.refs_8_ = bf16[160,640]{1,0:T(8,128)(2,1)S(1)} collective-permute-done((bf16[160,640]{1,0:T(8,128)(2,1)S(1)}, bf16[160,640]{1,0:T(8,128)(2,1)S(1)}, u32[]{:S(2)}, u32[]{:S(2)}) %collective-permute-start.7) | collective-permute-done | bytes 204832 | tf_op jit(solution)/shard_map/ppermute | solution.py:312
  41.9 1.5 %collective-permute-done.14.refs_16_ = bf16[160,640]{1,0:T(8,128)(2,1)S(1)} collective-permute-done((bf16[160,640]{1,0:T(8,128)(2,1)S(1)}, bf16[160,640]{1,0:T(8,128)(2,1)S(1)}, u32[]{:S(2)}, u32[]{:S(2)}) %collective-permute-start.14) | collective-permute-done | bytes 204832 | tf_op jit(solution)/shard_map/ppermute | solution.py:313
  43.4 11.9 %shard_map.141 = (bf16[1728,384]{1,0:T(8,128)(2,1)S(1)}, bf16[448,320]{1,0:T(8,128)(2,1)S(1)}, f32[40,640]{1,0:T(8,128)S(1)}, f32[40,640]{1,0:T(8,128)S(1)}, f32...) custom-call(s32[1]{0:T(128)} %bitcast.me.refs_0_, ...), custom_call_target="tpu_custom_call" | custom-call | flops 8999999488 | bytes 15000000 | tf_op jit(solution)/shard_map/pallas_call | solution.py:227
  55.4 1.6 %collective-permute-start.16 = (f32[40,640]{1,0:T(8,128)S(1)}, f32[40,640]{1,0:T(8,128)S(1)}, u32[]{:S(2)}, u32[]{:S(2)}) collective-permute-start(f32[40,640]{1,0:T(8,128)S(1)} %get-tuple-element.52), channel_id=1, source_target_pairs={{0,8},{2,10},{8,16},{10,18},{16,24},{18,26},{24,28},{26,30},{28,20... | collective-permute-start | bytes 307208 | tf_op jit(solution)/shard_map/ppermute | solution.py:312
  57.8 1.7 %collective-permute-start.27 = (f32[40,640]{1,0:T(8,128)S(1)}, f32[40,640]{1,0:T(8,128)S(1)}, u32[]{:S(2)}, u32[]{:S(2)}) collective-permute-start(f32[40,640]{1,0:T(8,128)S(1)} %get-tuple-element.64), channel_id=1, source_target_pairs={{0,8},{2,10},{8,16},{10,18},{16,24},{18,26},{24,28},{26,30},{28,20... | collective-permute-start | bytes 307208 | tf_op jit(solution)/shard_map/ppermute | solution.py:312
  59.6 1.6 %collective-permute-done.16 = f32[40,640]{1,0:T(8,128)S(1)} collective-permute-done((f32[40,640]{1,0:T(8,128)S(1)}, f32[40,640]{1,0:T(8,128)S(1)}, u32[]{:S(2)}, u32[]{:S(2)}) %collective-permute-start.16) | collective-permute-done | bytes 102432 | tf_op jit(solution)/shard_map/ppermute | solution.py:312
  61.2 1.6 %collective-permute-start.17 = (f32[40,640]{1,0:T(8,128)S(1)}, f32[40,640]{1,0:T(8,128)S(1)}, u32[]{:S(2)}, u32[]{:S(2)}) collective-permute-start(f32[40,640]{1,0:T(8,128)S(1)} %add.30), channel_id=1, source_target_pairs={{0,8},{2,10},{8,16},{10,18},{16,24},{18,26},{24,28},{26,30},{28,20... | collective-permute-start | bytes 307208 | tf_op jit(solution)/shard_map/ppermute | solution.py:312
  64.8 1.6 %collective-permute-start.28 = (f32[40,640]{1,0:T(8,128)S(1)}, f32[40,640]{1,0:T(8,128)S(1)}, u32[]{:S(2)}, u32[]{:S(2)}) collective-permute-start(f32[40,640]{1,0:T(8,128)S(1)} %add.38), channel_id=1, source_target_pairs={{0,8},{2,10},{8,16},{10,18},{16,24},{18,26},{24,28},{26,30},{28,20... | collective-permute-start | bytes 307208 | tf_op jit(solution)/shard_map/ppermute | solution.py:312
  66.4 1.6 %collective-permute-start.18 = (f32[40,640]{1,0:T(8,128)S(1)}, f32[40,640]{1,0:T(8,128)S(1)}, u32[]{:S(2)}, u32[]{:S(2)}) collective-permute-start(f32[40,640]{1,0:T(8,128)S(1)} %add.31), channel_id=1, source_target_pairs={{0,8},{2,10},{8,16},{10,18},{16,24},{18,26},{24,28},{26,30},{28,20... | collective-permute-start | bytes 307208 | tf_op jit(solution)/shard_map/ppermute | solution.py:312
  70.3 1.6 %collective-permute-start.29 = (f32[40,640]{1,0:T(8,128)S(1)}, f32[40,640]{1,0:T(8,128)S(1)}, u32[]{:S(2)}, u32[]{:S(2)}) collective-permute-start(f32[40,640]{1,0:T(8,128)S(1)} %add.39), channel_id=1, source_target_pairs={{0,8},{2,10},{8,16},{10,18},{16,24},{18,26},{24,28},{26,30},{28,20... | collective-permute-start | bytes 307208 | tf_op jit(solution)/shard_map/ppermute | solution.py:312
  71.9 2.0 %collective-permute-start.19 = (f32[40,640]{1,0:T(8,128)S(1)}, f32[40,640]{1,0:T(8,128)S(1)}, u32[]{:S(2)}, u32[]{:S(2)}) collective-permute-start(f32[40,640]{1,0:T(8,128)S(1)} %add.32), channel_id=1, source_target_pairs={{0,8},{2,10},{8,16},{10,18},{16,24},{18,26},{24,28},{26,30},{28,20... | collective-permute-start | bytes 307208 | tf_op jit(solution)/shard_map/ppermute | solution.py:312
  74.1 1.0 %collective-permute-done.22.refs_2_ = f32[40,640]{1,0:T(8,128)S(1)} collective-permute-done((f32[40,640]{1,0:T(8,128)S(1)}, f32[40,640]{1,0:T(8,128)S(1)}, u32[]{:S(2)}, u32[]{:S(2)}) %collective-permute-start.22) | collective-permute-done | bytes 102432 | tf_op jit(solution)/shard_map/ppermute | solution.py:313
  75.1 1.6 %collective-permute-done.19.refs_1_ = f32[40,640]{1,0:T(8,128)S(1)} collective-permute-done((f32[40,640]{1,0:T(8,128)S(1)}, f32[40,640]{1,0:T(8,128)S(1)}, u32[]{:S(2)}, u32[]{:S(2)}) %collective-permute-start.19) | collective-permute-done | bytes 102432 | tf_op jit(solution)/shard_map/ppermute | solution.py:312
  76.6 2.0 %collective-permute-done.26.refs_4_ = f32[40,640]{1,0:T(8,128)S(1)} collective-permute-done((f32[40,640]{1,0:T(8,128)S(1)}, f32[40,640]{1,0:T(8,128)S(1)}, u32[]{:S(2)}, u32[]{:S(2)}) %collective-permute-start.26) | collective-permute-done | bytes 102432 | tf_op jit(solution)/shard_map/ppermute | solution.py:313
  78.8 1.6 %collective-permute-start.30 = (f32[40,640]{1,0:T(8,128)S(1)}, f32[40,640]{1,0:T(8,128)S(1)}, u32[]{:S(2)}, u32[]{:S(2)}) collective-permute-start(f32[40,640]{1,0:T(8,128)S(1)} %get-tuple-element.67), channel_id=1, source_target_pairs={{0,2},{2,0},{4,6},{6,4},{8,10},{10,8},{12,14},{14,12},{16,18},{18,... | collective-permute-start | bytes 307208 | tf_op jit(solution)/shard_map/ppermute | solution.py:310
  80.9 2.4 %shard_map.143 = bf16[448,1280]{1,0:T(8,128)(2,1)} custom-call(bf16[448,320]{1,0:T(8,128)(2,1)S(1)} %get-tuple-element.69.ctx_own, bf16[1728,384]{1,0:T(8,128)(2,1)S(1)} %get-tuple-element.70.share, bf16[1728,384]{1,0:T(8,128)(2,1)S(1)} %collective-permute-done.33.got), custom_call_target="tpu_custom_call" | custom-call | flops 734003200 | bytes 4000000 | tf_op jit(solution)/shard_map/pallas_call | solution.py:416
  83.9 2.3 %collective-permute-done.31.keep_y = f32[40,640]{1,0:T(8,128)S(1)} collective-permute-done((f32[40,640]{1,0:T(8,128)S(1)}, f32[40,640]{1,0:T(8,128)S(1)}, u32[]{:S(2)}, u32[]{:S(2)}) %collective-permute-start.31) | collective-permute-done | bytes 102432 | tf_op jit(solution)/shard_map/ppermute | solution.py:400
  86.2 1.2 %shard_map.144 = (f32[80,640]{1,0:T(8,128)}, f32[80,640]{1,0:T(8,128)}, f32[80,640]{1,0:T(8,128)}, f32[80,640]{1,0:T(8,128)}) custom-call(s32[1]{0:T(128)} %bitcast.me.refs_0_, f32[40,640]{1,0:T(8,128)S(1)} %get-tuple-element.68.keep, f32[40,640]{1,0:T(8,128)S(1)} %collective-permute-done.31.keep_y, f32[40,640]{1,0:T(8,128)S(1)} %collective-permute-done.30.got, ...), custom_call_target="tpu_custom_call" | custom-call | tf_op jit(solution)/shard_map/pallas_call | solution.py:428
  (66 shorter events, 8.8 us)
Async XLA Ops:
  7.2 29.1 %collective-permute-start.15 = (bf16[1408,1280]{1,0:T(8,128)(2,1)}, bf16[1408,1280]{1,0:T(8,128)(2,1)S(1)}, u32[]{:S(2)}, u32[]{:S(2)}) collective-permute-start(bf16[1408,1280]{1,0:T(8,128)(2,1)} %shard_map.138.mine.refs_17_), channel_id=1, source_target_pairs={{0,2},{2,0},{4,6},{6,4},{8,10},{10,8},{12,14},{14,12},{16,18},{18,... | collective-permute-start | bytes 10813448 | tf_op jit(solution)/shard_map/ppermute | solution.py:310
  7.3 8.8 %collective-permute-start.1 = (bf16[160,640]{1,0:T(8,128)(2,1)S(1)}, bf16[160,640]{1,0:T(8,128)(2,1)S(1)}, u32[]{:S(2)}, u32[]{:S(2)}) collective-permute-start(bf16[160,640]{1,0:T(8,128)(2,1)S(1)} %get-tuple-element.46.refs_1_), channel_id=1, source_target_pairs={{0,8},{2,10},{8,16},{10,18},{16,24},{18,26},{24,28},{26,30},{28,20... | collective-permute-start | bytes 614408 | tf_op jit(solution)/shard_map/ppermute | solution.py:312
  10.3 8.0 %collective-permute-start.9 = (bf16[160,640]{1,0:T(8,128)(2,1)S(1)}, bf16[160,640]{1,0:T(8,128)(2,1)S(1)}, u32[]{:S(2)}, u32[]{:S(2)}) collective-permute-start(bf16[160,640]{1,0:T(8,128)(2,1)S(1)} %get-tuple-element.47.refs_9_), channel_id=1, source_target_pairs={{0,4},{2,6},{8,0},{10,2},{16,8},{18,10},{24,16},{26,18},{28,24},{3... | collective-permute-start | bytes 614408 | tf_op jit(solution)/shard_map/ppermute | solution.py:313
  10.3 12.4 %collective-permute-start.2 = (bf16[160,640]{1,0:T(8,128)(2,1)S(1)}, bf16[160,640]{1,0:T(8,128)(2,1)S(1)}, u32[]{:S(2)}, u32[]{:S(2)}) collective-permute-start(bf16[160,640]{1,0:T(8,128)(2,1)S(1)} %get-tuple-element.46.refs_1_), channel_id=1, source_target_pairs={{0,4},{2,6},{8,0},{10,2},{16,8},{18,10},{24,16},{26,18},{28,24},{3... | collective-permute-start | bytes 614408 | tf_op jit(solution)/shard_map/ppermute | solution.py:313
  12.3 10.4 %collective-permute-start.8 = (bf16[160,640]{1,0:T(8,128)(2,1)S(1)}, bf16[160,640]{1,0:T(8,128)(2,1)S(1)}, u32[]{:S(2)}, u32[]{:S(2)}) collective-permute-start(bf16[160,640]{1,0:T(8,128)(2,1)S(1)} %get-tuple-element.47.refs_9_), channel_id=1, source_target_pairs={{0,8},{2,10},{8,16},{10,18},{16,24},{18,26},{24,28},{26,30},{28,20... | collective-permute-start | bytes 614408 | tf_op jit(solution)/shard_map/ppermute | solution.py:312
  16.1 8.8 %collective-permute-start.3 = (bf16[160,640]{1,0:T(8,128)(2,1)S(1)}, bf16[160,640]{1,0:T(8,128)(2,1)S(1)}, u32[]{:S(2)}, u32[]{:S(2)}) collective-permute-start(bf16[160,640]{1,0:T(8,128)(2,1)S(1)} %collective-permute-done.1.refs_2_), channel_id=1, source_target_pairs={{0,8},{2,10},{8,16},{10,18},{16,24},{18,26},{24,28},{26,30},{28,20... | collective-permute-start | bytes 614408 | tf_op jit(solution)/shard_map/ppermute | solution.py:312
  18.3 8.8 %collective-permute-start.11 = (bf16[160,640]{1,0:T(8,128)(2,1)S(1)}, bf16[160,640]{1,0:T(8,128)(2,1)S(1)}, u32[]{:S(2)}, u32[]{:S(2)}) collective-permute-start(bf16[160,640]{1,0:T(8,128)(2,1)S(1)} %collective-permute-done.9.refs_11_), channel_id=1, source_target_pairs={{0,4},{2,6},{8,0},{10,2},{16,8},{18,10},{24,16},{26,18},{28,24},{3... | collective-permute-start | bytes 614408 | tf_op jit(solution)/shard_map/ppermute | solution.py:313
  22.7 8.8 %collective-permute-start.4 = (bf16[160,640]{1,0:T(8,128)(2,1)S(1)}, bf16[160,640]{1,0:T(8,128)(2,1)S(1)}, u32[]{:S(2)}, u32[]{:S(2)}) collective-permute-start(bf16[160,640]{1,0:T(8,128)(2,1)S(1)} %collective-permute-done.2.refs_3_), channel_id=1, source_target_pairs={{0,4},{2,6},{8,0},{10,2},{16,8},{18,10},{24,16},{26,18},{28,24},{3... | collective-permute-start | bytes 614408 | tf_op jit(solution)/shard_map/ppermute | solution.py:313
  22.7 8.8 %collective-permute-start.10 = (bf16[160,640]{1,0:T(8,128)(2,1)S(1)}, bf16[160,640]{1,0:T(8,128)(2,1)S(1)}, u32[]{:S(2)}, u32[]{:S(2)}) collective-permute-start(bf16[160,640]{1,0:T(8,128)(2,1)S(1)} %collective-permute-done.8.refs_10_), channel_id=1, source_target_pairs={{0,8},{2,10},{8,16},{10,18},{16,24},{18,26},{24,28},{26,30},{28,20... | collective-permute-start | bytes 614408 | tf_op jit(solution)/shard_map/ppermute | solution.py:312
  24.9 9.2 %collective-permute-start.5 = (bf16[160,640]{1,0:T(8,128)(2,1)S(1)}, bf16[160,640]{1,0:T(8,128)(2,1)S(1)}, u32[]{:S(2)}, u32[]{:S(2)}) collective-permute-start(bf16[160,640]{1,0:T(8,128)(2,1)S(1)} %collective-permute-done.3.refs_4_), channel_id=1, source_target_pairs={{0,8},{2,10},{8,16},{10,18},{16,24},{18,26},{24,28},{26,30},{28,20... | collective-permute-start | bytes 614408 | tf_op jit(solution)/shard_map/ppermute | solution.py:312
  27.1 9.2 %collective-permute-start.13 = (bf16[160,640]{1,0:T(8,128)(2,1)S(1)}, bf16[160,640]{1,0:T(8,128)(2,1)S(1)}, u32[]{:S(2)}, u32[]{:S(2)}) collective-permute-start(bf16[160,640]{1,0:T(8,128)(2,1)S(1)} %collective-permute-done.11.refs_13_), channel_id=1, source_target_pairs={{0,4},{2,6},{8,0},{10,2},{16,8},{18,10},{24,16},{26,18},{28,24},{3... | collective-permute-start | bytes 614408 | tf_op jit(solution)/shard_map/ppermute | solution.py:313
  31.5 8.8 %collective-permute-start.6 = (bf16[160,640]{1,0:T(8,128)(2,1)S(1)}, bf16[160,640]{1,0:T(8,128)(2,1)S(1)}, u32[]{:S(2)}, u32[]{:S(2)}) collective-permute-start(bf16[160,640]{1,0:T(8,128)(2,1)S(1)} %collective-permute-done.4.refs_5_), channel_id=1, source_target_pairs={{0,4},{2,6},{8,0},{10,2},{16,8},{18,10},{24,16},{26,18},{28,24},{3... | collective-permute-start | bytes 614408 | tf_op jit(solution)/shard_map/ppermute | solution.py:313
  31.5 8.8 %collective-permute-start.12 = (bf16[160,640]{1,0:T(8,128)(2,1)S(1)}, bf16[160,640]{1,0:T(8,128)(2,1)S(1)}, u32[]{:S(2)}, u32[]{:S(2)}) collective-permute-start(bf16[160,640]{1,0:T(8,128)(2,1)S(1)} %collective-permute-done.10.refs_12_), channel_id=1, source_target_pairs={{0,8},{2,10},{8,16},{10,18},{16,24},{18,26},{24,28},{26,30},{28,20... | collective-permute-start | bytes 614408 | tf_op jit(solution)/shard_map/ppermute | solution.py:312
  34.0 7.8 %collective-permute-start.7 = (bf16[160,640]{1,0:T(8,128)(2,1)S(1)}, bf16[160,640]{1,0:T(8,128)(2,1)S(1)}, u32[]{:S(2)}, u32[]{:S(2)}) collective-permute-start(bf16[160,640]{1,0:T(8,128)(2,1)S(1)} %collective-permute-done.5.refs_6_), channel_id=1, source_target_pairs={{0,8},{2,10},{8,16},{10,18},{16,24},{18,26},{24,28},{26,30},{28,20... | collective-permute-start | bytes 614408 | tf_op jit(solution)/shard_map/ppermute | solution.py:312
  36.3 7.1 %collective-permute-start.14 = (bf16[160,640]{1,0:T(8,128)(2,1)S(1)}, bf16[160,640]{1,0:T(8,128)(2,1)S(1)}, u32[]{:S(2)}, u32[]{:S(2)}) collective-permute-start(bf16[160,640]{1,0:T(8,128)(2,1)S(1)} %collective-permute-done.13.refs_15_), channel_id=1, source_target_pairs={{0,4},{2,6},{8,0},{10,2},{16,8},{18,10},{24,16},{26,18},{28,24},{3... | collective-permute-start | bytes 614408 | tf_op jit(solution)/shard_map/ppermute | solution.py:313
  55.4 25.6 %collective-permute-start.33 = (bf16[1728,384]{1,0:T(8,128)(2,1)S(1)}, bf16[1728,384]{1,0:T(8,128)(2,1)S(1)}, u32[]{:S(2)}, u32[]{:S(2)}) collective-permute-start(bf16[1728,384]{1,0:T(8,128)(2,1)S(1)} %get-tuple-element.70.share), channel_id=1, source_target_pairs={{0,2},{2,0},{4,6},{6,4},{8,10},{10,8},{12,14},{14,12},{16,18},{18,... | collective-permute-start | bytes 3981320 | tf_op jit(solution)/shard_map/ppermute | solution.py:310
  55.4 5.7 %collective-permute-start.16 = (f32[40,640]{1,0:T(8,128)S(1)}, f32[40,640]{1,0:T(8,128)S(1)}, u32[]{:S(2)}, u32[]{:S(2)}) collective-permute-start(f32[40,640]{1,0:T(8,128)S(1)} %get-tuple-element.52), channel_id=1, source_target_pairs={{0,8},{2,10},{8,16},{10,18},{16,24},{18,26},{24,28},{26,30},{28,20... | collective-permute-start | bytes 307208 | tf_op jit(solution)/shard_map/ppermute | solution.py:312
  57.1 5.8 %collective-permute-start.23 = (f32[40,640]{1,0:T(8,128)S(1)}, f32[40,640]{1,0:T(8,128)S(1)}, u32[]{:S(2)}, u32[]{:S(2)}) collective-permute-start(f32[40,640]{1,0:T(8,128)S(1)} %get-tuple-element.60), channel_id=1, source_target_pairs={{0,4},{2,6},{8,0},{10,2},{16,8},{18,10},{24,16},{26,18},{28,24},{3... | collective-permute-start | bytes 307208 | tf_op jit(solution)/shard_map/ppermute | solution.py:313
  57.5 6.7 %collective-permute-start.20 = (f32[40,640]{1,0:T(8,128)S(1)}, f32[40,640]{1,0:T(8,128)S(1)}, u32[]{:S(2)}, u32[]{:S(2)}) collective-permute-start(f32[40,640]{1,0:T(8,128)S(1)} %get-tuple-element.56), channel_id=1, source_target_pairs={{0,4},{2,6},{8,0},{10,2},{16,8},{18,10},{24,16},{26,18},{28,24},{3... | collective-permute-start | bytes 307208 | tf_op jit(solution)/shard_map/ppermute | solution.py:313
  57.8 6.9 %collective-permute-start.27 = (f32[40,640]{1,0:T(8,128)S(1)}, f32[40,640]{1,0:T(8,128)S(1)}, u32[]{:S(2)}, u32[]{:S(2)}) collective-permute-start(f32[40,640]{1,0:T(8,128)S(1)} %get-tuple-element.64), channel_id=1, source_target_pairs={{0,8},{2,10},{8,16},{10,18},{16,24},{18,26},{24,28},{26,30},{28,20... | collective-permute-start | bytes 307208 | tf_op jit(solution)/shard_map/ppermute | solution.py:312
  61.2 5.2 %collective-permute-start.17 = (f32[40,640]{1,0:T(8,128)S(1)}, f32[40,640]{1,0:T(8,128)S(1)}, u32[]{:S(2)}, u32[]{:S(2)}) collective-permute-start(f32[40,640]{1,0:T(8,128)S(1)} %add.30), channel_id=1, source_target_pairs={{0,8},{2,10},{8,16},{10,18},{16,24},{18,26},{24,28},{26,30},{28,20... | collective-permute-start | bytes 307208 | tf_op jit(solution)/shard_map/ppermute | solution.py:312
  62.8 5.6 %collective-permute-start.24 = (f32[40,640]{1,0:T(8,128)S(1)}, f32[40,640]{1,0:T(8,128)S(1)}, u32[]{:S(2)}, u32[]{:S(2)}) collective-permute-start(f32[40,640]{1,0:T(8,128)S(1)} %add.35), channel_id=1, source_target_pairs={{0,4},{2,6},{8,0},{10,2},{16,8},{18,10},{24,16},{26,18},{28,24},{3... | collective-permute-start | bytes 307208 | tf_op jit(solution)/shard_map/ppermute | solution.py:313
  64.2 5.5 %collective-permute-start.21 = (f32[40,640]{1,0:T(8,128)S(1)}, f32[40,640]{1,0:T(8,128)S(1)}, u32[]{:S(2)}, u32[]{:S(2)}) collective-permute-start(f32[40,640]{1,0:T(8,128)S(1)} %add.33), channel_id=1, source_target_pairs={{0,4},{2,6},{8,0},{10,2},{16,8},{18,10},{24,16},{26,18},{28,24},{3... | collective-permute-start | bytes 307208 | tf_op jit(solution)/shard_map/ppermute | solution.py:313
  64.8 5.5 %collective-permute-start.28 = (f32[40,640]{1,0:T(8,128)S(1)}, f32[40,640]{1,0:T(8,128)S(1)}, u32[]{:S(2)}, u32[]{:S(2)}) collective-permute-start(f32[40,640]{1,0:T(8,128)S(1)} %add.38), channel_id=1, source_target_pairs={{0,8},{2,10},{8,16},{10,18},{16,24},{18,26},{24,28},{26,30},{28,20... | collective-permute-start | bytes 307208 | tf_op jit(solution)/shard_map/ppermute | solution.py:312
  66.4 5.5 %collective-permute-start.18 = (f32[40,640]{1,0:T(8,128)S(1)}, f32[40,640]{1,0:T(8,128)S(1)}, u32[]{:S(2)}, u32[]{:S(2)}) collective-permute-start(f32[40,640]{1,0:T(8,128)S(1)} %add.31), channel_id=1, source_target_pairs={{0,8},{2,10},{8,16},{10,18},{16,24},{18,26},{24,28},{26,30},{28,20... | collective-permute-start | bytes 307208 | tf_op jit(solution)/shard_map/ppermute | solution.py:312
  68.4 5.5 %collective-permute-start.25 = (f32[40,640]{1,0:T(8,128)S(1)}, f32[40,640]{1,0:T(8,128)S(1)}, u32[]{:S(2)}, u32[]{:S(2)}) collective-permute-start(f32[40,640]{1,0:T(8,128)S(1)} %add.36), channel_id=1, source_target_pairs={{0,4},{2,6},{8,0},{10,2},{16,8},{18,10},{24,16},{26,18},{28,24},{3... | collective-permute-start | bytes 307208 | tf_op jit(solution)/shard_map/ppermute | solution.py:313
  69.8 5.3 %collective-permute-start.22 = (f32[40,640]{1,0:T(8,128)S(1)}, f32[40,640]{1,0:T(8,128)S(1)}, u32[]{:S(2)}, u32[]{:S(2)}) collective-permute-start(f32[40,640]{1,0:T(8,128)S(1)} %add.34), channel_id=1, source_target_pairs={{0,4},{2,6},{8,0},{10,2},{16,8},{18,10},{24,16},{26,18},{28,24},{3... | collective-permute-start | bytes 307208 | tf_op jit(solution)/shard_map/ppermute | solution.py:313
  70.3 4.8 %collective-permute-start.29 = (f32[40,640]{1,0:T(8,128)S(1)}, f32[40,640]{1,0:T(8,128)S(1)}, u32[]{:S(2)}, u32[]{:S(2)}) collective-permute-start(f32[40,640]{1,0:T(8,128)S(1)} %add.39), channel_id=1, source_target_pairs={{0,8},{2,10},{8,16},{10,18},{16,24},{18,26},{24,28},{26,30},{28,20... | collective-permute-start | bytes 307208 | tf_op jit(solution)/shard_map/ppermute | solution.py:312
  71.9 4.7 %collective-permute-start.19 = (f32[40,640]{1,0:T(8,128)S(1)}, f32[40,640]{1,0:T(8,128)S(1)}, u32[]{:S(2)}, u32[]{:S(2)}) collective-permute-start(f32[40,640]{1,0:T(8,128)S(1)} %add.32), channel_id=1, source_target_pairs={{0,8},{2,10},{8,16},{10,18},{16,24},{18,26},{24,28},{26,30},{28,20... | collective-permute-start | bytes 307208 | tf_op jit(solution)/shard_map/ppermute | solution.py:312
  78.7 5.2 %collective-permute-start.32 = (f32[40,640]{1,0:T(8,128)S(1)}, f32[40,640]{1,0:T(8,128)S(1)}, u32[]{:S(2)}, u32[]{:S(2)}) collective-permute-start(f32[40,640]{1,0:T(8,128)S(1)} %get-tuple-element.67), channel_id=1, source_target_pairs={{0,3},{1,2},{2,1},{3,0},{4,7},{5,6},{6,5},{7,4},{8,11},{9,10},{10,... | collective-permute-start | bytes 307208 | tf_op jit(solution)/shard_map/ppermute | solution.py:401
  78.8 5.1 %collective-permute-start.30 = (f32[40,640]{1,0:T(8,128)S(1)}, f32[40,640]{1,0:T(8,128)S(1)}, u32[]{:S(2)}, u32[]{:S(2)}) collective-permute-start(f32[40,640]{1,0:T(8,128)S(1)} %get-tuple-element.67), channel_id=1, source_target_pairs={{0,2},{2,0},{4,6},{6,4},{8,10},{10,8},{12,14},{14,12},{16,18},{18,... | collective-permute-start | bytes 307208 | tf_op jit(solution)/shard_map/ppermute | solution.py:310
  80.4 5.7 %collective-permute-start.31 = (f32[40,640]{1,0:T(8,128)S(1)}, f32[40,640]{1,0:T(8,128)S(1)}, u32[]{:S(2)}, u32[]{:S(2)}) collective-permute-start(f32[40,640]{1,0:T(8,128)S(1)} %get-tuple-element.68.keep), channel_id=1, source_target_pairs={{0,1},{1,0},{2,3},{3,2},{4,5},{5,4},{6,7},{7,6},{8,9},{9,8},{10,11... | collective-permute-start | bytes 307208 | tf_op jit(solution)/shard_map/ppermute | solution.py:400
  (8 other events, 35.2 us)
